TPU v7x, 32 devices: a whole 2x2x4 slice. The times are simulated.
32 devices in a mesh: tensor: 8 (over y, x, core), dp: 4 (over z).
Axes of the slice: x: 2, y: 2, z: 4, core: 2. Of those that a mesh axis runs over, the one named last changes fastest.
Arguments:
- layer_input: bfloat16 [4, 1024, 3072], P('dp', 'tensor'), may hold values from -6 to 6
- attn_output: bfloat16 [4, 1024, 4096], P('dp', 'tensor'), may hold values from -6 to 6
- grad_gated: bfloat16 [4, 1024, 4096], P('dp', 'tensor'), may hold values from -6 to 6
- gate_weight: bfloat16 [3072, 4096], P(None, 'tensor'), may hold values from -0.109375 to 0.109375
Outputs:
- grad_input: bfloat16 [4, 1024, 3072], P('dp', 'tensor')
- grad_attn: bfloat16 [4, 1024, 4096], P('dp', 'tensor')
- grad_weight: float32 [3072, 4096], P('dp', 'tensor')
All inputs are finite; a program needn't handle non-finite values.
Results may differ from a plain program's by a relative error of at most 0.005.
Values may be sent and summed in bfloat16 or wider, within the bound.
No kernel may reach another device: no remote copies, remote signals or barrier semaphores. Data moves between devices by JAX's collectives and lax.ppermute only.
A program may use at most 128 MiB of HBM per device.

v0:
```python
import jax
import jax.numpy as jnp
from jax import lax
from jax.sharding import PartitionSpec as P


def from_behind(x, axis, by):
    count = lax.axis_size(axis)
    return lax.ppermute(x, axis, [(i, (i + by) % count) for i in range(count)])


def gate_terms(row_block, gate_weight, cot_cols, att_cols):
    pre_act = jnp.dot(row_block, gate_weight, preferred_element_type=jnp.float32)
    gate_val = jax.nn.sigmoid(pre_act)
    cotangent = cot_cols.astype(jnp.float32)
    attention = att_cols.astype(jnp.float32)
    grad_attn_rows = (cotangent * gate_val).astype(jnp.bfloat16)
    grad_pre_rows = (cotangent * attention * gate_val * (1.0 - gate_val)).astype(jnp.bfloat16)
    return (grad_attn_rows, grad_pre_rows)


def weight_term(row_block, grad_pre_rows):
    return lax.dot_general(
        row_block, grad_pre_rows, (((0,), (0,)), ((), ())), preferred_element_type=jnp.float32
    )


def input_term(grad_pre_rows, gate_weight):
    return lax.dot_general(
        grad_pre_rows, gate_weight, (((1,), (1,)), ((), ())), preferred_element_type=jnp.float32
    )


def on_device(layer_input, attn_output, grad_gated, gate_weight):
    members = lax.axis_size("tensor")
    myself = lax.axis_index("tensor")
    tok_rows = layer_input.shape[1]
    width = layer_input.shape[2]
    cot_cols, att_cols = (
        lax.all_to_all(grad_gated, "tensor", split_axis=2, concat_axis=1, tiled=True),
        lax.all_to_all(attn_output, "tensor", split_axis=2, concat_axis=1, tiled=True),
    )
    cot_cols = cot_cols[0]
    att_cols = att_cols[0]
    row_block = lax.all_gather(layer_input, "tensor", axis=1, tiled=True)[0]
    grad_attn_rows, grad_pre_rows = gate_terms(row_block, gate_weight, cot_cols, att_cols)
    weight_sum = weight_term(row_block, grad_pre_rows)
    attn_all = grad_attn_rows
    weight_sum, pre_all, attn_all = (weight_sum, grad_pre_rows, attn_all)

    def block_term(block_id):
        grad_rows = lax.dynamic_slice_in_dim(pre_all, block_id * tok_rows, tok_rows, 0)
        return input_term(grad_rows, gate_weight)

    def carry_step(step_index, running):
        moved = from_behind(running, "tensor", 1)
        return moved + block_term((myself - step_index - 1) % members)

    running = lax.fori_loop(1, members, carry_step, block_term((myself - 1) % members))
    grad_attn = lax.all_to_all(attn_all[None], "tensor", split_axis=1, concat_axis=2, tiled=True)
    share_rows = width // lax.axis_size("dp")
    totals = lax.psum(weight_sum, "dp")
    grad_weight = lax.dynamic_slice_in_dim(totals, lax.axis_index("dp") * share_rows, share_rows, 0)
    return (running.astype(jnp.bfloat16)[None], grad_attn, grad_weight)


def solution(mesh):
    in_specs = (
        P("dp", "tensor", None),
        P("dp", "tensor", None),
        P("dp", "tensor", None),
        P(None, "tensor"),
    )
    out_specs = (P("dp", "tensor", None), P("dp", "tensor", None), P("dp", "tensor"))
    return jax.shard_map(
        on_device, mesh=mesh, in_specs=in_specs, out_specs=out_specs, check_vma=False
    )
```

profile of v0, /device:TPU:0, one launch (start us, length us, event | category | flops | bytes accessed | tf_op | source)
XLA Modules:
  0.0 350.5 jit_solution(2677704517987878580)
XLA Ops:
  7.9 5.0 %copy.26 = bf16[1,128,4096]{1,0,2:T(2,128)(2,1)S(1)} copy(bf16[1,128,4096]{2,1,0:T(8,128)(2,1)} %param.7) | data formatting | bytes 2097152 | tf_op args[1]
  13.5 22.4 %reduce.1 = bf16[4096,128]{1,0:T(8,128)(2,1)S(1)} reduce(bf16[4096,1,128]{2,1,0:T(2,128)(2,1)S(1)} %bitcast.56, bf16[]{:T(256)} %broadcast.8), dimensions={1}, to_apply=%bitcast.37.reduce_sub_computation | reduce | bytes 2097154
  37.1 5.2 %all-to-all-start.1 = ((bf16[8,2,32768]{2,1,0:T(2,128)(2,1)}), bf16[8,2,32768]{2,1,0:T(2,128)(2,1)S(1)}, u32[]{:S(2)}, u32[]{:S(2)}) async-start(bf16[8,2,32768]{2,1,0:T(2,128)(2,1)} %reshape.20), calls=%async_computation.1 | async-start | bytes 2097152 | tf_op jit(solution)/shard_map/all_to_all | solution.py:41
  42.3 5.0 %copy.24 = bf16[1,128,4096]{1,0,2:T(2,128)(2,1)S(1)} copy(bf16[1,128,4096]{2,1,0:T(8,128)(2,1)} %param.8) | data formatting | bytes 2097152 | tf_op args[2]
  47.3 23.4 %reduce = bf16[4096,128]{1,0:T(8,128)(2,1)} reduce(bf16[4096,1,128]{2,1,0:T(2,128)(2,1)S(1)} %bitcast.60, bf16[]{:T(256)} %broadcast.8), dimensions={1}, to_apply=%bitcast.39.reduce_sub_computation | reduce | bytes 2097154
  72.9 4.2 %all-to-all-start = ((bf16[8,2,32768]{2,1,0:T(2,128)(2,1)}), bf16[8,2,32768]{2,1,0:T(2,128)(2,1)}, u32[]{:S(2)}, u32[]{:S(2)}) async-start(bf16[8,2,32768]{2,1,0:T(2,128)(2,1)} %reshape.22), calls=%async_computation | async-start | bytes 2097152 | tf_op jit(solution)/shard_map/all_to_all | solution.py:40
  78.4 3.2 bitcast_convert_fusion.1
  84.6 8.0 %all-to-all-done = bf16[8,2,32768]{2,1,0:T(2,128)(2,1)} async-done(((bf16[8,2,32768]{2,1,0:T(2,128)(2,1)}), bf16[8,2,32768]{2,1,0:T(2,128)(2,1)}, u32[]{:S(2)}, u32[]{:S(2)}) %all-to-all-start) | async-done | bytes 1048608 | tf_op jit(solution)/shard_map/all_to_all | solution.py:40
  92.6 4.3 %reshape.23 = bf16[4096,1,128]{2,1,0:T(2,128)(2,1)S(1)} reshape(bf16[8,2,32768]{2,1,0:T(2,128)(2,1)} %all-to-all-done) | data formatting | bytes 2097152
  96.9 3.3 bitcast_convert_fusion
  103.3 8.4 %fusion.12 = (bf16[1024,512]{1,0:T(8,128)(2,1)}, bf16[1024,512]{1,0:T(8,128)(2,1)S(1)}) fusion(f32[1,128,8,512]{3,1,2,0:T(8,128)} %copy.25, f32[1,128,8,512]{3,1,2,0:T(8,128)} %copy.27, bf16[3072,512]{1,0:T(8,128)(2,1)S(1)} %copy-done, bf16[1,1024,3072]{2,1,0:T(8,128)(2,1)} %all-gather.2.cloned.1.call-done), kind=kOutput, calls=%fused_computation.13 | convolution fusion | flops 3226468352 | bytes 15728640 | tf_op jit(solution)/shard_map/dot_general | solution.py:13
  112.7 5.4 %fusion.6 = f32[3072,512]{0,1:T(8,128)} fusion(bf16[1024,512]{1,0:T(8,128)(2,1)S(1)} %get-tuple-element.196, bf16[1,1024,3072]{2,1,0:T(8,128)(2,1)S(1)} %copy-done.1), kind=kOutput, calls=%fused_computation.7 | convolution fusion | flops 3221225472 | bytes 13631488 | tf_op jit(solution)/shard_map/dot_general | solution.py:23
  118.1 4.1 %copy.34 = bf16[1,1024,512]{2,0,1:T(2,128)(2,1)} copy(bf16[1,1024,512]{2,1,0:T(8,128)(2,1)} %bitcast.63) | data formatting | bytes 2097152 | tf_op jit(solution)/shard_map/broadcast_in_dim | solution.py:60
  122.3 9.5 %reduce.2 = bf16[1024,512]{1,0:T(8,128)(2,1)} reduce(bf16[1024,1,512]{2,1,0:T(2,128)(2,1)} %bitcast.57, bf16[]{:T(256)} %broadcast.8), dimensions={1}, to_apply=%bitcast.52.reduce_sub_computation | reduce | bytes 2097154
  134.5 4.3 %all-to-all-start.2 = ((bf16[8,2,32768]{2,1,0:T(2,128)(2,1)}), bf16[8,2,32768]{2,1,0:T(2,128)(2,1)}, u32[]{:S(2)}, u32[]{:S(2)}) async-start(bf16[8,2,32768]{2,1,0:T(2,128)(2,1)} %reshape.24), calls=%async_computation.2 | async-start | bytes 2097152 | tf_op jit(solution)/shard_map/all_to_all | solution.py:60
  141.9 181.9 %while.15 = (s32[]{:T(128)}, f32[128,3072]{1,0:T(8,128)}, s32[]{:T(128)}, bf16[1024,512]{1,0:T(8,128)(2,1)}, bf16[3072,512]{1,0:T(8,128)(2,1)S(1)}, /*index=5*/s...) while((s32[]{:T(128)}, f32[128,3072]{1,0:T(8,128)}, ...), condition=%wide.region_1.2_spmd, body=%wide.region_0.1_spmd.sunk | while | flops 403046432 | bytes 12714324 | solution.py:59
  142.3 28.7 %collective-permute-done = f32[128,3072]{1,0:T(8,128)} collective-permute-done((f32[128,3072]{1,0:T(8,128)}, f32[128,3072]{1,0:T(8,128)}, u32[]{:S(2)}, u32[]{:S(2)}) %collective-permute-start) | collective-permute-done | bytes 1572896 | tf_op jit(solution)/shard_map/while/body/eval_jaxpr/ppermute | solution.py:9
  171.0 3.8 %convolution_add_fusion.2 = f32[128,3072]{1,0:T(8,128)} fusion(f32[128,3072]{1,0:T(8,128)} %collective-permute-done, bf16[3072,512]{1,0:T(8,128)(2,1)S(1)} %get-tuple-element.221, bf16[1024,512]{1,0:T(8,128)(2,1)} %get-tuple-element.220, s32[]{:T(128)S(6)} %select_n.46), kind=kOutput, calls=%fused_computation.clone.1 | convolution fusion | flops 403046400 | bytes 6422532 | tf_op jit(solution)/shard_map/while/body/eval_jaxpr/dot_general | solution.py:29
  174.8 21.1 %collective-permute-done = f32[128,3072]{1,0:T(8,128)} collective-permute-done((f32[128,3072]{1,0:T(8,128)}, f32[128,3072]{1,0:T(8,128)}, u32[]{:S(2)}, u32[]{:S(2)}) %collective-permute-start) | collective-permute-done | bytes 1572896 | tf_op jit(solution)/shard_map/while/body/eval_jaxpr/ppermute | solution.py:9
  195.8 3.8 %convolution_add_fusion.2 = f32[128,3072]{1,0:T(8,128)} fusion(f32[128,3072]{1,0:T(8,128)} %collective-permute-done, bf16[3072,512]{1,0:T(8,128)(2,1)S(1)} %get-tuple-element.221, bf16[1024,512]{1,0:T(8,128)(2,1)} %get-tuple-element.220, s32[]{:T(128)S(6)} %select_n.46), kind=kOutput, calls=%fused_computation.clone.1 | convolution fusion | flops 403046400 | bytes 6422532 | tf_op jit(solution)/shard_map/while/body/eval_jaxpr/dot_general | solution.py:29
  199.6 21.1 %collective-permute-done = f32[128,3072]{1,0:T(8,128)} collective-permute-done((f32[128,3072]{1,0:T(8,128)}, f32[128,3072]{1,0:T(8,128)}, u32[]{:S(2)}, u32[]{:S(2)}) %collective-permute-start) | collective-permute-done | bytes 1572896 | tf_op jit(solution)/shard_map/while/body/eval_jaxpr/ppermute | solution.py:9
  220.7 3.8 %convolution_add_fusion.2 = f32[128,3072]{1,0:T(8,128)} fusion(f32[128,3072]{1,0:T(8,128)} %collective-permute-done, bf16[3072,512]{1,0:T(8,128)(2,1)S(1)} %get-tuple-element.221, bf16[1024,512]{1,0:T(8,128)(2,1)} %get-tuple-element.220, s32[]{:T(128)S(6)} %select_n.46), kind=kOutput, calls=%fused_computation.clone.1 | convolution fusion | flops 403046400 | bytes 6422532 | tf_op jit(solution)/shard_map/while/body/eval_jaxpr/dot_general | solution.py:29
  224.5 21.1 %collective-permute-done = f32[128,3072]{1,0:T(8,128)} collective-permute-done((f32[128,3072]{1,0:T(8,128)}, f32[128,3072]{1,0:T(8,128)}, u32[]{:S(2)}, u32[]{:S(2)}) %collective-permute-start) | collective-permute-done | bytes 1572896 | tf_op jit(solution)/shard_map/while/body/eval_jaxpr/ppermute | solution.py:9
  245.5 3.8 %convolution_add_fusion.2 = f32[128,3072]{1,0:T(8,128)} fusion(f32[128,3072]{1,0:T(8,128)} %collective-permute-done, bf16[3072,512]{1,0:T(8,128)(2,1)S(1)} %get-tuple-element.221, bf16[1024,512]{1,0:T(8,128)(2,1)} %get-tuple-element.220, s32[]{:T(128)S(6)} %select_n.46), kind=kOutput, calls=%fused_computation.clone.1 | convolution fusion | flops 403046400 | bytes 6422532 | tf_op jit(solution)/shard_map/while/body/eval_jaxpr/dot_general | solution.py:29
  249.3 21.1 %collective-permute-done = f32[128,3072]{1,0:T(8,128)} collective-permute-done((f32[128,3072]{1,0:T(8,128)}, f32[128,3072]{1,0:T(8,128)}, u32[]{:S(2)}, u32[]{:S(2)}) %collective-permute-start) | collective-permute-done | bytes 1572896 | tf_op jit(solution)/shard_map/while/body/eval_jaxpr/ppermute | solution.py:9
  270.4 3.8 %convolution_add_fusion.2 = f32[128,3072]{1,0:T(8,128)} fusion(f32[128,3072]{1,0:T(8,128)} %collective-permute-done, bf16[3072,512]{1,0:T(8,128)(2,1)S(1)} %get-tuple-element.221, bf16[1024,512]{1,0:T(8,128)(2,1)} %get-tuple-element.220, s32[]{:T(128)S(6)} %select_n.46), kind=kOutput, calls=%fused_computation.clone.1 | convolution fusion | flops 403046400 | bytes 6422532 | tf_op jit(solution)/shard_map/while/body/eval_jaxpr/dot_general | solution.py:29
  274.1 21.1 %collective-permute-done = f32[128,3072]{1,0:T(8,128)} collective-permute-done((f32[128,3072]{1,0:T(8,128)}, f32[128,3072]{1,0:T(8,128)}, u32[]{:S(2)}, u32[]{:S(2)}) %collective-permute-start) | collective-permute-done | bytes 1572896 | tf_op jit(solution)/shard_map/while/body/eval_jaxpr/ppermute | solution.py:9
  295.2 3.8 %convolution_add_fusion.2 = f32[128,3072]{1,0:T(8,128)} fusion(f32[128,3072]{1,0:T(8,128)} %collective-permute-done, bf16[3072,512]{1,0:T(8,128)(2,1)S(1)} %get-tuple-element.221, bf16[1024,512]{1,0:T(8,128)(2,1)} %get-tuple-element.220, s32[]{:T(128)S(6)} %select_n.46), kind=kOutput, calls=%fused_computation.clone.1 | convolution fusion | flops 403046400 | bytes 6422532 | tf_op jit(solution)/shard_map/while/body/eval_jaxpr/dot_general | solution.py:29
  299.0 21.1 %collective-permute-done = f32[128,3072]{1,0:T(8,128)} collective-permute-done((f32[128,3072]{1,0:T(8,128)}, f32[128,3072]{1,0:T(8,128)}, u32[]{:S(2)}, u32[]{:S(2)}) %collective-permute-start) | collective-permute-done | bytes 1572896 | tf_op jit(solution)/shard_map/while/body/eval_jaxpr/ppermute | solution.py:9
  320.0 3.8 %convolution_add_fusion.2 = f32[128,3072]{1,0:T(8,128)} fusion(f32[128,3072]{1,0:T(8,128)} %collective-permute-done, bf16[3072,512]{1,0:T(8,128)(2,1)S(1)} %get-tuple-element.221, bf16[1024,512]{1,0:T(8,128)(2,1)} %get-tuple-element.220, s32[]{:T(128)S(6)} %select_n.46), kind=kOutput, calls=%fused_computation.clone.1 | convolution fusion | flops 403046400 | bytes 6422532 | tf_op jit(solution)/shard_map/while/body/eval_jaxpr/dot_general | solution.py:29
  326.2 4.3 %reshape.25 = bf16[1024,1,512]{2,1,0:T(2,128)(2,1)S(1)} reshape(bf16[8,2,32768]{2,1,0:T(2,128)(2,1)} %all-to-all-done.2) | data formatting | bytes 2097152
  332.8 7.7 %all-reduce.2.cloned.1.call-done = f32[3072,512]{0,1:T(8,128)} async-done(((f32[3072,512]{0,1:T(8,128)}), f32[3072,512]{0,1:T(8,128)}) %all-reduce.2.cloned.1.call-update) | async-done | bytes 6291472 | tf_op jit(solution)/shard_map/psum | solution.py:62
  (34 shorter events, 26.9 us)
Async XLA Ops:
  7.2 96.1 %all-gather.2.cloned.1.call-start = ((), (), s32[]{:S(2)}) async-start(), calls=%async_computation.3 | async-start | bytes 7077888 | tf_op jit(solution)/shard_map/all_gather | solution.py:45
  37.1 35.7 %all-to-all-start.1 = ((bf16[8,2,32768]{2,1,0:T(2,128)(2,1)}), bf16[8,2,32768]{2,1,0:T(2,128)(2,1)S(1)}, u32[]{:S(2)}, u32[]{:S(2)}) async-start(bf16[8,2,32768]{2,1,0:T(2,128)(2,1)} %reshape.20), calls=%async_computation.1 | async-start | bytes 2097152 | tf_op jit(solution)/shard_map/all_to_all | solution.py:41
  72.9 19.7 %all-to-all-start = ((bf16[8,2,32768]{2,1,0:T(2,128)(2,1)}), bf16[8,2,32768]{2,1,0:T(2,128)(2,1)}, u32[]{:S(2)}, u32[]{:S(2)}) async-start(bf16[8,2,32768]{2,1,0:T(2,128)(2,1)} %reshape.22), calls=%async_computation | async-start | bytes 2097152 | tf_op jit(solution)/shard_map/all_to_all | solution.py:40
  77.1 263.4 %all-reduce.2.cloned.1.call-start = ((), (), s32[]{:S(2)}) async-start(), calls=%async_computation.4 | async-start | bytes 12582912 | tf_op jit(solution)/shard_map/psum | solution.py:62
  100.2 3.1 copy-start
  103.3 9.4 %copy-start.1 = (bf16[1,1024,3072]{2,1,0:T(8,128)(2,1)S(1)}, bf16[1,1024,3072]{2,1,0:T(8,128)(2,1)}, u32[]{:S(2)}) copy-start(bf16[1,1024,3072]{2,1,0:T(8,128)(2,1)} %all-gather.2.cloned.1.call-done) | copy-start | bytes 18874372
  111.6 1.0 copy-start.2
  134.5 191.8 %all-to-all-start.2 = ((bf16[8,2,32768]{2,1,0:T(2,128)(2,1)}), bf16[8,2,32768]{2,1,0:T(2,128)(2,1)}, u32[]{:S(2)}, u32[]{:S(2)}) async-start(bf16[8,2,32768]{2,1,0:T(2,128)(2,1)} %reshape.24), calls=%async_computation.2 | async-start | bytes 2097152 | tf_op jit(solution)/shard_map/all_to_all | solution.py:60
  141.9 29.1 %collective-permute-start = (f32[128,3072]{1,0:T(8,128)}, f32[128,3072]{1,0:T(8,128)}, u32[]{:S(2)}, u32[]{:S(2)}) collective-permute-start(f32[128,3072]{1,0:T(8,128)} %get-tuple-element.206), channel_id=1, source_target_pairs={{0,4},{4,8},{8,12},{12,16},{16,20},{20,24},{24,28},{28,0},{1,5},{5... | collective-permute-start | bytes 4718600 | tf_op jit(solution)/shard_map/while/body/eval_jaxpr/ppermute | solution.py:9
  174.8 21.1 %collective-permute-start = (f32[128,3072]{1,0:T(8,128)}, f32[128,3072]{1,0:T(8,128)}, u32[]{:S(2)}, u32[]{:S(2)}) collective-permute-start(f32[128,3072]{1,0:T(8,128)} %get-tuple-element.206), channel_id=1, source_target_pairs={{0,4},{4,8},{8,12},{12,16},{16,20},{20,24},{24,28},{28,0},{1,5},{5... | collective-permute-start | bytes 4718600 | tf_op jit(solution)/shard_map/while/body/eval_jaxpr/ppermute | solution.py:9
  199.6 21.1 %collective-permute-start = (f32[128,3072]{1,0:T(8,128)}, f32[128,3072]{1,0:T(8,128)}, u32[]{:S(2)}, u32[]{:S(2)}) collective-permute-start(f32[128,3072]{1,0:T(8,128)} %get-tuple-element.206), channel_id=1, source_target_pairs={{0,4},{4,8},{8,12},{12,16},{16,20},{20,24},{24,28},{28,0},{1,5},{5... | collective-permute-start | bytes 4718600 | tf_op jit(solution)/shard_map/while/body/eval_jaxpr/ppermute | solution.py:9
  224.5 21.1 %collective-permute-start = (f32[128,3072]{1,0:T(8,128)}, f32[128,3072]{1,0:T(8,128)}, u32[]{:S(2)}, u32[]{:S(2)}) collective-permute-start(f32[128,3072]{1,0:T(8,128)} %get-tuple-element.206), channel_id=1, source_target_pairs={{0,4},{4,8},{8,12},{12,16},{16,20},{20,24},{24,28},{28,0},{1,5},{5... | collective-permute-start | bytes 4718600 | tf_op jit(solution)/shard_map/while/body/eval_jaxpr/ppermute | solution.py:9
  249.3 21.1 %collective-permute-start = (f32[128,3072]{1,0:T(8,128)}, f32[128,3072]{1,0:T(8,128)}, u32[]{:S(2)}, u32[]{:S(2)}) collective-permute-start(f32[128,3072]{1,0:T(8,128)} %get-tuple-element.206), channel_id=1, source_target_pairs={{0,4},{4,8},{8,12},{12,16},{16,20},{20,24},{24,28},{28,0},{1,5},{5... | collective-permute-start | bytes 4718600 | tf_op jit(solution)/shard_map/while/body/eval_jaxpr/ppermute | solution.py:9
  274.1 21.1 %collective-permute-start = (f32[128,3072]{1,0:T(8,128)}, f32[128,3072]{1,0:T(8,128)}, u32[]{:S(2)}, u32[]{:S(2)}) collective-permute-start(f32[128,3072]{1,0:T(8,128)} %get-tuple-element.206), channel_id=1, source_target_pairs={{0,4},{4,8},{8,12},{12,16},{16,20},{20,24},{24,28},{28,0},{1,5},{5... | collective-permute-start | bytes 4718600 | tf_op jit(solution)/shard_map/while/body/eval_jaxpr/ppermute | solution.py:9
  299.0 21.1 %collective-permute-start = (f32[128,3072]{1,0:T(8,128)}, f32[128,3072]{1,0:T(8,128)}, u32[]{:S(2)}, u32[]{:S(2)}) collective-permute-start(f32[128,3072]{1,0:T(8,128)} %get-tuple-element.206), channel_id=1, source_target_pairs={{0,4},{4,8},{8,12},{12,16},{16,20},{20,24},{24,28},{28,0},{1,5},{5... | collective-permute-start | bytes 4718600 | tf_op jit(solution)/shard_map/while/body/eval_jaxpr/ppermute | solution.py:9
Sparse Core Ops, SparseCore 0:
  9.9 58.8 all-gather.1
  118.2 222.2 all-reduce.1
where the time goes:
time: 352 us; the launch traced here: 350 us
  waiting for transfers between devices  171 us (49%)
  other arithmetic  64.3 us (18%)
  matrix products  43.5 us (12%)
  local copies, waits for them, and re-layouts  42.8 us (12%)
  starting transfers between devices  14.3 us (4%)
  between operations  14.2 us (4%)
    ppermute x7, waiting for transfers between devices, from_behind(): return lax.ppermute(x, axis, [(i, (i + by) % count) for i in range(count)])  155 us
    unnamed x3, other arithmetic  55.4 us
    unnamed x18, local copies, waits for them, and re-layouts  30.5 us
    dot_general x8, matrix products, input_term(): lax.dot_general(grad_pre_rows, gate_weight, (((1,), (1,)), ((), ())), pre...  29.7 us
    dot_general x1, matrix products, gate_terms(): jnp.dot(row_block, gate_weight, preferred_element_type=jnp.float32)  8.37 us
    all_to_all x1, waiting for transfers between devices, on_device(): lax.all_to_all(grad_gated, 'tensor', split_axis=2, concat_axis=1, tiled=T...  8.03 us
    psum x1, waiting for transfers between devices, on_device(): totals = lax.psum(weight_sum, 'dp')  7.68 us
  transfers between devices with their start and end apart: 12, of which 9 were waited for; matrix products, arithmetic and copies ran while one was open for 38% of the time, Pallas kernels for 0%

commit v1 on v0

v1 whole, which is shorter than its diff:
```python
import jax
import jax.numpy as jnp
from jax import lax
from jax.sharding import PartitionSpec as P

BF16 = jnp.bfloat16
F32 = jnp.float32


def swap(x, mask):
    count = lax.axis_size("tensor")
    return lax.ppermute(x, "tensor", [(i, i ^ mask) for i in range(count)])


def step_dp(x, by, senders):
    return lax.ppermute(x, "dp", [(i, i + by) for i in senders])


def columns_of(x, chip, core, width):
    own = lax.dynamic_slice_in_dim(x, (2 * chip + core) * width, width, 1)
    other = lax.dynamic_slice_in_dim(x, (2 * chip + 1 - core) * width, width, 1)
    return jnp.concatenate([own, other], 1)


def reduce_over_dp(partial):
    count = lax.axis_size("dp")
    me = lax.axis_index("dp")
    rows = partial.shape[0] // count

    def share(k):
        return lax.dynamic_slice_in_dim(partial, jnp.clip(k, 0, count - 1) * rows, rows, 0)

    right = left = None
    for r in range(1, count):
        to_right, to_left = share(me + count - r), share(me - count + r)
        if r > 1:
            to_right = to_right + right.astype(F32)
            to_left = to_left + left.astype(F32)
        right = step_dp(to_right.astype(BF16), 1, range(0, r))
        left = step_dp(to_left.astype(BF16), -1, range(count - r, count))
    return share(me) + (right.astype(F32) + left.astype(F32)) if count > 1 else share(me)


def on_device(layer_input, attn_output, grad_gated, gate_weight):
    members = lax.axis_size("tensor")
    chips = members // 2
    myself = lax.axis_index("tensor")
    chip, core = myself // 2, myself % 2
    width = gate_weight.shape[1]
    x0 = layer_input[0]
    cot = grad_gated[0]
    att = attn_output[0]

    w_other = swap(gate_weight, 1)
    w_both = jnp.concatenate([gate_weight, w_other], 1)
    xs = [x0] + [swap(x0, 2 * m) for m in range(1, chips)]
    ga = []
    for m in range(chips):
        cols = columns_of(cot, chip ^ m, core, width).astype(F32) * columns_of(att, chip ^ m, core, width).astype(F32)
        cols = cols.astype(BF16)
        ga.append(cols if m == 0 else swap(cols, 2 * m))
    xs_other = [swap(x, 1) for x in xs]

    gates, pres, dxs = [], [], []
    for m in range(chips):
        pre = jnp.dot(xs[m], w_both, preferred_element_type=F32)
        gate = jax.nn.sigmoid(pre)
        gp = (ga[m].astype(F32) * gate * (1.0 - gate)).astype(BF16)
        gate = gate.astype(BF16)
        dx = lax.dot_general(gp, w_both, (((1,), (1,)), ((), ())), preferred_element_type=F32)
        gates.append(gate if m == 0 else swap(gate, 2 * m))
        pres.append(gp)
        dxs.append(dx if m == 0 else swap(dx.astype(BF16), 2 * m))

    gp_all = jnp.concatenate(pres, 0)
    gp_mine = jnp.concatenate([gp_all[:, :width], swap(gp_all[:, width:], 1)], 0)
    x_all = jnp.concatenate(xs + xs_other, 0)
    halves = []
    half = width // 2
    for h in range(2):
        part = lax.dot_general(
            x_all, gp_mine[:, h * half : (h + 1) * half], (((0,), (0,)), ((), ())), preferred_element_type=F32
        )
        halves.append(reduce_over_dp(part))
    grad_weight = jnp.concatenate(halves, 1)

    grad_input = sum(d.astype(F32) for d in dxs).astype(BF16)
    grad_attn = jnp.zeros_like(cot)
    for m in range(chips):
        there = chip ^ m
        for which, cols in ((core, gates[m][:, :width]), (1 - core, gates[m][:, width:])):
            at = (2 * there + which) * width
            piece = lax.dynamic_slice_in_dim(cot, at, width, 1).astype(F32) * cols.astype(F32)
            grad_attn = lax.dynamic_update_slice_in_dim(grad_attn, piece.astype(BF16), at, 1)
    return (grad_input[None], grad_attn[None], grad_weight)


def solution(mesh):
    in_specs = (
        P("dp", "tensor", None),
        P("dp", "tensor", None),
        P("dp", "tensor", None),
        P(None, "tensor"),
    )
    out_specs = (P("dp", "tensor", None), P("dp", "tensor", None), P("dp", "tensor"))
    return jax.shard_map(
        on_device, mesh=mesh, in_specs=in_specs, out_specs=out_specs, check_vma=False
    )
```

time: 352 us -> 166 us (0.47)
  waiting for transfers between devices: 171 us -> 63.7 us
  other arithmetic: 64.3 us -> 7.59 us
  starting transfers between devices: 14.3 us -> 52.9 us
  local copies, waits for them, and re-layouts: 42.8 us -> 12 us
  matrix products: 43.5 us -> 28 us
  between operations: 14.2 us -> 1.16 us
    ppermute x7 -> x30, waiting for transfers between devices: 155 us -> 63.7 us  [the longest x18 51.6 us: swap(): return lax.ppermute(x, 'tensor', [(i, i ^ mask) for i in range(count)])]
    unnamed x3 -> x0, other arithmetic: 55.4 us -> none
    ppermute x7 -> x30, starting transfers between devices: 0.39 us -> 52.9 us  [the longest x12 36.3 us: step_dp(): return lax.ppermute(x, 'dp', [(i, i + by) for i in senders])]
    unnamed x18 -> x23, local copies, waits for them, and re-layouts: 30.5 us -> 11 us
    dot_general x10, matrix products: 43.5 us -> 28 us  [the longest x4 15.8 us: on_device(): lax.dot_general(gp, w_both, (((1,), (1,)), ((), ())), preferred_element_t...]
    all_to_all x3 -> x0, starting transfers between devices: 13.7 us -> none  [the longest x1 5.17 us: on_device(): lax.all_to_all(attn_output, 'tensor', split_axis=2, concat_axis=1, tiled=...]
    all_to_all x3 -> x0, waiting for transfers between devices: 8.04 us -> none  [the longest x1 8.03 us: on_device(): lax.all_to_all(grad_gated, 'tensor', split_axis=2, concat_axis=1, tiled=T...]
    psum x1 -> x0, waiting for transfers between devices: 7.68 us -> none  [on_device(): totals = lax.psum(weight_sum, 'dp')]
  transfers between devices with their start and end apart: 12 -> 30, of which waited for: 9 -> 11; matrix products, arithmetic and copies ran while one was open for 38% -> 26% of each run, Pallas kernels for 0% -> 0%
where the time goes in v1:
time: 166 us; the launch traced here: 165 us
  waiting for transfers between devices  63.7 us (38%)
  starting transfers between devices  52.9 us (32%)
  matrix products  28 us (17%)
  local copies, waits for them, and re-layouts  12 us (7%)
  other arithmetic  7.59 us (5%)
    ppermute x18, waiting for transfers between devices, swap(): return lax.ppermute(x, 'tensor', [(i, i ^ mask) for i in range(count)])  51.6 us
    ppermute x12, starting transfers between devices, step_dp(): return lax.ppermute(x, 'dp', [(i, i + by) for i in senders])  36.3 us
    ppermute x18, starting transfers between devices, swap(): return lax.ppermute(x, 'tensor', [(i, i ^ mask) for i in range(count)])  16.6 us
    dot_general x4, matrix products, on_device(): lax.dot_general(gp, w_both, (((1,), (1,)), ((), ())), preferred_element_t...  15.8 us
    ppermute x12, waiting for transfers between devices, step_dp(): return lax.ppermute(x, 'dp', [(i, i + by) for i in senders])  12 us
    unnamed x23, local copies, waits for them, and re-layouts  11 us
    dot_general x4, matrix products, on_device(): pre = jnp.dot(xs[m], w_both, preferred_element_type=F32)  8.36 us
    dot_general x2, matrix products, on_device(): lax.dot_general(x_all, gp_mine[:, h * half:(h + 1) * half], (((0,), (0,))...  3.84 us
  transfers between devices with their start and end apart: 30, of which 11 were waited for; matrix products, arithmetic and copies ran while one was open for 26% of the time, Pallas kernels for 0%

profile of v1, /device:TPU:0, one launch (start us, length us, event | category | flops | bytes accessed | tf_op | source)
XLA Modules:
  0.0 165.3 jit_solution(12952561007190313661)
XLA Ops:
  0.6 3.0 %collective-permute-start.2 = (bf16[128,3072]{1,0:T(8,128)(2,1)}, bf16[128,3072]{1,0:T(8,128)(2,1)}, u32[]{:S(2)}, u32[]{:S(2)}) collective-permute-start(bf16[128,3072]{1,0:T(8,128)(2,1)} %bitcast.117), channel_id=1, source_target_pairs={{0,8},{4,12},{8,0},{12,4},{16,24},{20,28},{24,16},{28,20},{1,9},{5... | collective-permute-start | bytes 2359304 | tf_op jit(solution)/shard_map/ppermute | solution.py:12
  3.6 1.5 collective-permute-start.5
  5.7 2.1 %constant_dynamic-update-slice_fusion.9 = bf16[1024,3072]{1,0:T(8,128)(2,1)} fusion(bf16[1,128,3072]{2,1,0:T(8,128)(2,1)} %param.4), kind=kLoop, calls=%fused_computation.112 | loop fusion | bytes 1572864
  7.8 2.4 %constant_dynamic-update-slice_fusion.1 = bf16[3072,1024]{1,0:T(8,128)(2,1)S(1)} fusion(bf16[3072,512]{1,0:T(8,128)(2,1)} %param.7), kind=kLoop, calls=%fused_computation.104 | loop fusion | bytes 6291456
  10.4 12.0 %collective-permute-done.2 = bf16[128,3072]{1,0:T(8,128)(2,1)} collective-permute-done((bf16[128,3072]{1,0:T(8,128)(2,1)}, bf16[128,3072]{1,0:T(8,128)(2,1)}, u32[]{:S(2)}, u32[]{:S(2)}) %collective-permute-start.2) | collective-permute-done | bytes 786464 | tf_op jit(solution)/shard_map/ppermute | solution.py:12
  23.5 16.3 %collective-permute-done.5 = bf16[128,3072]{1,0:T(8,128)(2,1)} collective-permute-done((bf16[128,3072]{1,0:T(8,128)(2,1)}, bf16[128,3072]{1,0:T(8,128)(2,1)}, u32[]{:S(2)}, u32[]{:S(2)}) %collective-permute-start.5) | collective-permute-done | bytes 786464 | tf_op jit(solution)/shard_map/ppermute | solution.py:12
  45.6 2.8 %fusion.50 = (bf16[128,1024]{1,0:T(8,128)(2,1)S(1)}, f32[128,1024]{1,0:T(8,128)S(1)}) fusion(bf16[128,3072]{1,0:T(8,128)(2,1)} %collective-permute-done.2, bf16[3072,1024]{1,0:T(8,128)(2,1)S(1)} %constant_dynamic-update-slice_fusion), kind=kOutput, calls=%fused_computation.118 | convolution fusion | flops 805830656 | bytes 7864320 | tf_op jit(solution)/shard_map/dot_general | solution.py:66
  48.5 2.2 %fusion.51 = (bf16[128,1024]{1,0:T(8,128)(2,1)S(1)}, f32[128,1024]{1,0:T(8,128)S(1)}) fusion(bf16[128,3072]{1,0:T(8,128)(2,1)} %collective-permute-done.5, bf16[3072,1024]{1,0:T(8,128)(2,1)S(1)} %constant_dynamic-update-slice_fusion), kind=kOutput, calls=%fused_computation.119 | convolution fusion | flops 805830656 | bytes 7864320 | tf_op jit(solution)/shard_map/dot_general | solution.py:66
  50.8 2.1 %collective-permute-start.11 = (bf16[128,1024]{1,0:T(8,128)(2,1)S(1)}, bf16[128,1024]{1,0:T(8,128)(2,1)S(1)}, u32[]{:S(2)}, u32[]{:S(2)}) collective-permute-start(bf16[128,1024]{1,0:T(8,128)(2,1)S(1)} %get-tuple-element.37), channel_id=1, source_target_pairs={{0,16},{4,20},{8,24},{12,28},{16,0},{20,4},{24,8},{28,12},{1,17},{... | collective-permute-start | bytes 786440 | tf_op jit(solution)/shard_map/ppermute | solution.py:12
  52.9 2.2 %fusion.52 = (bf16[128,1024]{1,0:T(8,128)(2,1)S(1)}, f32[128,1024]{1,0:T(8,128)S(1)}) fusion(bf16[128,3072]{1,0:T(8,128)(2,1)} %collective-permute-done.8, bf16[3072,1024]{1,0:T(8,128)(2,1)S(1)} %constant_dynamic-update-slice_fusion), kind=kOutput, calls=%fused_computation.120 | convolution fusion | flops 805830656 | bytes 7864320 | tf_op jit(solution)/shard_map/dot_general | solution.py:66
  55.1 1.5 collective-permute-start.12
  57.0 7.8 %collective-permute-done.11 = bf16[128,1024]{1,0:T(8,128)(2,1)S(1)} collective-permute-done((bf16[128,1024]{1,0:T(8,128)(2,1)S(1)}, bf16[128,1024]{1,0:T(8,128)(2,1)S(1)}, u32[]{:S(2)}, u32[]{:S(2)}) %collective-permute-start.11) | collective-permute-done | bytes 262176 | tf_op jit(solution)/shard_map/ppermute | solution.py:12
  65.2 2.7 %collective-permute-start.7 = (bf16[128,1024]{1,0:T(8,128)(2,1)S(1)}, bf16[128,1024]{1,0:T(8,128)(2,1)S(1)}, u32[]{:S(2)}, u32[]{:S(2)}) collective-permute-start(bf16[128,1024]{1,0:T(8,128)(2,1)S(1)} %multiply_convert_fusion.1), channel_id=1, source_target_pairs={{0,24},{4,28},{8,16},{12,20},{16,8},{20,12},{24,0},{28,4},{1,25},{... | collective-permute-start | bytes 786440 | tf_op jit(solution)/shard_map/ppermute | solution.py:12
  69.2 6.3 %collective-permute-done.7 = bf16[128,1024]{1,0:T(8,128)(2,1)S(1)} collective-permute-done((bf16[128,1024]{1,0:T(8,128)(2,1)S(1)}, bf16[128,1024]{1,0:T(8,128)(2,1)S(1)}, u32[]{:S(2)}, u32[]{:S(2)}) %collective-permute-start.7) | collective-permute-done | bytes 262176 | tf_op jit(solution)/shard_map/ppermute | solution.py:12
  75.6 3.4 %collective-permute-done.4 = bf16[128,1024]{1,0:T(8,128)(2,1)S(1)} collective-permute-done((bf16[128,1024]{1,0:T(8,128)(2,1)S(1)}, bf16[128,1024]{1,0:T(8,128)(2,1)S(1)}, u32[]{:S(2)}, u32[]{:S(2)}) %collective-permute-start.4) | collective-permute-done | bytes 262176 | tf_op jit(solution)/shard_map/ppermute | solution.py:12
  79.6 3.1 %convolution_convert_fusion = bf16[128,3072]{1,0:T(8,128)(2,1)} fusion(bf16[128,1024]{1,0:T(8,128)(2,1)S(1)} %multiply_convert_fusion, bf16[3072,1024]{1,0:T(8,128)(2,1)S(1)} %constant_dynamic-update-slice_fusion), kind=kOutput, calls=%fused_computation.3 | convolution fusion | flops 805699584 | bytes 7340032 | tf_op jit(solution)/shard_map/dot_general | solution.py:70
  82.7 1.9 %fusion.23 = f32[3072,256]{0,1:T(8,128)S(1)} fusion(bf16[1024,3072]{1,0:T(8,128)(2,1)S(1)} %constant_dynamic-update-slice_fusion.2, bf16[512,512]{1,0:T(8,128)(2,1)S(1)} %collective-permute-done.17, bf16[512,512]{1,0:T(8,128)(2,1)S(1)} %get-tuple-element.14), kind=kOutput, calls=%fused_computation.49 | convolution fusion | flops 1611661312 | bytes 10485760 | tf_op jit(solution)/shard_map/dot_general | solution.py:81
  84.7 3.7 %collective-permute-start.24 = (bf16[768,256]{0,1:T(8,128)(2,1)S(1)}, bf16[768,256]{0,1:T(8,128)(2,1)S(1)}, u32[]{:S(2)}, u32[]{:S(2)}) collective-permute-start(bf16[768,256]{0,1:T(8,128)(2,1)S(1)} %get-tuple-element.12), channel_id=1, source_target_pairs={{0,1},{4,5},{8,9},{12,13},{16,17},{20,21},{24,25},{28,29}} | collective-permute-start | bytes 1179656 | tf_op jit(solution)/shard_map/ppermute | solution.py:16
  88.4 1.9 %fusion.21 = f32[3072,256]{0,1:T(8,128)S(1)} fusion(bf16[1024,3072]{1,0:T(8,128)(2,1)S(1)} %constant_dynamic-update-slice_fusion.2, bf16[512,512]{1,0:T(8,128)(2,1)S(1)} %get-tuple-element.14, bf16[512,512]{1,0:T(8,128)(2,1)S(1)} %collective-permute-done.17), kind=kOutput, calls=%fused_computation.47 | convolution fusion | flops 1611661312 | bytes 10485760 | tf_op jit(solution)/shard_map/dot_general | solution.py:81
  91.8 3.1 %convolution_convert_fusion.1 = bf16[128,3072]{1,0:T(8,128)(2,1)} fusion(bf16[128,1024]{1,0:T(8,128)(2,1)S(1)} %multiply_convert_fusion.2, bf16[3072,1024]{1,0:T(8,128)(2,1)S(1)} %constant_dynamic-update-slice_fusion), kind=kOutput, calls=%fused_computation.4 | convolution fusion | flops 805699584 | bytes 7340032 | tf_op jit(solution)/shard_map/dot_general | solution.py:70
  97.7 4.4 %collective-permute-start.25 = (bf16[768,256]{0,1:T(8,128)(2,1)S(1)}, bf16[768,256]{0,1:T(8,128)(2,1)S(1)}, u32[]{:S(2)}, u32[]{:S(2)}) collective-permute-start(bf16[768,256]{0,1:T(8,128)(2,1)S(1)} %add_convert_fusion.3), channel_id=1, source_target_pairs={{0,1},{1,2},{4,5},{5,6},{8,9},{9,10},{12,13},{13,14},{16,17},{17,1... | collective-permute-start | bytes 1179656 | tf_op jit(solution)/shard_map/ppermute | solution.py:16
  102.2 3.9 %collective-permute-done.18 = bf16[768,256]{0,1:T(8,128)(2,1)S(1)} collective-permute-done((bf16[768,256]{0,1:T(8,128)(2,1)S(1)}, bf16[768,256]{0,1:T(8,128)(2,1)S(1)}, u32[]{:S(2)}, u32[]{:S(2)}) %collective-permute-start.18) | collective-permute-done | bytes 393248 | tf_op jit(solution)/shard_map/ppermute | solution.py:16
  106.2 4.4 %collective-permute-start.19 = (bf16[768,256]{0,1:T(8,128)(2,1)S(1)}, bf16[768,256]{0,1:T(8,128)(2,1)S(1)}, u32[]{:S(2)}, u32[]{:S(2)}) collective-permute-start(bf16[768,256]{0,1:T(8,128)(2,1)S(1)} %add_convert_fusion.7), channel_id=1, source_target_pairs={{0,1},{1,2},{4,5},{5,6},{8,9},{9,10},{12,13},{13,14},{16,17},{17,1... | collective-permute-start | bytes 1179656 | tf_op jit(solution)/shard_map/ppermute | solution.py:16
  110.6 3.1 %convolution_convert_fusion.2 = bf16[128,3072]{1,0:T(8,128)(2,1)} fusion(bf16[128,1024]{1,0:T(8,128)(2,1)S(1)} %multiply_convert_fusion.4, bf16[3072,1024]{1,0:T(8,128)(2,1)S(1)} %constant_dynamic-update-slice_fusion), kind=kOutput, calls=%fused_computation.5 | convolution fusion | flops 805699584 | bytes 7340032 | tf_op jit(solution)/shard_map/dot_general | solution.py:70
  113.7 1.7 %collective-permute-start.9 = (bf16[128,3072]{1,0:T(8,128)(2,1)}, bf16[128,3072]{1,0:T(8,128)(2,1)}, u32[]{:S(2)}, u32[]{:S(2)}) collective-permute-start(bf16[128,3072]{1,0:T(8,128)(2,1)} %convolution_convert_fusion), channel_id=1, source_target_pairs={{0,24},{4,28},{8,16},{12,20},{16,8},{20,12},{24,0},{28,4},{1,25},{... | collective-permute-start | bytes 2359304 | tf_op jit(solution)/shard_map/ppermute | solution.py:12
  119.8 2.7 %collective-permute-done.19 = bf16[768,256]{0,1:T(8,128)(2,1)S(1)} collective-permute-done((bf16[768,256]{0,1:T(8,128)(2,1)S(1)}, bf16[768,256]{0,1:T(8,128)(2,1)S(1)}, u32[]{:S(2)}, u32[]{:S(2)}) %collective-permute-start.19) | collective-permute-done | bytes 393248 | tf_op jit(solution)/shard_map/ppermute | solution.py:16
  125.1 9.7 %collective-permute-start.26 = (bf16[768,256]{0,1:T(8,128)(2,1)}, bf16[768,256]{0,1:T(8,128)(2,1)S(1)}, u32[]{:S(2)}, u32[]{:S(2)}) collective-permute-start(bf16[768,256]{0,1:T(8,128)(2,1)} %get-tuple-element.10), channel_id=1, source_target_pairs={{0,1},{1,2},{2,3},{4,5},{5,6},{6,7},{8,9},{9,10},{10,11},{12,13},{... | collective-permute-start | bytes 1179656 | tf_op jit(solution)/shard_map/ppermute | solution.py:16
  136.1 6.0 %collective-permute-start.20 = (bf16[768,256]{0,1:T(8,128)(2,1)}, bf16[768,256]{0,1:T(8,128)(2,1)S(1)}, u32[]{:S(2)}, u32[]{:S(2)}) collective-permute-start(bf16[768,256]{0,1:T(8,128)(2,1)} %get-tuple-element.6), channel_id=1, source_target_pairs={{0,1},{1,2},{2,3},{4,5},{5,6},{6,7},{8,9},{9,10},{10,11},{12,13},{... | collective-permute-start | bytes 1179656 | tf_op jit(solution)/shard_map/ppermute | solution.py:16
  144.6 5.6 %collective-permute-done.6 = bf16[128,3072]{1,0:T(8,128)(2,1)} collective-permute-done((bf16[128,3072]{1,0:T(8,128)(2,1)}, bf16[128,3072]{1,0:T(8,128)(2,1)}, u32[]{:S(2)}, u32[]{:S(2)}) %collective-permute-start.6) | collective-permute-done | bytes 786464 | tf_op jit(solution)/shard_map/ppermute | solution.py:12
  151.5 6.6 %fusion.3 = bf16[1,128,3072]{2,1,0:T(8,128)(2,1)} fusion(bf16[128,1024]{1,0:T(8,128)(2,1)S(1)} %multiply_convert_fusion.6, bf16[3072,1024]{1,0:T(8,128)(2,1)} %copy-done, bf16[128,3072]{1,0:T(8,128)(2,1)} %collective-permute-done.9, bf16[128,3072]{1,0:T(8,128)(2,1)} %collective-permute-done.6, bf16[128,3072]{1,0:T(8,128)(2,1)} %collective-permute-done.3), kind=kOutput, calls=%fused_computation.7 | convolution fusion | flops 808058880 | bytes 9699328 | tf_op jit(solution)/shard_map/dot_general | solution.py:70
  159.4 4.0 %collective-permute-done.23 = bf16[768,256]{0,1:T(8,128)(2,1)S(1)} collective-permute-done((bf16[768,256]{0,1:T(8,128)(2,1)S(1)}, bf16[768,256]{0,1:T(8,128)(2,1)S(1)}, u32[]{:S(2)}, u32[]{:S(2)}) %collective-permute-start.23) | collective-permute-done | bytes 393248 | tf_op jit(solution)/shard_map/ppermute | solution.py:16
  163.7 1.6 copy.7
  (93 shorter events, 28.2 us)
Async XLA Ops:
  0.6 21.7 %collective-permute-start.2 = (bf16[128,3072]{1,0:T(8,128)(2,1)}, bf16[128,3072]{1,0:T(8,128)(2,1)}, u32[]{:S(2)}, u32[]{:S(2)}) collective-permute-start(bf16[128,3072]{1,0:T(8,128)(2,1)} %bitcast.117), channel_id=1, source_target_pairs={{0,8},{4,12},{8,0},{12,4},{16,24},{20,28},{24,16},{28,20},{1,9},{5... | collective-permute-start | bytes 2359304 | tf_op jit(solution)/shard_map/ppermute | solution.py:12
  3.6 36.2 %collective-permute-start.5 = (bf16[128,3072]{1,0:T(8,128)(2,1)}, bf16[128,3072]{1,0:T(8,128)(2,1)}, u32[]{:S(2)}, u32[]{:S(2)}) collective-permute-start(bf16[128,3072]{1,0:T(8,128)(2,1)} %bitcast.118), channel_id=1, source_target_pairs={{0,16},{4,20},{8,24},{12,28},{16,0},{20,4},{24,8},{28,12},{1,17},{... | collective-permute-start | bytes 2359304 | tf_op jit(solution)/shard_map/ppermute | solution.py:12
  5.2 35.9 %collective-permute-start.8 = (bf16[128,3072]{1,0:T(8,128)(2,1)}, bf16[128,3072]{1,0:T(8,128)(2,1)}, u32[]{:S(2)}, u32[]{:S(2)}) collective-permute-start(bf16[128,3072]{1,0:T(8,128)(2,1)} %bitcast.119), channel_id=1, source_target_pairs={{0,24},{4,28},{8,16},{12,20},{16,8},{20,12},{24,0},{28,4},{1,25},{... | collective-permute-start | bytes 2359304 | tf_op jit(solution)/shard_map/ppermute | solution.py:12
  5.2 37.6 %collective-permute-start.13 = (bf16[128,3072]{1,0:T(8,128)(2,1)}, bf16[128,3072]{1,0:T(8,128)(2,1)}, u32[]{:S(2)}, u32[]{:S(2)}) collective-permute-start(bf16[128,3072]{1,0:T(8,128)(2,1)} %bitcast.120), channel_id=1, source_target_pairs={{0,4},{4,0},{8,12},{12,8},{16,20},{20,16},{24,28},{28,24},{1,5},{5... | collective-permute-start | bytes 2359304 | tf_op jit(solution)/shard_map/ppermute | solution.py:12
  5.2 38.9 %collective-permute-start = (bf16[3072,512]{1,0:T(8,128)(2,1)}, bf16[3072,512]{1,0:T(8,128)(2,1)S(1)}, u32[]{:S(2)}, u32[]{:S(2)}) collective-permute-start(bf16[3072,512]{1,0:T(8,128)(2,1)} %param.7), channel_id=1, source_target_pairs={{0,4},{4,0},{8,12},{12,8},{16,20},{20,16},{24,28},{28,24},{1,5},{5... | collective-permute-start | bytes 9437192 | tf_op jit(solution)/shard_map/ppermute | solution.py:12
  22.3 21.7 %collective-permute-start.14 = (bf16[128,3072]{1,0:T(8,128)(2,1)}, bf16[128,3072]{1,0:T(8,128)(2,1)S(1)}, u32[]{:S(2)}, u32[]{:S(2)}) collective-permute-start(bf16[128,3072]{1,0:T(8,128)(2,1)} %collective-permute-done.2), channel_id=1, source_target_pairs={{0,4},{4,0},{8,12},{12,8},{16,20},{20,16},{24,28},{28,24},{1,5},{5... | collective-permute-start | bytes 2359304 | tf_op jit(solution)/shard_map/ppermute | solution.py:12
  39.8 4.2 %collective-permute-start.15 = (bf16[128,3072]{1,0:T(8,128)(2,1)}, bf16[128,3072]{1,0:T(8,128)(2,1)S(1)}, u32[]{:S(2)}, u32[]{:S(2)}) collective-permute-start(bf16[128,3072]{1,0:T(8,128)(2,1)} %collective-permute-done.5), channel_id=1, source_target_pairs={{0,4},{4,0},{8,12},{12,8},{16,20},{20,16},{24,28},{28,24},{1,5},{5... | collective-permute-start | bytes 2359304 | tf_op jit(solution)/shard_map/ppermute | solution.py:12
  41.0 38.6 %collective-permute-start.16 = (bf16[128,3072]{1,0:T(8,128)(2,1)}, bf16[128,3072]{1,0:T(8,128)(2,1)S(1)}, u32[]{:S(2)}, u32[]{:S(2)}) collective-permute-start(bf16[128,3072]{1,0:T(8,128)(2,1)} %collective-permute-done.8), channel_id=1, source_target_pairs={{0,4},{4,0},{8,12},{12,8},{16,20},{20,16},{24,28},{28,24},{1,5},{5... | collective-permute-start | bytes 2359304 | tf_op jit(solution)/shard_map/ppermute | solution.py:12
  44.5 66.1 %copy-start = (bf16[3072,1024]{1,0:T(8,128)(2,1)}, bf16[3072,1024]{1,0:T(8,128)(2,1)S(1)}, u32[]{:S(2)}) copy-start(bf16[3072,1024]{1,0:T(8,128)(2,1)S(1)} %constant_dynamic-update-slice_fusion) | copy-start | bytes 18874372
  48.5 8.4 %collective-permute-start.10 = (bf16[128,1024]{1,0:T(8,128)(2,1)S(1)}, bf16[128,1024]{1,0:T(8,128)(2,1)S(1)}, u32[]{:S(2)}, u32[]{:S(2)}) collective-permute-start(bf16[128,1024]{1,0:T(8,128)(2,1)S(1)} %get-tuple-element.35), channel_id=1, source_target_pairs={{0,8},{4,12},{8,0},{12,4},{16,24},{20,28},{24,16},{28,20},{1,9},{5... | collective-permute-start | bytes 786440 | tf_op jit(solution)/shard_map/ppermute | solution.py:12
  50.8 14.0 %collective-permute-start.11 = (bf16[128,1024]{1,0:T(8,128)(2,1)S(1)}, bf16[128,1024]{1,0:T(8,128)(2,1)S(1)}, u32[]{:S(2)}, u32[]{:S(2)}) collective-permute-start(bf16[128,1024]{1,0:T(8,128)(2,1)S(1)} %get-tuple-element.37), channel_id=1, source_target_pairs={{0,16},{4,20},{8,24},{12,28},{16,0},{20,4},{24,8},{28,12},{1,17},{... | collective-permute-start | bytes 786440 | tf_op jit(solution)/shard_map/ppermute | solution.py:12
  55.1 9.7 %collective-permute-start.12 = (bf16[128,1024]{1,0:T(8,128)(2,1)S(1)}, bf16[128,1024]{1,0:T(8,128)(2,1)S(1)}, u32[]{:S(2)}, u32[]{:S(2)}) collective-permute-start(bf16[128,1024]{1,0:T(8,128)(2,1)S(1)} %get-tuple-element.39), channel_id=1, source_target_pairs={{0,24},{4,28},{8,16},{12,20},{16,8},{20,12},{24,0},{28,4},{1,25},{... | collective-permute-start | bytes 786440 | tf_op jit(solution)/shard_map/ppermute | solution.py:12
  65.2 10.3 %collective-permute-start.7 = (bf16[128,1024]{1,0:T(8,128)(2,1)S(1)}, bf16[128,1024]{1,0:T(8,128)(2,1)S(1)}, u32[]{:S(2)}, u32[]{:S(2)}) collective-permute-start(bf16[128,1024]{1,0:T(8,128)(2,1)S(1)} %multiply_convert_fusion.1), channel_id=1, source_target_pairs={{0,24},{4,28},{8,16},{12,20},{16,8},{20,12},{24,0},{28,4},{1,25},{... | collective-permute-start | bytes 786440 | tf_op jit(solution)/shard_map/ppermute | solution.py:12
  68.0 10.9 %collective-permute-start.4 = (bf16[128,1024]{1,0:T(8,128)(2,1)S(1)}, bf16[128,1024]{1,0:T(8,128)(2,1)S(1)}, u32[]{:S(2)}, u32[]{:S(2)}) collective-permute-start(bf16[128,1024]{1,0:T(8,128)(2,1)S(1)} %multiply_convert_fusion.3), channel_id=1, source_target_pairs={{0,16},{4,20},{8,24},{12,28},{16,0},{20,4},{24,8},{28,12},{1,17},{... | collective-permute-start | bytes 786440 | tf_op jit(solution)/shard_map/ppermute | solution.py:12
  68.7 10.6 %collective-permute-start.1 = (bf16[128,1024]{1,0:T(8,128)(2,1)S(1)}, bf16[128,1024]{1,0:T(8,128)(2,1)S(1)}, u32[]{:S(2)}, u32[]{:S(2)}) collective-permute-start(bf16[128,1024]{1,0:T(8,128)(2,1)S(1)} %multiply_convert_fusion.5), channel_id=1, source_target_pairs={{0,8},{4,12},{8,0},{12,4},{16,24},{20,28},{24,16},{28,20},{1,9},{5... | collective-permute-start | bytes 786440 | tf_op jit(solution)/shard_map/ppermute | solution.py:12
  79.5 3.2 %collective-permute-start.17 = (bf16[512,512]{1,0:T(8,128)(2,1)S(1)}, bf16[512,512]{1,0:T(8,128)(2,1)S(1)}, u32[]{:S(2)}, u32[]{:S(2)}) collective-permute-start(bf16[512,512]{1,0:T(8,128)(2,1)S(1)} %get-tuple-element.15), channel_id=1, source_target_pairs={{0,4},{4,0},{8,12},{12,8},{16,20},{20,16},{24,28},{28,24},{1,5},{5... | collective-permute-start | bytes 1572872 | tf_op jit(solution)/shard_map/ppermute | solution.py:12
  84.6 32.6 %copy-start.1 = (f32[3072,256]{0,1:T(8,128)}, f32[3072,256]{0,1:T(8,128)S(1)}, u32[]{:S(2)}) copy-start(f32[3072,256]{0,1:T(8,128)S(1)} %fusion.23) | copy-start | bytes 9437188
  84.7 12.9 %collective-permute-start.24 = (bf16[768,256]{0,1:T(8,128)(2,1)S(1)}, bf16[768,256]{0,1:T(8,128)(2,1)S(1)}, u32[]{:S(2)}, u32[]{:S(2)}) collective-permute-start(bf16[768,256]{0,1:T(8,128)(2,1)S(1)} %get-tuple-element.12), channel_id=1, source_target_pairs={{0,1},{4,5},{8,9},{12,13},{16,17},{20,21},{24,25},{28,29}} | collective-permute-start | bytes 1179656 | tf_op jit(solution)/shard_map/ppermute | solution.py:16
  90.5 15.6 %collective-permute-start.18 = (bf16[768,256]{0,1:T(8,128)(2,1)S(1)}, bf16[768,256]{0,1:T(8,128)(2,1)S(1)}, u32[]{:S(2)}, u32[]{:S(2)}) collective-permute-start(bf16[768,256]{0,1:T(8,128)(2,1)S(1)} %get-tuple-element.8), channel_id=1, source_target_pairs={{0,1},{4,5},{8,9},{12,13},{16,17},{20,21},{24,25},{28,29}} | collective-permute-start | bytes 1179656 | tf_op jit(solution)/shard_map/ppermute | solution.py:16
  94.9 20.5 %collective-permute-start.27 = (bf16[768,256]{0,1:T(8,128)(2,1)S(1)}, bf16[768,256]{0,1:T(8,128)(2,1)S(1)}, u32[]{:S(2)}, u32[]{:S(2)}) collective-permute-start(bf16[768,256]{0,1:T(8,128)(2,1)S(1)} %get-tuple-element.13), channel_id=1, source_target_pairs={{3,2},{7,6},{11,10},{15,14},{19,18},{23,22},{27,26},{31,30}} | collective-permute-start | bytes 1179656 | tf_op jit(solution)/shard_map/ppermute | solution.py:16
  95.6 22.8 %collective-permute-start.21 = (bf16[768,256]{0,1:T(8,128)(2,1)S(1)}, bf16[768,256]{0,1:T(8,128)(2,1)S(1)}, u32[]{:S(2)}, u32[]{:S(2)}) collective-permute-start(bf16[768,256]{0,1:T(8,128)(2,1)S(1)} %get-tuple-element.9), channel_id=1, source_target_pairs={{3,2},{7,6},{11,10},{15,14},{19,18},{23,22},{27,26},{31,30}} | collective-permute-start | bytes 1179656 | tf_op jit(solution)/shard_map/ppermute | solution.py:16
  97.7 18.9 %collective-permute-start.25 = (bf16[768,256]{0,1:T(8,128)(2,1)S(1)}, bf16[768,256]{0,1:T(8,128)(2,1)S(1)}, u32[]{:S(2)}, u32[]{:S(2)}) collective-permute-start(bf16[768,256]{0,1:T(8,128)(2,1)S(1)} %add_convert_fusion.3), channel_id=1, source_target_pairs={{0,1},{1,2},{4,5},{5,6},{8,9},{9,10},{12,13},{13,14},{16,17},{17,1... | collective-permute-start | bytes 1179656 | tf_op jit(solution)/shard_map/ppermute | solution.py:16
  106.2 16.3 %collective-permute-start.19 = (bf16[768,256]{0,1:T(8,128)(2,1)S(1)}, bf16[768,256]{0,1:T(8,128)(2,1)S(1)}, u32[]{:S(2)}, u32[]{:S(2)}) collective-permute-start(bf16[768,256]{0,1:T(8,128)(2,1)S(1)} %add_convert_fusion.7), channel_id=1, source_target_pairs={{0,1},{1,2},{4,5},{5,6},{8,9},{9,10},{12,13},{13,14},{16,17},{17,1... | collective-permute-start | bytes 1179656 | tf_op jit(solution)/shard_map/ppermute | solution.py:16
  113.7 29.6 %collective-permute-start.9 = (bf16[128,3072]{1,0:T(8,128)(2,1)}, bf16[128,3072]{1,0:T(8,128)(2,1)}, u32[]{:S(2)}, u32[]{:S(2)}) collective-permute-start(bf16[128,3072]{1,0:T(8,128)(2,1)} %convolution_convert_fusion), channel_id=1, source_target_pairs={{0,24},{4,28},{8,16},{12,20},{16,8},{20,12},{24,0},{28,4},{1,25},{... | collective-permute-start | bytes 2359304 | tf_op jit(solution)/shard_map/ppermute | solution.py:12
  115.4 34.8 %collective-permute-start.6 = (bf16[128,3072]{1,0:T(8,128)(2,1)}, bf16[128,3072]{1,0:T(8,128)(2,1)}, u32[]{:S(2)}, u32[]{:S(2)}) collective-permute-start(bf16[128,3072]{1,0:T(8,128)(2,1)} %convolution_convert_fusion.1), channel_id=1, source_target_pairs={{0,16},{4,20},{8,24},{12,28},{16,0},{20,4},{24,8},{28,12},{1,17},{... | collective-permute-start | bytes 2359304 | tf_op jit(solution)/shard_map/ppermute | solution.py:12
  116.7 34.9 %collective-permute-start.3 = (bf16[128,3072]{1,0:T(8,128)(2,1)}, bf16[128,3072]{1,0:T(8,128)(2,1)}, u32[]{:S(2)}, u32[]{:S(2)}) collective-permute-start(bf16[128,3072]{1,0:T(8,128)(2,1)} %convolution_convert_fusion.2), channel_id=1, source_target_pairs={{0,8},{4,12},{8,0},{12,4},{16,24},{20,28},{24,16},{28,20},{1,9},{5... | collective-permute-start | bytes 2359304 | tf_op jit(solution)/shard_map/ppermute | solution.py:12
  118.3 6.7 %collective-permute-start.28 = (bf16[768,256]{0,1:T(8,128)(2,1)}, bf16[768,256]{0,1:T(8,128)(2,1)}, u32[]{:S(2)}, u32[]{:S(2)}) collective-permute-start(bf16[768,256]{0,1:T(8,128)(2,1)} %get-tuple-element.11), channel_id=1, source_target_pairs={{2,1},{3,2},{6,5},{7,6},{10,9},{11,10},{14,13},{15,14},{18,17},{19... | collective-permute-start | bytes 1179656 | tf_op jit(solution)/shard_map/ppermute | solution.py:16
  123.7 12.5 %collective-permute-start.22 = (bf16[768,256]{0,1:T(8,128)(2,1)}, bf16[768,256]{0,1:T(8,128)(2,1)}, u32[]{:S(2)}, u32[]{:S(2)}) collective-permute-start(bf16[768,256]{0,1:T(8,128)(2,1)} %get-tuple-element.7), channel_id=1, source_target_pairs={{2,1},{3,2},{6,5},{7,6},{10,9},{11,10},{14,13},{15,14},{18,17},{19... | collective-permute-start | bytes 1179656 | tf_op jit(solution)/shard_map/ppermute | solution.py:16
  125.1 33.1 %collective-permute-start.26 = (bf16[768,256]{0,1:T(8,128)(2,1)}, bf16[768,256]{0,1:T(8,128)(2,1)S(1)}, u32[]{:S(2)}, u32[]{:S(2)}) collective-permute-start(bf16[768,256]{0,1:T(8,128)(2,1)} %get-tuple-element.10), channel_id=1, source_target_pairs={{0,1},{1,2},{2,3},{4,5},{5,6},{6,7},{8,9},{9,10},{10,11},{12,13},{... | collective-permute-start | bytes 1179656 | tf_op jit(solution)/shard_map/ppermute | solution.py:16
  136.1 23.3 %collective-permute-start.20 = (bf16[768,256]{0,1:T(8,128)(2,1)}, bf16[768,256]{0,1:T(8,128)(2,1)S(1)}, u32[]{:S(2)}, u32[]{:S(2)}) collective-permute-start(bf16[768,256]{0,1:T(8,128)(2,1)} %get-tuple-element.6), channel_id=1, source_target_pairs={{0,1},{1,2},{2,3},{4,5},{5,6},{6,7},{8,9},{9,10},{10,11},{12,13},{... | collective-permute-start | bytes 1179656 | tf_op jit(solution)/shard_map/ppermute | solution.py:16
  143.3 14.9 %collective-permute-start.29 = (bf16[768,256]{0,1:T(8,128)(2,1)S(1)}, bf16[768,256]{0,1:T(8,128)(2,1)S(1)}, u32[]{:S(2)}, u32[]{:S(2)}) collective-permute-start(bf16[768,256]{0,1:T(8,128)(2,1)S(1)} %add_convert_fusion), channel_id=1, source_target_pairs={{1,0},{2,1},{3,2},{5,4},{6,5},{7,6},{9,8},{10,9},{11,10},{13,12},{... | collective-permute-start | bytes 1179656 | tf_op jit(solution)/shard_map/ppermute | solution.py:16
  150.2 13.2 %collective-permute-start.23 = (bf16[768,256]{0,1:T(8,128)(2,1)S(1)}, bf16[768,256]{0,1:T(8,128)(2,1)S(1)}, u32[]{:S(2)}, u32[]{:S(2)}) collective-permute-start(bf16[768,256]{0,1:T(8,128)(2,1)S(1)} %add_convert_fusion.4), channel_id=1, source_target_pairs={{1,0},{2,1},{3,2},{5,4},{6,5},{7,6},{9,8},{10,9},{11,10},{13,12},{... | collective-permute-start | bytes 1179656 | tf_op jit(solution)/shard_map/ppermute | solution.py:16
  (5 other events, 40.6 us)

commit v2 on v1

v2 whole, which is shorter than its diff:
```python
import functools

import jax
import jax.numpy as jnp
from jax import lax
from jax.experimental import pallas as pl
from jax.experimental.pallas import tpu as pltpu
from jax.sharding import PartitionSpec as P

BF16 = jnp.bfloat16
F32 = jnp.float32
LIMIT = 24 << 20
ROWS = (((0,), (0,)), ((), ()))
COLUMNS = (((1,), (1,)), ((), ()))


def swap(x, mask):
    count = lax.axis_size("tensor")
    return lax.ppermute(x, "tensor", [(i, i ^ mask) for i in range(count)])


def along_dp(x, pairs):
    return lax.ppermute(x, "dp", pairs)


def tie(*groups):
    return lax.optimization_barrier(groups)


def call(kernel, name, out_shapes, *operands):
    spec = pl.BlockSpec(memory_space=pltpu.VMEM)
    return pl.pallas_call(
        kernel,
        in_specs=[spec] * len(operands),
        out_specs=[spec] * len(out_shapes),
        out_shape=[jax.ShapeDtypeStruct(shape, dtype) for shape, dtype in out_shapes],
        compiler_params=pltpu.CompilerParams(vmem_limit_bytes=LIMIT),
        name=name,
    )(*[pltpu.with_memory_space_constraint(x, pltpu.VMEM) for x in operands])


def stack(refs):
    return jnp.concatenate([ref[...] for ref in refs], 0)


def columns_at(index, width):
    return pl.ds(pl.multiple_of(index * width, width), width)


def chip_columns(m, which, width):
    myself = lax.axis_index("tensor")
    return columns_at(myself ^ (2 * m + which), width)


def product_kernel(width, g_ref, a_ref, *outs):
    for m, out_ref in enumerate(outs):
        for which in range(2):
            cols = chip_columns(m, which, width)
            product = (g_ref[:, cols].astype(F32) * a_ref[:, cols].astype(F32)).astype(BF16)
            out_ref[:, which * width : (which + 1) * width] = product


def products(cot, att, chips, width):
    kernel = functools.partial(product_kernel, width)
    return call(kernel, "products", [((cot.shape[0], 2 * width), BF16)] * chips, cot, att)


def half_kernel(pairs, *refs):
    x_refs, outs = refs[: 2 * pairs], refs[2 * pairs :]
    rows = outs[0].shape[0]
    for i in range(pairs):
        outs[2 * i][...] = x_refs[2 * i][:rows]
        outs[2 * i + 1][...] = x_refs[2 * i + 1][rows:]


def halves(xs):
    shape = (xs[0].shape[0] // 2, xs[0].shape[1])
    return call(functools.partial(half_kernel, len(xs) // 2), "halves", [(shape, BF16)] * len(xs), *xs)


def gate_kernel(xs, gas, *refs):
    x_refs, ga_refs = refs[:xs], refs[xs : xs + gas]
    w_refs, gp_ref, gate_ref = refs[xs + gas : xs + gas + 2], *refs[xs + gas + 2 :]
    x = stack(x_refs)
    width = w_refs[0].shape[1]
    for i, w_ref in enumerate(w_refs):
        cols = slice(i * width, (i + 1) * width)
        gate = jax.nn.sigmoid(jnp.dot(x, w_ref[...], preferred_element_type=F32))
        product = jnp.concatenate([ref[:, cols] for ref in ga_refs], 0).astype(F32)
        gp_ref[:, cols] = (product * gate * (1.0 - gate)).astype(BF16)
        gate_ref[:, cols] = gate.astype(BF16)


def gate_terms(xs, gas, weight, w_other):
    shape = (sum(x.shape[0] for x in xs), 2 * weight.shape[1])
    kernel = functools.partial(gate_kernel, len(xs), len(gas))
    return call(kernel, "gate_terms", [(shape, BF16)] * 2, *xs, *gas, weight, w_other)


def pick(index, table):
    value = jnp.int32(table[-1])
    for i, entry in enumerate(table[:-1]):
        value = jnp.where(index == i, entry, value)
    return value


def share_kernel(tables, rows, xs, *refs):
    x_refs, gp_refs, outs = refs[:xs], refs[xs : -2 * len(tables)], refs[-2 * len(tables) :]
    me = lax.axis_index("dp")
    gp = stack(gp_refs)
    width = outs[0].shape[1]
    for i, table in enumerate(tables):
        cols = columns_at(pick(me, table), rows)
        x = jnp.concatenate([ref[:, cols] for ref in x_refs], 0)
        share = lax.dot_general(x, gp, ROWS, preferred_element_type=F32)
        outs[2 * i][...] = share[:, :width]
        outs[2 * i + 1][...] = share[:, width:].astype(BF16)


def weight_shares(tables, xs, gps, count):
    width = gps[0].shape[1] // 2
    rows = xs[0].shape[1] // count
    shapes = [((rows, width), F32), ((rows, width), BF16)] * len(tables)
    return call(functools.partial(share_kernel, tables, rows, len(xs)), "weight_shares", shapes, *xs, *gps)


def return_kernel(own, gp_ref, gate_ref, w_ref, w_other_ref, *outs):
    width = gp_ref.shape[1] // 2
    tokens = outs[0].shape[0]
    depth = w_ref.shape[0]
    tile = min(depth, 1024)
    for at in range(0, depth, tile):
        rows = slice(at, at + tile)
        dx = lax.dot_general(gp_ref[:, :width], w_ref[rows], COLUMNS, preferred_element_type=F32)
        dx = dx + lax.dot_general(gp_ref[:, width:], w_other_ref[rows], COLUMNS, preferred_element_type=F32)
        for m, out_ref in enumerate(outs):
            out_ref[:, rows] = dx[m * tokens : (m + 1) * tokens].astype(out_ref.dtype)
    for m in range(own, len(outs)):
        outs[m][:, depth:] = gate_ref[m * tokens : (m + 1) * tokens]


def returns_of(own, gp, gate, weight, w_other, tokens):
    depth, width = weight.shape
    chips = gate.shape[0] // tokens
    shapes = [((tokens, depth), F32)] * own + [((tokens, depth + 2 * width), BF16)] * (chips - own)
    return call(functools.partial(return_kernel, own), "returns", shapes, gp, gate, weight, w_other)


def finish_kernel(chips, width, *refs):
    cot_ref, mine_ref, gate_ref = refs[:3]
    back, (input_ref, attn_ref) = refs[3:-2], refs[-2:]
    tokens, depth = mine_ref.shape
    total = mine_ref[...]
    for ref in back:
        total = total + ref[:, :depth].astype(F32)
    input_ref[...] = total.astype(BF16)
    for m in range(chips):
        for which in range(2):
            at = which * width
            gate = back[m - 1][:, depth + at : depth + at + width] if m else gate_ref[:tokens, at : at + width]
            cols = chip_columns(m, which, width)
            attn_ref[:, cols] = (cot_ref[:, cols].astype(F32) * gate.astype(F32)).astype(BF16)


def finish(cot, mine, gate, back, width):
    kernel = functools.partial(finish_kernel, len(back) + 1, width)
    return call(kernel, "finish", [(mine.shape, BF16), (cot.shape, BF16)], cot, mine, gate, *back)


def sum_over_line(share_of, count):
    me = lax.axis_index("dp")
    right = left = None
    for r in range(1, count):
        to_right = share_of(jnp.clip(me + count - r, 0, count - 1))
        to_left = share_of(jnp.clip(me - count + r, 0, count - 1))
        if r > 1:
            to_right = to_right + right.astype(F32)
            to_left = to_left + left.astype(F32)
        right = along_dp(to_right.astype(BF16), [(i, i + 1) for i in range(0, r)])
        left = along_dp(to_left.astype(BF16), [(i, i - 1) for i in range(count - r, count)])
    return share_of(me) + (right.astype(F32) + left.astype(F32))


def on_device(layer_input, attn_output, grad_gated, gate_weight):
    count = lax.axis_size("dp")
    chips = lax.axis_size("tensor") // 2
    depth, width = gate_weight.shape
    tokens = layer_input.shape[1]
    x0 = layer_input[0]
    cot = grad_gated[0]
    near = [1 << bit for bit in range(chips.bit_length() - 1)]
    far = [m for m in range(chips) if m and m not in near]

    xs = {0: [x0]}
    for m in near:
        xs[m] = [swap(x0, 2 * m)]
    w_other = swap(gate_weight, 1)
    ga = products(cot, attn_output[0], chips, width)
    ga, w_other = tie(ga, w_other)
    ga = [swap(piece, 2 * m) if m else piece for m, piece in enumerate(ga)]

    pairs = [m for m in far if (m & (m - 1)) in near]
    held, xs = tie([ga[m] for m in near], xs)
    for m, piece in zip(near, held):
        ga[m] = piece
    if pairs:
        out = halves([xs[bit][0] for m in pairs for bit in (m & -m, m & (m - 1))])
        out, xs = tie(out, xs)
    for m in far:
        if m in pairs:
            i = 2 * pairs.index(m)
            xs[m] = [swap(out[i], 2 * (m & (m - 1))), swap(out[i + 1], 2 * (m & -m))]
        else:
            xs[m] = [swap(x0, 2 * m)]

    def terms_of(some):
        return gate_terms([x for m in some for x in xs[m]], [ga[m] for m in some], gate_weight, w_other)

    first = [0] + near
    gp_near, gate_near = terms_of(first)
    mine, *returns = returns_of(1, gp_near, gate_near, gate_weight, w_other, tokens)
    xs, gp_near, returns = tie(xs, gp_near, returns)
    gps = [gp_near]
    if far:
        gp_far, gate_far = terms_of(far)
        gps.append(gp_far)
    x_list = [x for m in first + far for x in xs[m]]

    back = {m: swap(piece, 2 * m) for m, piece in zip(near, returns)}
    if count == 4:
        rows = depth // count
        own1, other1 = weight_shares([[3, 0, 3, 0]], x_list, gps, count)
        other1, gps = tie(other1, gps)
        other1 = swap(other1, 1)
        own2, other2, own3, other3, own4, other4 = weight_shares(
            [[2, 2, 1, 1], [1, 3, 0, 2], [0, 1, 2, 3]], x_list, gps, count
        )
        other1, other2, other3, other4 = tie(other1, other2, other3, other4)
        other2 = swap(other2, 1)
        message = (own1 + other1.astype(F32)).astype(BF16)
        message, other3, other4 = tie(message, other3, other4)
        ends = along_dp(message, [(0, 1), (1, 0), (2, 3), (3, 2)])
        other3, other4 = swap(other3, 1), swap(other4, 1)
        middle = (own2 + other2.astype(F32)).astype(BF16)
        inner = along_dp(middle, [(1, 2), (2, 1)])
    if far:
        returns = returns_of(0, gp_far, gate_far, gate_weight, w_other, tokens)
    if count == 4:
        kept = own3 + other3.astype(F32)
        own = own4 + other4.astype(F32)
        kept, own, middle, ends, inner, returns, back = tie(
            kept, own, middle, ends, inner, returns, back
        )
        me = lax.axis_index("dp")
        is_end = (me == 0) | (me == count - 1)
        passed = jnp.where(is_end, 0.0, ends.astype(F32))
        message = (kept + passed).astype(BF16)
        own = own + (ends.astype(F32) - passed) + inner.astype(F32)
        message, own, middle, returns = tie(message, own, middle, returns)
        last = along_dp(message, [(0, 1), (1, 3), (2, 0), (3, 2)])
        over = along_dp(middle, [(0, 2), (3, 1)])
    if far:
        back.update({m: swap(piece, 2 * m) for m, piece in zip(far, returns)})
    if count == 4:
        own = own + over.astype(F32)
    grad_input, grad_attn = finish(cot, mine, gate_near, [back[m] for m in range(1, chips)], width)
    if count == 4:
        own, last = tie(own, last)
        grad_weight = own + last.astype(F32)
    else:
        x_all = jnp.concatenate(x_list, 0)
        gp_all = jnp.concatenate(gps, 0)

        def share_of(k):
            cols = lax.dynamic_slice_in_dim(x_all, k * (depth // count), depth // count, 1)
            share = lax.dot_general(cols, gp_all, ROWS, preferred_element_type=F32)
            return share[:, :width] + swap(share[:, width:].astype(BF16), 1).astype(F32)

        grad_weight = sum_over_line(share_of, count)
    return (grad_input[None], grad_attn[None], grad_weight)


def solution(mesh):
    in_specs = (
        P("dp", "tensor", None),
        P("dp", "tensor", None),
        P("dp", "tensor", None),
        P(None, "tensor"),
    )
    out_specs = (P("dp", "tensor", None), P("dp", "tensor", None), P("dp", "tensor"))
    return jax.shard_map(
        on_device, mesh=mesh, in_specs=in_specs, out_specs=out_specs, check_vma=False
    )
```

time: 166 us -> 127 us (0.77)
  starting transfers between devices: 52.9 us -> 24.6 us
  matrix products: 28 us -> 0 us
  Pallas kernels: 0 us -> 17.2 us
  waiting for transfers between devices: 63.7 us -> 67.8 us
  local copies, waits for them, and re-layouts: 12 us -> 8.52 us
    dot_general x10 -> x0, matrix products: 28 us -> none  [the longest x4 15.8 us: on_device(): lax.dot_general(gp, w_both, (((1,), (1,)), ((), ())), preferred_element_t...]
    ppermute x12 -> x4, starting transfers between devices: 36.3 us -> 8.54 us  [along_dp(): return lax.ppermute(x, 'dp', pairs)]
    ppermute x12 -> x4, waiting for transfers between devices: 12 us -> 32.7 us  [along_dp(): return lax.ppermute(x, 'dp', pairs)]
    pallas_call x0 -> x9, Pallas kernels: none -> 17.2 us  [call(): pl.pallas_call(kernel, in_specs=[spec] * len(operands), out_specs=[spec]...]
    ppermute x18 -> x15, waiting for transfers between devices: 51.6 us -> 35.1 us  [swap(): return lax.ppermute(x, 'tensor', [(i, i ^ mask) for i in range(count)])]
    add x2 -> x5, other arithmetic: 1.4 us -> 5.29 us  [the longest x1 1.99 us: on_device(): own = own + (ends.astype(F32) - passed) + inner.astype(F32)]
    convert_element_type x13 -> x2, other arithmetic: 5.51 us -> 2.54 us  [the longest x1 1.4 us: on_device(): message = (own1 + other1.astype(F32)).astype(BF16)]
    unnamed x23 -> x38, local copies, waits for them, and re-layouts: 11 us -> 8.52 us
  transfers between devices with their start and end apart: 30 -> 19, of which waited for: 11 -> 10; matrix products, arithmetic and copies ran while one was open for 26% -> 5% of each run, Pallas kernels for 0% -> 9%
where the time goes in v2:
time: 127 us
  waiting for transfers between devices  67.8 us (53%)
  starting transfers between devices  24.6 us (19%)
  Pallas kernels  17.2 us (14%)
  local copies, waits for them, and re-layouts  8.52 us (7%)
  other arithmetic  7.84 us (6%)
    ppermute x15, waiting for transfers between devices, swap(): return lax.ppermute(x, 'tensor', [(i, i ^ mask) for i in range(count)])  35.1 us
    ppermute x4, waiting for transfers between devices, along_dp(): return lax.ppermute(x, 'dp', pairs)  32.7 us
    pallas_call x9, Pallas kernels, call(): pl.pallas_call(kernel, in_specs=[spec] * len(operands), out_specs=[spec]...  17.2 us
    ppermute x15, starting transfers between devices, swap(): return lax.ppermute(x, 'tensor', [(i, i ^ mask) for i in range(count)])  16.1 us
    ppermute x4, starting transfers between devices, along_dp(): return lax.ppermute(x, 'dp', pairs)  8.54 us
    unnamed x38, local copies, waits for them, and re-layouts  8.52 us
  transfers between devices with their start and end apart: 19, of which 10 were waited for; matrix products, arithmetic and copies ran while one was open for 5% of the time, Pallas kernels for 9%

profile of v2, /device:TPU:0, one launch (start us, length us, event | category | flops | bytes accessed | tf_op | source)
XLA Modules:
  0.0 126.9 jit_solution(12104280265416413701)
XLA Ops:
  1.1 2.6 %collective-permute-start.3 = (bf16[128,3072]{1,0:T(8,128)(2,1)}, bf16[128,3072]{1,0:T(8,128)(2,1)S(1)}, u32[]{:S(2)}, u32[]{:S(2)}) collective-permute-start(bf16[128,3072]{1,0:T(8,128)(2,1)} %bitcast.5), channel_id=1, source_target_pairs={{0,8},{4,12},{8,0},{12,4},{16,24},{20,28},{24,16},{28,20},{1,9},{5... | collective-permute-start | bytes 2359304 | tf_op jit(solution)/shard_map/ppermute | solution.py:19
  3.7 1.5 %collective-permute-start.4 = (bf16[128,3072]{1,0:T(8,128)(2,1)}, bf16[128,3072]{1,0:T(8,128)(2,1)S(1)}, u32[]{:S(2)}, u32[]{:S(2)}) collective-permute-start(bf16[128,3072]{1,0:T(8,128)(2,1)} %bitcast.6), channel_id=1, source_target_pairs={{0,16},{4,20},{8,24},{12,28},{16,0},{20,4},{24,8},{28,12},{1,17},{... | collective-permute-start | bytes 2359304 | tf_op jit(solution)/shard_map/ppermute | solution.py:19
  5.2 1.2 copy-done.4
  6.5 1.2 copy-done.14
  7.9 1.6 %collective-permute-start.1 = (bf16[128,1024]{1,0:T(8,128)(2,1)S(1)}, bf16[128,1024]{1,0:T(8,128)(2,1)S(1)}, u32[]{:S(2)}, u32[]{:S(2)}) collective-permute-start(bf16[128,1024]{1,0:T(8,128)(2,1)S(1)} %get-tuple-element.77), channel_id=1, source_target_pairs={{0,8},{4,12},{8,0},{12,4},{16,24},{20,28},{24,16},{28,20},{1,9},{5... | collective-permute-start | bytes 786440 | tf_op jit(solution)/shard_map/ppermute | solution.py:19
  9.5 1.5 %collective-permute-start.2 = (bf16[128,1024]{1,0:T(8,128)(2,1)S(1)}, bf16[128,1024]{1,0:T(8,128)(2,1)S(1)}, u32[]{:S(2)}, u32[]{:S(2)}) collective-permute-start(bf16[128,1024]{1,0:T(8,128)(2,1)S(1)} %get-tuple-element.78), channel_id=1, source_target_pairs={{0,16},{4,20},{8,24},{12,28},{16,0},{20,4},{24,8},{28,12},{1,17},{... | collective-permute-start | bytes 786440 | tf_op jit(solution)/shard_map/ppermute | solution.py:19
  11.0 11.3 %collective-permute-done.3.refs_0_.refs_1_ = bf16[128,3072]{1,0:T(8,128)(2,1)S(1)} collective-permute-done((bf16[128,3072]{1,0:T(8,128)(2,1)}, bf16[128,3072]{1,0:T(8,128)(2,1)S(1)}, u32[]{:S(2)}, u32[]{:S(2)}) %collective-permute-start.3) | collective-permute-done | bytes 786464 | tf_op jit(solution)/shard_map/ppermute | solution.py:19
  22.3 2.0 %collective-permute-done.4.refs_1_.refs_2_ = bf16[128,3072]{1,0:T(8,128)(2,1)S(1)} collective-permute-done((bf16[128,3072]{1,0:T(8,128)(2,1)}, bf16[128,3072]{1,0:T(8,128)(2,1)S(1)}, u32[]{:S(2)}, u32[]{:S(2)}) %collective-permute-start.4) | collective-permute-done | bytes 786464 | tf_op jit(solution)/shard_map/ppermute | solution.py:19
  24.3 3.4 %collective-permute-done.1.refs_4_ = bf16[128,1024]{1,0:T(8,128)(2,1)S(1)} collective-permute-done((bf16[128,1024]{1,0:T(8,128)(2,1)S(1)}, bf16[128,1024]{1,0:T(8,128)(2,1)S(1)}, u32[]{:S(2)}, u32[]{:S(2)}) %collective-permute-start.1) | collective-permute-done | bytes 262176 | tf_op jit(solution)/shard_map/ppermute | solution.py:19
  27.7 1.5 %collective-permute-done.2.refs_5_ = bf16[128,1024]{1,0:T(8,128)(2,1)S(1)} collective-permute-done((bf16[128,1024]{1,0:T(8,128)(2,1)S(1)}, bf16[128,1024]{1,0:T(8,128)(2,1)S(1)}, u32[]{:S(2)}, u32[]{:S(2)}) %collective-permute-start.2) | collective-permute-done | bytes 262176 | tf_op jit(solution)/shard_map/ppermute | solution.py:19
  29.2 1.6 %collective-permute-start.5 = (bf16[64,3072]{1,0:T(8,128)(2,1)S(1)}, bf16[64,3072]{1,0:T(8,128)(2,1)S(1)}, u32[]{:S(2)}, u32[]{:S(2)}) collective-permute-start(bf16[64,3072]{1,0:T(8,128)(2,1)S(1)} %get-tuple-element.94), channel_id=1, source_target_pairs={{0,16},{4,20},{8,24},{12,28},{16,0},{20,4},{24,8},{28,12},{1,17},{... | collective-permute-start | bytes 1179656 | tf_op jit(solution)/shard_map/ppermute | solution.py:19
  31.3 1.4 %collective-permute-start.7 = (bf16[128,1024]{1,0:T(8,128)(2,1)S(1)}, bf16[128,1024]{1,0:T(8,128)(2,1)S(1)}, u32[]{:S(2)}, u32[]{:S(2)}) collective-permute-start(bf16[128,1024]{1,0:T(8,128)(2,1)S(1)} %get-tuple-element.104), channel_id=1, source_target_pairs={{0,24},{4,28},{8,16},{12,20},{16,8},{20,12},{24,0},{28,4},{1,25},{... | collective-permute-start | bytes 786440 | tf_op jit(solution)/shard_map/ppermute | solution.py:19
  33.9 2.7 %gate_terms.2 = (bf16[384,1024]{1,0:T(8,128)(2,1)S(1)}, bf16[384,1024]{1,0:T(8,128)(2,1)S(1)}) custom-call(bf16[128,3072]{1,0:T(8,128)(2,1)S(1)} %bitcast.7, bf16[128,3072]{1,0:T(8,128)(2,1)S(1)} %collective-permute-done.3.refs_0_.refs_1_, bf16[128,3072]{1,0:T(8,128)(2,1)S(1)} %collective-permute-done.4.refs_1_.refs_2_, ...), custom_call_target="tpu_custom_call" | custom-call | tf_op jit(solution)/shard_map/gate_terms/pallas_call | solution.py:32
  36.6 3.9 %returns.2 = (f32[128,3072]{1,0:T(8,128)S(1)}, bf16[128,4096]{1,0:T(8,128)(2,1)}, bf16[128,4096]{1,0:T(8,128)(2,1)}) custom-call(bf16[384,1024]{1,0:T(8,128)(2,1)S(1)} %get-tuple-element.107.gp_ref.refs_5_, bf16[384,1024]{1,0:T(8,128)(2,1)S(1)} %get-tuple-element.92.gate_ref.refs_2_, bf16[3072,512]{1,0:T(8,128)(2,1)S(1)} %copy-done, ...), custom_call_target="tpu_custom_call" | custom-call | tf_op jit(solution)/shard_map/returns/pallas_call | solution.py:32
  40.6 2.3 %collective-permute-done.6.refs_1_.refs_4_ = bf16[64,3072]{1,0:T(8,128)(2,1)S(1)} collective-permute-done((bf16[64,3072]{1,0:T(8,128)(2,1)S(1)}, bf16[64,3072]{1,0:T(8,128)(2,1)S(1)}, u32[]{:S(2)}, u32[]{:S(2)}) %collective-permute-start.6) | collective-permute-done | bytes 393248 | tf_op jit(solution)/shard_map/ppermute | solution.py:19
  42.8 3.6 %collective-permute-done.7.refs_2_ = bf16[128,1024]{1,0:T(8,128)(2,1)S(1)} collective-permute-done((bf16[128,1024]{1,0:T(8,128)(2,1)S(1)}, bf16[128,1024]{1,0:T(8,128)(2,1)S(1)}, u32[]{:S(2)}, u32[]{:S(2)}) %collective-permute-start.7) | collective-permute-done | bytes 262176 | tf_op jit(solution)/shard_map/ppermute | solution.py:19
  48.6 2.8 %weight_shares.3 = (f32[768,512]{1,0:T(8,128)S(1)}, bf16[768,512]{1,0:T(8,128)(2,1)S(1)}, f32[768,512]{1,0:T(8,128)S(1)}, bf16[768,512]{1,0:T(8,128)(2,1)}, f32[...) custom-call(bf16[128,3072]{1,0:T(8,128)(2,1)S(1)} %bitcast.9, ...), custom_call_target="tpu_custom_call" | custom-call | tf_op jit(solution)/shard_map/weight_shares/pallas_call | solution.py:32
  51.9 1.4 %add_convert_fusion.1 = bf16[768,512]{1,0:T(8,128)(2,1)} fusion(f32[768,512]{1,0:T(8,128)S(1)} %get-tuple-element.110, bf16[768,512]{1,0:T(8,128)(2,1)S(1)} %collective-permute-done.8), kind=kLoop, calls=%fused_computation.10 | loop fusion | flops 1179648 | bytes 3145728 | tf_op jit(solution)/shard_map/convert_element_type | solution.py:240
  54.5 1.5 %collective-permute-start.15 = (bf16[128,4096]{1,0:T(8,128)(2,1)}, bf16[128,4096]{1,0:T(8,128)(2,1)}, u32[]{:S(2)}, u32[]{:S(2)}) collective-permute-start(bf16[128,4096]{1,0:T(8,128)(2,1)} %get-tuple-element.126), channel_id=1, source_target_pairs={{0,16},{4,20},{8,24},{12,28},{16,0},{20,4},{24,8},{28,12},{1,17},{... | collective-permute-start | bytes 3145736 | tf_op jit(solution)/shard_map/ppermute | solution.py:19
  56.0 1.6 %collective-permute-start.12 = (bf16[768,512]{1,0:T(8,128)(2,1)}, bf16[768,512]{1,0:T(8,128)(2,1)}, u32[]{:S(2)}, u32[]{:S(2)}) collective-permute-start(bf16[768,512]{1,0:T(8,128)(2,1)} %add_convert_fusion.1), channel_id=1, source_target_pairs={{0,1},{1,0},{2,3},{3,2},{4,5},{5,4},{6,7},{7,6},{8,9},{9,8},{10,11... | collective-permute-start | bytes 2359304 | tf_op jit(solution)/shard_map/ppermute | solution.py:23
  59.6 1.5 %collective-permute-start.13 = (bf16[768,512]{1,0:T(8,128)(2,1)}, bf16[768,512]{1,0:T(8,128)(2,1)}, u32[]{:S(2)}, u32[]{:S(2)}) collective-permute-start(bf16[768,512]{1,0:T(8,128)(2,1)} %add_convert_fusion), channel_id=1, source_target_pairs={{1,2},{2,1},{5,6},{6,5},{9,10},{10,9},{13,14},{14,13},{17,18},{18,... | collective-permute-start | bytes 2359304 | tf_op jit(solution)/shard_map/ppermute | solution.py:23
  61.1 1.9 %copy-done.2 = bf16[3072,512]{1,0:T(8,128)(2,1)S(1)} copy-done((bf16[3072,512]{1,0:T(8,128)(2,1)S(1)}, bf16[3072,512]{1,0:T(8,128)(2,1)}, u32[]{:S(2)}) %copy-start.2) | copy-done | bytes 3145752
  64.0 2.1 %returns.3 = bf16[128,4096]{1,0:T(8,128)(2,1)S(1)} custom-call(bf16[128,1024]{1,0:T(8,128)(2,1)S(1)} %get-tuple-element.108.refs_6_.gp_ref, bf16[128,1024]{1,0:T(8,128)(2,1)S(1)} %copy-done.16, bf16[3072,512]{1,0:T(8,128)(2,1)S(1)} %copy-done, bf16[3072,512]{1,0:T(8,128)(2,1)S(1)} %copy-done.2), custom_call_target="tpu_custom_call" | custom-call | tf_op jit(solution)/shard_map/returns/pallas_call | solution.py:32
  67.5 1.4 %convert_add_fusion.3 = f32[768,512]{1,0:T(8,128)S(1)} fusion(f32[768,512]{1,0:T(8,128)S(1)} %copy-done.11, bf16[768,512]{1,0:T(8,128)(2,1)} %collective-permute-done.9), kind=kLoop, calls=%fused_computation.9 | loop fusion | flops 786432 | bytes 3932160 | tf_op jit(solution)/shard_map/add | solution.py:249
  69.0 10.7 %collective-permute-done.14.refs_3_ = bf16[128,4096]{1,0:T(8,128)(2,1)} collective-permute-done((bf16[128,4096]{1,0:T(8,128)(2,1)}, bf16[128,4096]{1,0:T(8,128)(2,1)}, u32[]{:S(2)}, u32[]{:S(2)}) %collective-permute-start.14) | collective-permute-done | bytes 1048608 | tf_op jit(solution)/shard_map/ppermute | solution.py:19
  80.0 2.0 %fusion.2 = (f32[768,512]{1,0:T(8,128)S(1)}, bf16[768,512]{1,0:T(8,128)(2,1)S(1)}) fusion(f32[768,512]{1,0:T(8,128)S(1)} %convert_add_fusion.2, bf16[768,512]{1,0:T(8,128)(2,1)} %collective-permute-done.12, bf16[768,512]{1,0:T(8,128)(2,1)} %collective-permute-done.13, pred[]{:T(512)S(6)} %or.3, f32[768,512]{1,0:T(8,128)S(1)} %convert_add_fusion.3), kind=kLoop, calls=%fused_computation.4 | loop fusion | flops 3145728 | bytes 7077889 | tf_op jit(solution)/shard_map/add | solution.py:258
  82.0 5.4 %collective-permute-start.17 = (bf16[768,512]{1,0:T(8,128)(2,1)}, bf16[768,512]{1,0:T(8,128)(2,1)S(1)}, u32[]{:S(2)}, u32[]{:S(2)}) collective-permute-start(bf16[768,512]{1,0:T(8,128)(2,1)} %add_convert_fusion), channel_id=1, source_target_pairs={{0,2},{3,1},{4,6},{7,5},{8,10},{11,9},{12,14},{15,13},{16,18},{19,... | collective-permute-start | bytes 2359304 | tf_op jit(solution)/shard_map/ppermute | solution.py:23
  87.5 1.6 %collective-permute-start.16 = (bf16[128,4096]{1,0:T(8,128)(2,1)S(1)}, bf16[128,4096]{1,0:T(8,128)(2,1)S(1)}, u32[]{:S(2)}, u32[]{:S(2)}) collective-permute-start(bf16[128,4096]{1,0:T(8,128)(2,1)S(1)} %returns.3), channel_id=1, source_target_pairs={{0,24},{4,28},{8,16},{12,20},{16,8},{20,12},{24,0},{28,4},{1,25},{... | collective-permute-start | bytes 3145736 | tf_op jit(solution)/shard_map/ppermute | solution.py:19
  89.1 16.6 %collective-permute-done.17 = bf16[768,512]{1,0:T(8,128)(2,1)S(1)} collective-permute-done((bf16[768,512]{1,0:T(8,128)(2,1)}, bf16[768,512]{1,0:T(8,128)(2,1)S(1)}, u32[]{:S(2)}, u32[]{:S(2)}) %collective-permute-start.17) | collective-permute-done | bytes 786464 | tf_op jit(solution)/shard_map/ppermute | solution.py:23
  105.9 16.1 %collective-permute-done.18 = bf16[768,512]{1,0:T(8,128)(2,1)S(1)} collective-permute-done((bf16[768,512]{1,0:T(8,128)(2,1)S(1)}, bf16[768,512]{1,0:T(8,128)(2,1)S(1)}, u32[]{:S(2)}, u32[]{:S(2)}) %collective-permute-start.18) | collective-permute-done | bytes 786464 | tf_op jit(solution)/shard_map/ppermute | solution.py:23
  122.1 1.4 %convert_add_fusion = f32[768,512]{1,0:T(8,128)} fusion(f32[768,512]{1,0:T(8,128)S(1)} %convert_add_fusion.1, bf16[768,512]{1,0:T(8,128)(2,1)S(1)} %collective-permute-done.18), kind=kLoop, calls=%fused_computation.5 | loop fusion | flops 786432 | bytes 3932160 | tf_op jit(solution)/shard_map/add | solution.py:269
  123.5 3.4 %finish.1 = (bf16[128,3072]{1,0:T(8,128)(2,1)}, bf16[128,4096]{1,0:T(8,128)(2,1)}) custom-call(bf16[128,4096]{1,0:T(8,128)(2,1)S(1)} %bitcast.11, f32[128,3072]{1,0:T(8,128)S(1)} %copy-done.9, bf16[384,1024]{1,0:T(8,128)(2,1)S(1)} %copy-done.7, bf16[128,4096]{1,0:T(8,128)(2,1)} %collective-permute-done.14.refs_3_, ...), custom_call_target="tpu_custom_call" | custom-call | tf_op jit(solution)/shard_map/finish/pallas_call | solution.py:32
  (60 shorter events, 11.4 us)
Async XLA Ops:
  0.6 7.3 %collective-permute-start = (bf16[3072,512]{1,0:T(8,128)(2,1)}, bf16[3072,512]{1,0:T(8,128)(2,1)S(1)}, u32[]{:S(2)}, u32[]{:S(2)}) collective-permute-start(bf16[3072,512]{1,0:T(8,128)(2,1)} %w_ref.3), channel_id=1, source_target_pairs={{0,4},{4,0},{8,12},{12,8},{16,20},{20,16},{24,28},{28,24},{1,5},{5... | collective-permute-start | bytes 9437192 | tf_op jit(solution)/shard_map/ppermute | solution.py:19
  1.1 21.2 %collective-permute-start.3 = (bf16[128,3072]{1,0:T(8,128)(2,1)}, bf16[128,3072]{1,0:T(8,128)(2,1)S(1)}, u32[]{:S(2)}, u32[]{:S(2)}) collective-permute-start(bf16[128,3072]{1,0:T(8,128)(2,1)} %bitcast.5), channel_id=1, source_target_pairs={{0,8},{4,12},{8,0},{12,4},{16,24},{20,28},{24,16},{28,20},{1,9},{5... | collective-permute-start | bytes 2359304 | tf_op jit(solution)/shard_map/ppermute | solution.py:19
  3.7 20.6 %collective-permute-start.4 = (bf16[128,3072]{1,0:T(8,128)(2,1)}, bf16[128,3072]{1,0:T(8,128)(2,1)S(1)}, u32[]{:S(2)}, u32[]{:S(2)}) collective-permute-start(bf16[128,3072]{1,0:T(8,128)(2,1)} %bitcast.6), channel_id=1, source_target_pairs={{0,16},{4,20},{8,24},{12,28},{16,0},{20,4},{24,8},{28,12},{1,17},{... | collective-permute-start | bytes 2359304 | tf_op jit(solution)/shard_map/ppermute | solution.py:19
  7.7 25.1 %copy-start = (bf16[3072,512]{1,0:T(8,128)(2,1)S(1)}, bf16[3072,512]{1,0:T(8,128)(2,1)}, u32[]{:S(2)}) copy-start(bf16[3072,512]{1,0:T(8,128)(2,1)} %w_ref.3) | copy-start | bytes 9437188
  7.9 38.5 %copy-start.1 = (bf16[3072,512]{1,0:T(8,128)(2,1)}, bf16[3072,512]{1,0:T(8,128)(2,1)S(1)}, u32[]{:S(2)}) copy-start(bf16[3072,512]{1,0:T(8,128)(2,1)S(1)} %collective-permute-done.refs_7_.w_other_ref.refs_4_) | copy-start | bytes 9437188
  7.9 19.7 %collective-permute-start.1 = (bf16[128,1024]{1,0:T(8,128)(2,1)S(1)}, bf16[128,1024]{1,0:T(8,128)(2,1)S(1)}, u32[]{:S(2)}, u32[]{:S(2)}) collective-permute-start(bf16[128,1024]{1,0:T(8,128)(2,1)S(1)} %get-tuple-element.77), channel_id=1, source_target_pairs={{0,8},{4,12},{8,0},{12,4},{16,24},{20,28},{24,16},{28,20},{1,9},{5... | collective-permute-start | bytes 786440 | tf_op jit(solution)/shard_map/ppermute | solution.py:19
  9.5 19.6 %collective-permute-start.2 = (bf16[128,1024]{1,0:T(8,128)(2,1)S(1)}, bf16[128,1024]{1,0:T(8,128)(2,1)S(1)}, u32[]{:S(2)}, u32[]{:S(2)}) collective-permute-start(bf16[128,1024]{1,0:T(8,128)(2,1)S(1)} %get-tuple-element.78), channel_id=1, source_target_pairs={{0,16},{4,20},{8,24},{12,28},{16,0},{20,4},{24,8},{28,12},{1,17},{... | collective-permute-start | bytes 786440 | tf_op jit(solution)/shard_map/ppermute | solution.py:19
  29.2 11.3 %collective-permute-start.5 = (bf16[64,3072]{1,0:T(8,128)(2,1)S(1)}, bf16[64,3072]{1,0:T(8,128)(2,1)S(1)}, u32[]{:S(2)}, u32[]{:S(2)}) collective-permute-start(bf16[64,3072]{1,0:T(8,128)(2,1)S(1)} %get-tuple-element.94), channel_id=1, source_target_pairs={{0,16},{4,20},{8,24},{12,28},{16,0},{20,4},{24,8},{28,12},{1,17},{... | collective-permute-start | bytes 1179656 | tf_op jit(solution)/shard_map/ppermute | solution.py:19
  30.8 12.1 %collective-permute-start.6 = (bf16[64,3072]{1,0:T(8,128)(2,1)S(1)}, bf16[64,3072]{1,0:T(8,128)(2,1)S(1)}, u32[]{:S(2)}, u32[]{:S(2)}) collective-permute-start(bf16[64,3072]{1,0:T(8,128)(2,1)S(1)} %get-tuple-element.95), channel_id=1, source_target_pairs={{0,8},{4,12},{8,0},{12,4},{16,24},{20,28},{24,16},{28,20},{1,9},{5... | collective-permute-start | bytes 1179656 | tf_op jit(solution)/shard_map/ppermute | solution.py:19
  31.3 15.1 %collective-permute-start.7 = (bf16[128,1024]{1,0:T(8,128)(2,1)S(1)}, bf16[128,1024]{1,0:T(8,128)(2,1)S(1)}, u32[]{:S(2)}, u32[]{:S(2)}) collective-permute-start(bf16[128,1024]{1,0:T(8,128)(2,1)S(1)} %get-tuple-element.104), channel_id=1, source_target_pairs={{0,24},{4,28},{8,16},{12,20},{16,8},{20,12},{24,0},{28,4},{1,25},{... | collective-permute-start | bytes 786440 | tf_op jit(solution)/shard_map/ppermute | solution.py:19
  36.6 3.9 %copy-start.6 = (bf16[384,1024]{1,0:T(8,128)(2,1)}, bf16[384,1024]{1,0:T(8,128)(2,1)S(1)}, u32[]{:S(2)}) copy-start(bf16[384,1024]{1,0:T(8,128)(2,1)S(1)} %get-tuple-element.92.gate_ref.refs_2_) | copy-start | bytes 2359300
  40.6 6.9 %copy-start.8 = (f32[128,3072]{1,0:T(8,128)}, f32[128,3072]{1,0:T(8,128)S(1)}, u32[]{:S(2)}) copy-start(f32[128,3072]{1,0:T(8,128)S(1)} %get-tuple-element.93.refs_1_) | copy-start | bytes 4718596
  48.5 2.9 %collective-permute-start.8 = (bf16[768,512]{1,0:T(8,128)(2,1)S(1)}, bf16[768,512]{1,0:T(8,128)(2,1)S(1)}, u32[]{:S(2)}, u32[]{:S(2)}) collective-permute-start(bf16[768,512]{1,0:T(8,128)(2,1)S(1)} %get-tuple-element.111), channel_id=1, source_target_pairs={{0,4},{4,0},{8,12},{12,8},{16,20},{20,16},{24,28},{28,24},{1,5},{5... | collective-permute-start | bytes 2359304 | tf_op jit(solution)/shard_map/ppermute | solution.py:19
  51.4 1.9 %copy-start.10 = (f32[768,512]{1,0:T(8,128)}, f32[768,512]{1,0:T(8,128)S(1)}, u32[]{:S(2)}) copy-start(f32[768,512]{1,0:T(8,128)S(1)} %get-tuple-element.109) | copy-start | bytes 4718596
  51.4 1.9 %copy-start.12 = (f32[768,512]{1,0:T(8,128)}, f32[768,512]{1,0:T(8,128)S(1)}, u32[]{:S(2)}) copy-start(f32[768,512]{1,0:T(8,128)S(1)} %get-tuple-element.119) | copy-start | bytes 4718596
  51.4 4.6 %collective-permute-start.11 = (bf16[768,512]{1,0:T(8,128)(2,1)S(1)}, bf16[768,512]{1,0:T(8,128)(2,1)S(1)}, u32[]{:S(2)}, u32[]{:S(2)}) collective-permute-start(bf16[768,512]{1,0:T(8,128)(2,1)S(1)} %get-tuple-element.122), channel_id=1, source_target_pairs={{0,4},{4,0},{8,12},{12,8},{16,20},{20,16},{24,28},{28,24},{1,5},{5... | collective-permute-start | bytes 2359304 | tf_op jit(solution)/shard_map/ppermute | solution.py:19
  53.3 5.4 %collective-permute-start.10 = (bf16[768,512]{1,0:T(8,128)(2,1)S(1)}, bf16[768,512]{1,0:T(8,128)(2,1)S(1)}, u32[]{:S(2)}, u32[]{:S(2)}) collective-permute-start(bf16[768,512]{1,0:T(8,128)(2,1)S(1)} %get-tuple-element.120), channel_id=1, source_target_pairs={{0,4},{4,0},{8,12},{12,8},{16,20},{20,16},{24,28},{28,24},{1,5},{5... | collective-permute-start | bytes 2359304 | tf_op jit(solution)/shard_map/ppermute | solution.py:19
  53.8 12.6 %collective-permute-start.9 = (bf16[768,512]{1,0:T(8,128)(2,1)}, bf16[768,512]{1,0:T(8,128)(2,1)}, u32[]{:S(2)}, u32[]{:S(2)}) collective-permute-start(bf16[768,512]{1,0:T(8,128)(2,1)} %get-tuple-element.118), channel_id=1, source_target_pairs={{0,4},{4,0},{8,12},{12,8},{16,20},{20,16},{24,28},{28,24},{1,5},{5... | collective-permute-start | bytes 2359304 | tf_op jit(solution)/shard_map/ppermute | solution.py:19
  53.8 25.8 %collective-permute-start.14 = (bf16[128,4096]{1,0:T(8,128)(2,1)}, bf16[128,4096]{1,0:T(8,128)(2,1)}, u32[]{:S(2)}, u32[]{:S(2)}) collective-permute-start(bf16[128,4096]{1,0:T(8,128)(2,1)} %get-tuple-element.125), channel_id=1, source_target_pairs={{0,8},{4,12},{8,0},{12,4},{16,24},{20,28},{24,16},{28,20},{1,9},{5... | collective-permute-start | bytes 3145736 | tf_op jit(solution)/shard_map/ppermute | solution.py:19
  54.5 25.6 %collective-permute-start.15 = (bf16[128,4096]{1,0:T(8,128)(2,1)}, bf16[128,4096]{1,0:T(8,128)(2,1)}, u32[]{:S(2)}, u32[]{:S(2)}) collective-permute-start(bf16[128,4096]{1,0:T(8,128)(2,1)} %get-tuple-element.126), channel_id=1, source_target_pairs={{0,16},{4,20},{8,24},{12,28},{16,0},{20,4},{24,8},{28,12},{1,17},{... | collective-permute-start | bytes 3145736 | tf_op jit(solution)/shard_map/ppermute | solution.py:19
  56.0 24.1 %collective-permute-start.12 = (bf16[768,512]{1,0:T(8,128)(2,1)}, bf16[768,512]{1,0:T(8,128)(2,1)}, u32[]{:S(2)}, u32[]{:S(2)}) collective-permute-start(bf16[768,512]{1,0:T(8,128)(2,1)} %add_convert_fusion.1), channel_id=1, source_target_pairs={{0,1},{1,0},{2,3},{3,2},{4,5},{5,4},{6,7},{7,6},{8,9},{9,8},{10,11... | collective-permute-start | bytes 2359304 | tf_op jit(solution)/shard_map/ppermute | solution.py:23
  59.6 20.4 %collective-permute-start.13 = (bf16[768,512]{1,0:T(8,128)(2,1)}, bf16[768,512]{1,0:T(8,128)(2,1)}, u32[]{:S(2)}, u32[]{:S(2)}) collective-permute-start(bf16[768,512]{1,0:T(8,128)(2,1)} %add_convert_fusion), channel_id=1, source_target_pairs={{1,2},{2,1},{5,6},{6,5},{9,10},{10,9},{13,14},{14,13},{17,18},{18,... | collective-permute-start | bytes 2359304 | tf_op jit(solution)/shard_map/ppermute | solution.py:23
  61.1 1.9 %copy-start.2 = (bf16[3072,512]{1,0:T(8,128)(2,1)S(1)}, bf16[3072,512]{1,0:T(8,128)(2,1)}, u32[]{:S(2)}) copy-start(bf16[3072,512]{1,0:T(8,128)(2,1)} %copy-done.1) | copy-start | bytes 9437188
  64.0 2.1 %copy-start.13 = (f32[768,512]{1,0:T(8,128)S(1)}, f32[768,512]{1,0:T(8,128)}, u32[]{:S(2)}) copy-start(f32[768,512]{1,0:T(8,128)} %copy-done.12) | copy-start | bytes 4718596
  64.0 2.2 %copy-start.18 = (bf16[768,512]{1,0:T(8,128)(2,1)S(1)}, bf16[768,512]{1,0:T(8,128)(2,1)}, u32[]{:S(2)}) copy-start(bf16[768,512]{1,0:T(8,128)(2,1)} %copy-done.17) | copy-start | bytes 2359300
  66.1 1.4 %copy-start.11 = (f32[768,512]{1,0:T(8,128)S(1)}, f32[768,512]{1,0:T(8,128)}, u32[]{:S(2)}) copy-start(f32[768,512]{1,0:T(8,128)} %copy-done.10) | copy-start | bytes 4718596
  82.0 23.6 %collective-permute-start.17 = (bf16[768,512]{1,0:T(8,128)(2,1)}, bf16[768,512]{1,0:T(8,128)(2,1)S(1)}, u32[]{:S(2)}, u32[]{:S(2)}) collective-permute-start(bf16[768,512]{1,0:T(8,128)(2,1)} %add_convert_fusion), channel_id=1, source_target_pairs={{0,2},{3,1},{4,6},{7,5},{8,10},{11,9},{12,14},{15,13},{16,18},{19,... | collective-permute-start | bytes 2359304 | tf_op jit(solution)/shard_map/ppermute | solution.py:23
  87.4 34.6 %collective-permute-start.18 = (bf16[768,512]{1,0:T(8,128)(2,1)S(1)}, bf16[768,512]{1,0:T(8,128)(2,1)S(1)}, u32[]{:S(2)}, u32[]{:S(2)}) collective-permute-start(bf16[768,512]{1,0:T(8,128)(2,1)S(1)} %get-tuple-element.140), channel_id=1, source_target_pairs={{0,1},{1,3},{2,0},{3,2},{4,5},{5,7},{6,4},{7,6},{8,9},{9,11},{10,8... | collective-permute-start | bytes 2359304 | tf_op jit(solution)/shard_map/ppermute | solution.py:23
  87.5 36.0 %collective-permute-start.16 = (bf16[128,4096]{1,0:T(8,128)(2,1)S(1)}, bf16[128,4096]{1,0:T(8,128)(2,1)S(1)}, u32[]{:S(2)}, u32[]{:S(2)}) collective-permute-start(bf16[128,4096]{1,0:T(8,128)(2,1)S(1)} %returns.3), channel_id=1, source_target_pairs={{0,24},{4,28},{8,16},{12,20},{16,8},{20,12},{24,0},{28,4},{1,25},{... | collective-permute-start | bytes 3145736 | tf_op jit(solution)/shard_map/ppermute | solution.py:19
  105.9 17.6 %copy-start.5 = (bf16[1,128,4096]{2,1,0:T(8,128)(2,1)S(1)}, bf16[1,128,4096]{2,1,0:T(8,128)(2,1)}, u32[]{:S(2)}) copy-start(bf16[1,128,4096]{2,1,0:T(8,128)(2,1)} %param.6) | copy-start | bytes 3145732
  105.9 17.6 %copy-start.7 = (bf16[384,1024]{1,0:T(8,128)(2,1)S(1)}, bf16[384,1024]{1,0:T(8,128)(2,1)}, u32[]{:S(2)}) copy-start(bf16[384,1024]{1,0:T(8,128)(2,1)} %copy-done.6) | copy-start | bytes 2359300
  105.9 17.6 %copy-start.9 = (f32[128,3072]{1,0:T(8,128)S(1)}, f32[128,3072]{1,0:T(8,128)}, u32[]{:S(2)}) copy-start(f32[128,3072]{1,0:T(8,128)} %copy-done.8) | copy-start | bytes 4718596
  (6 other events, 6.5 us)

commit v3 on v2

--- a/solution.py
+++ b/solution.py
@@ -105,7 +105,8 @@
 
 
 def share_kernel(tables, rows, xs, *refs):
-    x_refs, gp_refs, outs = refs[:xs], refs[xs : -2 * len(tables)], refs[-2 * len(tables) :]
+    outs = len(tables) + min(len(tables), 2)
+    x_refs, gp_refs, outs = refs[:xs], refs[xs:-outs], refs[-outs:]
     me = lax.axis_index("dp")
     gp = stack(gp_refs)
     width = outs[0].shape[1]
@@ -113,58 +114,114 @@
         cols = columns_at(pick(me, table), rows)
         x = jnp.concatenate([ref[:, cols] for ref in x_refs], 0)
         share = lax.dot_general(x, gp, ROWS, preferred_element_type=F32)
-        outs[2 * i][...] = share[:, :width]
-        outs[2 * i + 1][...] = share[:, width:].astype(BF16)
+        outs[i][...] = share[:, :width]
+        at = max(i - 1, 0) * rows
+        outs[len(tables) + min(i, 1)][at : at + rows] = share[:, width:].astype(BF16)
 
 
 def weight_shares(tables, xs, gps, count):
     width = gps[0].shape[1] // 2
     rows = xs[0].shape[1] // count
-    shapes = [((rows, width), F32), ((rows, width), BF16)] * len(tables)
+    shapes = [((rows, width), F32)] * len(tables) + [((rows, width), BF16)]
+    if len(tables) > 1:
+        shapes.append((((len(tables) - 1) * rows, width), BF16))
     return call(functools.partial(share_kernel, tables, rows, len(xs)), "weight_shares", shapes, *xs, *gps)
 
 
 def return_kernel(own, gp_ref, gate_ref, w_ref, w_other_ref, *outs):
     width = gp_ref.shape[1] // 2
-    tokens = outs[0].shape[0]
     depth = w_ref.shape[0]
     tile = min(depth, 1024)
     for at in range(0, depth, tile):
         rows = slice(at, at + tile)
         dx = lax.dot_general(gp_ref[:, :width], w_ref[rows], COLUMNS, preferred_element_type=F32)
         dx = dx + lax.dot_general(gp_ref[:, width:], w_other_ref[rows], COLUMNS, preferred_element_type=F32)
-        for m, out_ref in enumerate(outs):
-            out_ref[:, rows] = dx[m * tokens : (m + 1) * tokens].astype(out_ref.dtype)
-    for m in range(own, len(outs)):
-        outs[m][:, depth:] = gate_ref[m * tokens : (m + 1) * tokens]
-
-
-def returns_of(own, gp, gate, weight, w_other, tokens):
+        first = 0
+        for out_ref in outs:
+            last = first + out_ref.shape[0]
+            out_ref[:, rows] = dx[first:last].astype(out_ref.dtype)
+            first = last
+    first = 0
+    for i, out_ref in enumerate(outs):
+        last = first + out_ref.shape[0]
+        if i >= own:
+            out_ref[:, depth:] = gate_ref[first:last]
+        first = last
+
+
+def returns_of(own, gp, gate, weight, w_other, tokens, rows):
     depth, width = weight.shape
-    chips = gate.shape[0] // tokens
-    shapes = [((tokens, depth), F32)] * own + [((tokens, depth + 2 * width), BF16)] * (chips - own)
+    sent = gate.shape[0] - own * tokens
+    shapes = [((tokens, depth), F32)] * own + [((rows, depth + 2 * width), BF16)] * (sent // rows)
     return call(functools.partial(return_kernel, own), "returns", shapes, gp, gate, weight, w_other)
 
 
-def finish_kernel(chips, width, *refs):
+def finish_kernel(pieces, width, *refs):
     cot_ref, mine_ref, gate_ref = refs[:3]
-    back, (input_ref, attn_ref) = refs[3:-2], refs[-2:]
+    arrived, (input_ref, attn_ref) = refs[3:-2], refs[-2:]
     tokens, depth = mine_ref.shape
+    back = []
+    for count in pieces:
+        back.append(arrived[:count])
+        arrived = arrived[count:]
+
+    def read(refs, first, last):
+        return jnp.concatenate([ref[:, first:last] for ref in refs], 0).astype(F32)
+
     total = mine_ref[...]
-    for ref in back:
-        total = total + ref[:, :depth].astype(F32)
+    for group in back:
+        total = total + read(group, 0, depth)
     input_ref[...] = total.astype(BF16)
-    for m in range(chips):
+    for m in range(len(pieces) + 1):
         for which in range(2):
             at = which * width
-            gate = back[m - 1][:, depth + at : depth + at + width] if m else gate_ref[:tokens, at : at + width]
+            if m:
+                gate = read(back[m - 1], depth + at, depth + at + width)
+            else:
+                gate = gate_ref[:tokens, at : at + width].astype(F32)
             cols = chip_columns(m, which, width)
-            attn_ref[:, cols] = (cot_ref[:, cols].astype(F32) * gate.astype(F32)).astype(BF16)
+            attn_ref[:, cols] = (cot_ref[:, cols].astype(F32) * gate).astype(BF16)
 
 
 def finish(cot, mine, gate, back, width):
-    kernel = functools.partial(finish_kernel, len(back) + 1, width)
-    return call(kernel, "finish", [(mine.shape, BF16), (cot.shape, BF16)], cot, mine, gate, *back)
+    kernel = functools.partial(finish_kernel, [len(group) for group in back], width)
+    arrived = [piece for group in back for piece in group]
+    return call(kernel, "finish", [(mine.shape, BF16), (cot.shape, BF16)], cot, mine, gate, *arrived)
+
+
+def on_ends(ref, count):
+    me = lax.axis_index("dp")
+    is_end = (me == 0) | (me == count - 1)
+    return jnp.where(is_end, ref[...].astype(F32), 0.0)
+
+
+def add_kernel(own_ref, other_ref, out_ref):
+    out_ref[...] = (own_ref[...] + other_ref[...].astype(F32)).astype(BF16)
+
+
+def add(own, other):
+    return call(add_kernel, "add", [(own.shape, BF16)], own, other)[0]
+
+
+def pass_kernel(count, own_ref, other_ref, ends_ref, out_ref):
+    ends = ends_ref[...].astype(F32) - on_ends(ends_ref, count)
+    out_ref[...] = (own_ref[...] + other_ref[: own_ref.shape[0]].astype(F32) + ends).astype(BF16)
+
+
+def add_passed(own, other, ends, count):
+    return call(functools.partial(pass_kernel, count), "add_passed", [(own.shape, BF16)], own, other, ends)[0]
+
+
+def total_kernel(count, own_ref, other_ref, ends_ref, *refs):
+    total = own_ref[...] + other_ref[own_ref.shape[0] :].astype(F32) + on_ends(ends_ref, count)
+    for ref in refs[:-1]:
+        total = total + ref[...].astype(F32)
+    refs[-1][...] = total
+
+
+def total(own, other, ends, arrived, count):
+    kernel = functools.partial(total_kernel, count)
+    return call(kernel, "total", [(own.shape, F32)], own, other, ends, *arrived)[0]
 
 
 def sum_over_line(share_of, count):
@@ -218,7 +275,7 @@
 
     first = [0] + near
     gp_near, gate_near = terms_of(first)
-    mine, *returns = returns_of(1, gp_near, gate_near, gate_weight, w_other, tokens)
+    mine, *returns = returns_of(1, gp_near, gate_near, gate_weight, w_other, tokens, tokens)
     xs, gp_near, returns = tie(xs, gp_near, returns)
     gps = [gp_near]
     if far:
@@ -226,47 +283,29 @@
         gps.append(gp_far)
     x_list = [x for m in first + far for x in xs[m]]
 
-    back = {m: swap(piece, 2 * m) for m, piece in zip(near, returns)}
+    back = {m: [swap(piece, 2 * m)] for m, piece in zip(near, returns)}
     if count == 4:
-        rows = depth // count
         own1, other1 = weight_shares([[3, 0, 3, 0]], x_list, gps, count)
         other1, gps = tie(other1, gps)
         other1 = swap(other1, 1)
-        own2, other2, own3, other3, own4, other4 = weight_shares(
+        own2, own3, own4, other2, other34 = weight_shares(
             [[2, 2, 1, 1], [1, 3, 0, 2], [0, 1, 2, 3]], x_list, gps, count
         )
-        other1, other2, other3, other4 = tie(other1, other2, other3, other4)
-        other2 = swap(other2, 1)
-        message = (own1 + other1.astype(F32)).astype(BF16)
-        message, other3, other4 = tie(message, other3, other4)
+        other2, other34 = swap(other2, 1), swap(other34, 1)
+        message = add(own1, other1)
         ends = along_dp(message, [(0, 1), (1, 0), (2, 3), (3, 2)])
-        other3, other4 = swap(other3, 1), swap(other4, 1)
-        middle = (own2 + other2.astype(F32)).astype(BF16)
+        middle = add(own2, other2)
         inner = along_dp(middle, [(1, 2), (2, 1)])
+        ends, inner = tie(ends, inner)
+        over = along_dp(middle, [(0, 2), (3, 1)])
+        message = add_passed(own3, other34, ends, count)
+        last = along_dp(message, [(0, 1), (1, 3), (2, 0), (3, 2)])
+        message, back, gp_far = tie(message, back, gp_far)
     if far:
-        returns = returns_of(0, gp_far, gate_far, gate_weight, w_other, tokens)
+        returns = returns_of(0, gp_far, gate_far, gate_weight, w_other, tokens, tokens // 2)
+        back.update({m: [swap(piece, 2 * m) for piece in returns[2 * i : 2 * i + 2]] for i, m in enumerate(far)})
     if count == 4:
-        kept = own3 + other3.astype(F32)
-        own = own4 + other4.astype(F32)
-        kept, own, middle, ends, inner, returns, back = tie(
-            kept, own, middle, ends, inner, returns, back
-        )
-        me = lax.axis_index("dp")
-        is_end = (me == 0) | (me == count - 1)
-        passed = jnp.where(is_end, 0.0, ends.astype(F32))
-        message = (kept + passed).astype(BF16)
-        own = own + (ends.astype(F32) - passed) + inner.astype(F32)
-        message, own, middle, returns = tie(message, own, middle, returns)
-        last = along_dp(message, [(0, 1), (1, 3), (2, 0), (3, 2)])
-        over = along_dp(middle, [(0, 2), (3, 1)])
-    if far:
-        back.update({m: swap(piece, 2 * m) for m, piece in zip(far, returns)})
-    if count == 4:
-        own = own + over.astype(F32)
-    grad_input, grad_attn = finish(cot, mine, gate_near, [back[m] for m in range(1, chips)], width)
-    if count == 4:
-        own, last = tie(own, last)
-        grad_weight = own + last.astype(F32)
+        grad_weight = total(own4, other34, ends, [inner, over, last], count)
     else:
         x_all = jnp.concatenate(x_list, 0)
         gp_all = jnp.concatenate(gps, 0)
@@ -277,6 +316,8 @@
             return share[:, :width] + swap(share[:, width:].astype(BF16), 1).astype(F32)
 
         grad_weight = sum_over_line(share_of, count)
+    grad_weight, back, cot = tie(grad_weight, back, cot)
+    grad_input, grad_attn = finish(cot, mine, gate_near, [back[m] for m in range(1, chips)], width)
     return (grad_input[None], grad_attn[None], grad_weight)
 
 

time: 127 us -> 116 us (0.913)
  other arithmetic: 7.84 us -> 0 us
  local copies, waits for them, and re-layouts: 8.52 us -> 3.59 us
  waiting for transfers between devices: 67.8 us -> 69.6 us
    ppermute x4, waiting for transfers between devices: 32.7 us -> 40.6 us  [along_dp(): return lax.ppermute(x, 'dp', pairs)]
    ppermute x15, waiting for transfers between devices: 35.1 us -> 29 us  [swap(): return lax.ppermute(x, 'tensor', [(i, i ^ mask) for i in range(count)])]
    add x5 -> x0, other arithmetic: 5.29 us -> none  [the longest x1 1.99 us: on_device(): own = own + (ends.astype(F32) - passed) + inner.astype(F32)]
    unnamed x38 -> x10, local copies, waits for them, and re-layouts: 8.52 us -> 3.59 us
    convert_element_type x2 -> x0, other arithmetic: 2.54 us -> none  [the longest x1 1.4 us: on_device(): message = (own1 + other1.astype(F32)).astype(BF16)]
    pallas_call x9 -> x13, Pallas kernels: 17.2 us -> 16.6 us  [call(): pl.pallas_call(kernel, in_specs=[spec] * len(operands), out_specs=[spec]...]
  transfers between devices with their start and end apart: 19 -> 19, of which waited for: 10 -> 12; matrix products, arithmetic and copies ran while one was open for 5% -> 0% of each run, Pallas kernels for 9% -> 11%
where the time goes in v3:
time: 116 us; the launch traced here: 115 us
  waiting for transfers between devices  69.6 us (60%)
  starting transfers between devices  24.8 us (21%)
  Pallas kernels  16.6 us (14%)
  local copies, waits for them, and re-layouts  3.59 us (3%)
    ppermute x4, waiting for transfers between devices, along_dp(): return lax.ppermute(x, 'dp', pairs)  40.6 us
    ppermute x15, waiting for transfers between devices, swap(): return lax.ppermute(x, 'tensor', [(i, i ^ mask) for i in range(count)])  29 us
    ppermute x15, starting transfers between devices, swap(): return lax.ppermute(x, 'tensor', [(i, i ^ mask) for i in range(count)])  17.1 us
    pallas_call x13, Pallas kernels, call(): pl.pallas_call(kernel, in_specs=[spec] * len(operands), out_specs=[spec]...  16.6 us
    ppermute x4, starting transfers between devices, along_dp(): return lax.ppermute(x, 'dp', pairs)  7.68 us
    unnamed x10, local copies, waits for them, and re-layouts  3.59 us
  transfers between devices with their start and end apart: 19, of which 12 were waited for; matrix products, arithmetic and copies ran while one was open for 0% of the time, Pallas kernels for 11%

profile of v3, /device:TPU:0, one launch (start us, length us, event | category | flops | bytes accessed | tf_op | source)
XLA Modules:
  0.0 115.3 jit_solution(18130402153042629498)
XLA Ops:
  1.1 2.6 %collective-permute-start.4 = (bf16[128,3072]{1,0:T(8,128)(2,1)}, bf16[128,3072]{1,0:T(8,128)(2,1)S(1)}, u32[]{:S(2)}, u32[]{:S(2)}) collective-permute-start(bf16[128,3072]{1,0:T(8,128)(2,1)} %bitcast.5), channel_id=1, source_target_pairs={{0,16},{4,20},{8,24},{12,28},{16,0},{20,4},{24,8},{28,12},{1,17},{... | collective-permute-start | bytes 2359304 | tf_op jit(solution)/shard_map/ppermute | solution.py:19
  3.7 1.5 %collective-permute-start.3 = (bf16[128,3072]{1,0:T(8,128)(2,1)}, bf16[128,3072]{1,0:T(8,128)(2,1)S(1)}, u32[]{:S(2)}, u32[]{:S(2)}) collective-permute-start(bf16[128,3072]{1,0:T(8,128)(2,1)} %bitcast.6), channel_id=1, source_target_pairs={{0,8},{4,12},{8,0},{12,4},{16,24},{20,28},{24,16},{28,20},{1,9},{5... | collective-permute-start | bytes 2359304 | tf_op jit(solution)/shard_map/ppermute | solution.py:19
  5.2 1.2 %copy-done.2 = bf16[1,128,4096]{2,1,0:T(8,128)(2,1)S(1)} copy-done((bf16[1,128,4096]{2,1,0:T(8,128)(2,1)S(1)}, bf16[1,128,4096]{2,1,0:T(8,128)(2,1)}, u32[]{:S(2)}) %copy-start.2) | copy-done | bytes 1048600
  6.5 1.2 %copy-done.4 = bf16[1,128,4096]{2,1,0:T(8,128)(2,1)S(1)} copy-done((bf16[1,128,4096]{2,1,0:T(8,128)(2,1)S(1)}, bf16[1,128,4096]{2,1,0:T(8,128)(2,1)}, u32[]{:S(2)}) %copy-start.4) | copy-done | bytes 1048600
  7.9 1.6 %collective-permute-start.1 = (bf16[128,1024]{1,0:T(8,128)(2,1)S(1)}, bf16[128,1024]{1,0:T(8,128)(2,1)S(1)}, u32[]{:S(2)}, u32[]{:S(2)}) collective-permute-start(bf16[128,1024]{1,0:T(8,128)(2,1)S(1)} %get-tuple-element.68), channel_id=1, source_target_pairs={{0,8},{4,12},{8,0},{12,4},{16,24},{20,28},{24,16},{28,20},{1,9},{5... | collective-permute-start | bytes 786440 | tf_op jit(solution)/shard_map/ppermute | solution.py:19
  9.5 1.5 %collective-permute-start.2 = (bf16[128,1024]{1,0:T(8,128)(2,1)S(1)}, bf16[128,1024]{1,0:T(8,128)(2,1)S(1)}, u32[]{:S(2)}, u32[]{:S(2)}) collective-permute-start(bf16[128,1024]{1,0:T(8,128)(2,1)S(1)} %get-tuple-element.69), channel_id=1, source_target_pairs={{0,16},{4,20},{8,24},{12,28},{16,0},{20,4},{24,8},{28,12},{1,17},{... | collective-permute-start | bytes 786440 | tf_op jit(solution)/shard_map/ppermute | solution.py:19
  11.0 11.3 %collective-permute-done.4.refs_1_.refs_2_ = bf16[128,3072]{1,0:T(8,128)(2,1)S(1)} collective-permute-done((bf16[128,3072]{1,0:T(8,128)(2,1)}, bf16[128,3072]{1,0:T(8,128)(2,1)S(1)}, u32[]{:S(2)}, u32[]{:S(2)}) %collective-permute-start.4) | collective-permute-done | bytes 786464 | tf_op jit(solution)/shard_map/ppermute | solution.py:19
  22.3 2.0 %collective-permute-done.3.refs_0_.refs_1_ = bf16[128,3072]{1,0:T(8,128)(2,1)S(1)} collective-permute-done((bf16[128,3072]{1,0:T(8,128)(2,1)}, bf16[128,3072]{1,0:T(8,128)(2,1)S(1)}, u32[]{:S(2)}, u32[]{:S(2)}) %collective-permute-start.3) | collective-permute-done | bytes 786464 | tf_op jit(solution)/shard_map/ppermute | solution.py:19
  24.3 4.8 %collective-permute-done.1.refs_4_ = bf16[128,1024]{1,0:T(8,128)(2,1)S(1)} collective-permute-done((bf16[128,1024]{1,0:T(8,128)(2,1)S(1)}, bf16[128,1024]{1,0:T(8,128)(2,1)S(1)}, u32[]{:S(2)}, u32[]{:S(2)}) %collective-permute-start.1) | collective-permute-done | bytes 262176 | tf_op jit(solution)/shard_map/ppermute | solution.py:19
  29.6 1.7 %collective-permute-start.6 = (bf16[64,3072]{1,0:T(8,128)(2,1)S(1)}, bf16[64,3072]{1,0:T(8,128)(2,1)S(1)}, u32[]{:S(2)}, u32[]{:S(2)}) collective-permute-start(bf16[64,3072]{1,0:T(8,128)(2,1)S(1)} %get-tuple-element.79), channel_id=1, source_target_pairs={{0,8},{4,12},{8,0},{12,4},{16,24},{20,28},{24,16},{28,20},{1,9},{5... | collective-permute-start | bytes 1179656 | tf_op jit(solution)/shard_map/ppermute | solution.py:19
  31.3 1.5 %collective-permute-start.7 = (bf16[128,1024]{1,0:T(8,128)(2,1)S(1)}, bf16[128,1024]{1,0:T(8,128)(2,1)S(1)}, u32[]{:S(2)}, u32[]{:S(2)}) collective-permute-start(bf16[128,1024]{1,0:T(8,128)(2,1)S(1)} %get-tuple-element.94), channel_id=1, source_target_pairs={{0,24},{4,28},{8,16},{12,20},{16,8},{20,12},{24,0},{28,4},{1,25},{... | collective-permute-start | bytes 786440 | tf_op jit(solution)/shard_map/ppermute | solution.py:19
  32.8 1.1 copy-done.1
  33.9 2.7 %gate_terms.2 = (bf16[384,1024]{1,0:T(8,128)(2,1)S(1)}, bf16[384,1024]{1,0:T(8,128)(2,1)S(1)}) custom-call(bf16[128,3072]{1,0:T(8,128)(2,1)S(1)} %bitcast.7, bf16[128,3072]{1,0:T(8,128)(2,1)S(1)} %collective-permute-done.3.refs_0_.refs_1_, bf16[128,3072]{1,0:T(8,128)(2,1)S(1)} %collective-permute-done.4.refs_1_.refs_2_, ...), custom_call_target="tpu_custom_call" | custom-call | tf_op jit(solution)/shard_map/gate_terms/pallas_call | solution.py:32
  36.7 2.6 %returns.2 = (f32[128,3072]{1,0:T(8,128)S(1)}, bf16[128,4096]{1,0:T(8,128)(2,1)S(1)}, bf16[128,4096]{1,0:T(8,128)(2,1)S(1)}) custom-call(bf16[384,1024]{1,0:T(8,128)(2,1)S(1)} %get-tuple-element.97.gp_ref.refs_5_, bf16[384,1024]{1,0:T(8,128)(2,1)S(1)} %get-tuple-element.85.gate_ref.refs_2_, bf16[3072,512]{1,0:T(8,128)(2,1)S(1)} %copy-done, ...), custom_call_target="tpu_custom_call" | custom-call | tf_op jit(solution)/shard_map/returns/pallas_call | solution.py:32
  39.3 1.2 %collective-permute-done.5.refs_0_.refs_3_ = bf16[64,3072]{1,0:T(8,128)(2,1)S(1)} collective-permute-done((bf16[64,3072]{1,0:T(8,128)(2,1)S(1)}, bf16[64,3072]{1,0:T(8,128)(2,1)S(1)}, u32[]{:S(2)}, u32[]{:S(2)}) %collective-permute-start.5) | collective-permute-done | bytes 393248 | tf_op jit(solution)/shard_map/ppermute | solution.py:19
  40.5 1.2 %collective-permute-done.6.refs_1_.refs_4_ = bf16[64,3072]{1,0:T(8,128)(2,1)S(1)} collective-permute-done((bf16[64,3072]{1,0:T(8,128)(2,1)S(1)}, bf16[64,3072]{1,0:T(8,128)(2,1)S(1)}, u32[]{:S(2)}, u32[]{:S(2)}) %collective-permute-start.6) | collective-permute-done | bytes 393248 | tf_op jit(solution)/shard_map/ppermute | solution.py:19
  41.6 4.8 %collective-permute-done.7.refs_2_ = bf16[128,1024]{1,0:T(8,128)(2,1)S(1)} collective-permute-done((bf16[128,1024]{1,0:T(8,128)(2,1)S(1)}, bf16[128,1024]{1,0:T(8,128)(2,1)S(1)}, u32[]{:S(2)}, u32[]{:S(2)}) %collective-permute-start.7) | collective-permute-done | bytes 262176 | tf_op jit(solution)/shard_map/ppermute | solution.py:19
  46.5 1.0 gate_terms.3
  47.5 1.0 weight_shares.2
  48.6 2.7 %weight_shares.3 = (f32[768,512]{1,0:T(8,128)S(1)}, f32[768,512]{1,0:T(8,128)S(1)}, f32[768,512]{1,0:T(8,128)S(1)}, bf16[768,512]{1,0:T(8,128)(2,1)S(1)}, bf16[1536,512]{1,0:T(8,128)(2,1)S(1)}) custom-call(bf16[128,3072]{1,0:T(8,128)(2,1)S(1)} %bitcast.9, bf16[128,3072]{1,0:T(8,128)(2,1)S(1)} %collective-permute-done.3.refs_0_.refs_1_, ...), custom_call_target="tpu_custom_call" | custom-call | tf_op jit(solution)/shard_map/weight_shares/pallas_call | solution.py:32
  52.1 1.6 %collective-permute-start.10 = (bf16[768,512]{1,0:T(8,128)(2,1)S(1)}, bf16[768,512]{1,0:T(8,128)(2,1)S(1)}, u32[]{:S(2)}, u32[]{:S(2)}) collective-permute-start(bf16[768,512]{1,0:T(8,128)(2,1)S(1)} %add.2), channel_id=1, source_target_pairs={{0,1},{1,0},{2,3},{3,2},{4,5},{5,4},{6,7},{7,6},{8,9},{9,8},{10,11... | collective-permute-start | bytes 2359304 | tf_op jit(solution)/shard_map/ppermute | solution.py:23
  54.6 1.6 %collective-permute-start.15 = (bf16[128,4096]{1,0:T(8,128)(2,1)S(1)}, bf16[128,4096]{1,0:T(8,128)(2,1)S(1)}, u32[]{:S(2)}, u32[]{:S(2)}) collective-permute-start(bf16[128,4096]{1,0:T(8,128)(2,1)S(1)} %get-tuple-element.108), channel_id=1, source_target_pairs={{0,8},{4,12},{8,0},{12,4},{16,24},{20,28},{24,16},{28,20},{1,9},{5... | collective-permute-start | bytes 3145736 | tf_op jit(solution)/shard_map/ppermute | solution.py:19
  56.8 15.3 %collective-permute-done.10.ends_ref = bf16[768,512]{1,0:T(8,128)(2,1)S(1)} collective-permute-done((bf16[768,512]{1,0:T(8,128)(2,1)S(1)}, bf16[768,512]{1,0:T(8,128)(2,1)S(1)}, u32[]{:S(2)}, u32[]{:S(2)}) %collective-permute-start.10) | collective-permute-done | bytes 786464 | tf_op jit(solution)/shard_map/ppermute | solution.py:23
  72.0 4.5 %collective-permute-start.13 = (bf16[768,512]{1,0:T(8,128)(2,1)S(1)}, bf16[768,512]{1,0:T(8,128)(2,1)S(1)}, u32[]{:S(2)}, u32[]{:S(2)}) collective-permute-start(bf16[768,512]{1,0:T(8,128)(2,1)S(1)} %add.3), channel_id=1, source_target_pairs={{0,2},{3,1},{4,6},{7,5},{8,10},{11,9},{12,14},{15,13},{16,18},{19,... | collective-permute-start | bytes 2359304 | tf_op jit(solution)/shard_map/ppermute | solution.py:23
  77.7 2.4 %collective-permute-done.15.refs_3_ = bf16[128,4096]{1,0:T(8,128)(2,1)S(1)} collective-permute-done((bf16[128,4096]{1,0:T(8,128)(2,1)S(1)}, bf16[128,4096]{1,0:T(8,128)(2,1)S(1)}, u32[]{:S(2)}, u32[]{:S(2)}) %collective-permute-start.15) | collective-permute-done | bytes 1048608 | tf_op jit(solution)/shard_map/ppermute | solution.py:19
  80.1 1.2 %collective-permute-done.16.refs_4_ = bf16[128,4096]{1,0:T(8,128)(2,1)S(1)} collective-permute-done((bf16[128,4096]{1,0:T(8,128)(2,1)S(1)}, bf16[128,4096]{1,0:T(8,128)(2,1)S(1)}, u32[]{:S(2)}, u32[]{:S(2)}) %collective-permute-start.16) | collective-permute-done | bytes 1048608 | tf_op jit(solution)/shard_map/ppermute | solution.py:19
  81.3 2.1 %returns.3 = (bf16[64,4096]{1,0:T(8,128)(2,1)S(1)}, bf16[64,4096]{1,0:T(8,128)(2,1)S(1)}) custom-call(bf16[128,1024]{1,0:T(8,128)(2,1)S(1)} %get-tuple-element.112.refs_6_.gp_ref, bf16[128,1024]{1,0:T(8,128)(2,1)S(1)} %get-tuple-element.113.gate_ref, bf16[3072,512]{1,0:T(8,128)(2,1)S(1)} %copy-done, ...), custom_call_target="tpu_custom_call" | custom-call | tf_op jit(solution)/shard_map/returns/pallas_call | solution.py:32
  84.1 2.4 %collective-permute-start.18 = (bf16[64,4096]{1,0:T(8,128)(2,1)S(1)}, bf16[64,4096]{1,0:T(8,128)(2,1)S(1)}, u32[]{:S(2)}, u32[]{:S(2)}) collective-permute-start(bf16[64,4096]{1,0:T(8,128)(2,1)S(1)} %get-tuple-element.115), channel_id=1, source_target_pairs={{0,24},{4,28},{8,16},{12,20},{16,8},{20,12},{24,0},{28,4},{1,25},{... | collective-permute-start | bytes 1572872 | tf_op jit(solution)/shard_map/ppermute | solution.py:19
  86.4 8.1 %collective-permute-done.13.refs_1_ = bf16[768,512]{1,0:T(8,128)(2,1)S(1)} collective-permute-done((bf16[768,512]{1,0:T(8,128)(2,1)S(1)}, bf16[768,512]{1,0:T(8,128)(2,1)S(1)}, u32[]{:S(2)}, u32[]{:S(2)}) %collective-permute-start.13) | collective-permute-done | bytes 786464 | tf_op jit(solution)/shard_map/ppermute | solution.py:23
  94.5 17.3 %collective-permute-done.14.refs_2_ = bf16[768,512]{1,0:T(8,128)(2,1)S(1)} collective-permute-done((bf16[768,512]{1,0:T(8,128)(2,1)S(1)}, bf16[768,512]{1,0:T(8,128)(2,1)S(1)}, u32[]{:S(2)}, u32[]{:S(2)}) %collective-permute-start.14) | collective-permute-done | bytes 786464 | tf_op jit(solution)/shard_map/ppermute | solution.py:23
  111.8 1.7 %total.1 = f32[768,512]{1,0:T(8,128)} custom-call(f32[768,512]{1,0:T(8,128)S(1)} %get-tuple-element.99.own_ref, bf16[1536,512]{1,0:T(8,128)(2,1)S(1)} %collective-permute-done.8.other_ref, bf16[768,512]{1,0:T(8,128)(2,1)S(1)} %collective-permute-done.10.ends_ref, bf16[768,512]{1,0:T(8,128)(2,1)S(1)} %collective-permute-done.12.refs_0_, ...), custom_call_target="tpu_custom_call" | custom-call | tf_op jit(solution)/shard_map/total/pallas_call | solution.py:32
  113.5 1.8 %finish.1 = (bf16[128,3072]{1,0:T(8,128)(2,1)}, bf16[128,4096]{1,0:T(8,128)(2,1)}) custom-call(bf16[128,4096]{1,0:T(8,128)(2,1)S(1)} %bitcast.11, f32[128,3072]{1,0:T(8,128)S(1)} %get-tuple-element.117.refs_1_, bf16[384,1024]{1,0:T(8,128)(2,1)S(1)} %get-tuple-element.85.gate_ref.refs_2_, bf16[128,4096]{1,0:T(8,128)(2,1)S(1)} %collective-permute-done.15.refs_3_, ...), custom_call_target="tpu_custom_call" | custom-call | tf_op jit(solution)/shard_map/finish/pallas_call | solution.py:32
  (29 shorter events, 5.3 us)
Async XLA Ops:
  0.6 7.3 %collective-permute-start = (bf16[3072,512]{1,0:T(8,128)(2,1)}, bf16[3072,512]{1,0:T(8,128)(2,1)S(1)}, u32[]{:S(2)}, u32[]{:S(2)}) collective-permute-start(bf16[3072,512]{1,0:T(8,128)(2,1)} %w_ref.3), channel_id=1, source_target_pairs={{0,4},{4,0},{8,12},{12,8},{16,20},{20,16},{24,28},{28,24},{1,5},{5... | collective-permute-start | bytes 9437192 | tf_op jit(solution)/shard_map/ppermute | solution.py:19
  1.1 21.2 %collective-permute-start.4 = (bf16[128,3072]{1,0:T(8,128)(2,1)}, bf16[128,3072]{1,0:T(8,128)(2,1)S(1)}, u32[]{:S(2)}, u32[]{:S(2)}) collective-permute-start(bf16[128,3072]{1,0:T(8,128)(2,1)} %bitcast.5), channel_id=1, source_target_pairs={{0,16},{4,20},{8,24},{12,28},{16,0},{20,4},{24,8},{28,12},{1,17},{... | collective-permute-start | bytes 2359304 | tf_op jit(solution)/shard_map/ppermute | solution.py:19
  3.7 20.6 %collective-permute-start.3 = (bf16[128,3072]{1,0:T(8,128)(2,1)}, bf16[128,3072]{1,0:T(8,128)(2,1)S(1)}, u32[]{:S(2)}, u32[]{:S(2)}) collective-permute-start(bf16[128,3072]{1,0:T(8,128)(2,1)} %bitcast.6), channel_id=1, source_target_pairs={{0,8},{4,12},{8,0},{12,4},{16,24},{20,28},{24,16},{28,20},{1,9},{5... | collective-permute-start | bytes 2359304 | tf_op jit(solution)/shard_map/ppermute | solution.py:19
  5.2 1.2 %copy-start.2 = (bf16[1,128,4096]{2,1,0:T(8,128)(2,1)S(1)}, bf16[1,128,4096]{2,1,0:T(8,128)(2,1)}, u32[]{:S(2)}) copy-start(bf16[1,128,4096]{2,1,0:T(8,128)(2,1)} %param.6) | copy-start | bytes 3145732
  6.5 1.2 %copy-start.4 = (bf16[1,128,4096]{2,1,0:T(8,128)(2,1)S(1)}, bf16[1,128,4096]{2,1,0:T(8,128)(2,1)}, u32[]{:S(2)}) copy-start(bf16[1,128,4096]{2,1,0:T(8,128)(2,1)} %param.5) | copy-start | bytes 3145732
  7.7 25.1 %copy-start = (bf16[3072,512]{1,0:T(8,128)(2,1)S(1)}, bf16[3072,512]{1,0:T(8,128)(2,1)}, u32[]{:S(2)}) copy-start(bf16[3072,512]{1,0:T(8,128)(2,1)} %w_ref.3) | copy-start | bytes 9437188
  7.9 21.2 %collective-permute-start.1 = (bf16[128,1024]{1,0:T(8,128)(2,1)S(1)}, bf16[128,1024]{1,0:T(8,128)(2,1)S(1)}, u32[]{:S(2)}, u32[]{:S(2)}) collective-permute-start(bf16[128,1024]{1,0:T(8,128)(2,1)S(1)} %get-tuple-element.68), channel_id=1, source_target_pairs={{0,8},{4,12},{8,0},{12,4},{16,24},{20,28},{24,16},{28,20},{1,9},{5... | collective-permute-start | bytes 786440 | tf_op jit(solution)/shard_map/ppermute | solution.py:19
  9.5 19.7 %collective-permute-start.2 = (bf16[128,1024]{1,0:T(8,128)(2,1)S(1)}, bf16[128,1024]{1,0:T(8,128)(2,1)S(1)}, u32[]{:S(2)}, u32[]{:S(2)}) collective-permute-start(bf16[128,1024]{1,0:T(8,128)(2,1)S(1)} %get-tuple-element.69), channel_id=1, source_target_pairs={{0,16},{4,20},{8,24},{12,28},{16,0},{20,4},{24,8},{28,12},{1,17},{... | collective-permute-start | bytes 786440 | tf_op jit(solution)/shard_map/ppermute | solution.py:19
  29.2 11.2 %collective-permute-start.5 = (bf16[64,3072]{1,0:T(8,128)(2,1)S(1)}, bf16[64,3072]{1,0:T(8,128)(2,1)S(1)}, u32[]{:S(2)}, u32[]{:S(2)}) collective-permute-start(bf16[64,3072]{1,0:T(8,128)(2,1)S(1)} %get-tuple-element.78), channel_id=1, source_target_pairs={{0,16},{4,20},{8,24},{12,28},{16,0},{20,4},{24,8},{28,12},{1,17},{... | collective-permute-start | bytes 1179656 | tf_op jit(solution)/shard_map/ppermute | solution.py:19
  29.6 12.1 %collective-permute-start.6 = (bf16[64,3072]{1,0:T(8,128)(2,1)S(1)}, bf16[64,3072]{1,0:T(8,128)(2,1)S(1)}, u32[]{:S(2)}, u32[]{:S(2)}) collective-permute-start(bf16[64,3072]{1,0:T(8,128)(2,1)S(1)} %get-tuple-element.79), channel_id=1, source_target_pairs={{0,8},{4,12},{8,0},{12,4},{16,24},{20,28},{24,16},{28,20},{1,9},{5... | collective-permute-start | bytes 1179656 | tf_op jit(solution)/shard_map/ppermute | solution.py:19
  31.3 15.2 %collective-permute-start.7 = (bf16[128,1024]{1,0:T(8,128)(2,1)S(1)}, bf16[128,1024]{1,0:T(8,128)(2,1)S(1)}, u32[]{:S(2)}, u32[]{:S(2)}) collective-permute-start(bf16[128,1024]{1,0:T(8,128)(2,1)S(1)} %get-tuple-element.94), channel_id=1, source_target_pairs={{0,24},{4,28},{8,16},{12,20},{16,8},{20,12},{24,0},{28,4},{1,25},{... | collective-permute-start | bytes 786440 | tf_op jit(solution)/shard_map/ppermute | solution.py:19
  32.8 1.1 copy-start.1
  48.5 3.4 %collective-permute-start.9 = (bf16[768,512]{1,0:T(8,128)(2,1)S(1)}, bf16[768,512]{1,0:T(8,128)(2,1)S(1)}, u32[]{:S(2)}, u32[]{:S(2)}) collective-permute-start(bf16[768,512]{1,0:T(8,128)(2,1)S(1)} %get-tuple-element.102), channel_id=1, source_target_pairs={{0,4},{4,0},{8,12},{12,8},{16,20},{20,16},{24,28},{28,24},{1,5},{5... | collective-permute-start | bytes 2359304 | tf_op jit(solution)/shard_map/ppermute | solution.py:19
  51.3 2.5 %collective-permute-start.11 = (bf16[768,512]{1,0:T(8,128)(2,1)S(1)}, bf16[768,512]{1,0:T(8,128)(2,1)S(1)}, u32[]{:S(2)}, u32[]{:S(2)}) collective-permute-start(bf16[768,512]{1,0:T(8,128)(2,1)S(1)} %get-tuple-element.104), channel_id=1, source_target_pairs={{0,4},{4,0},{8,12},{12,8},{16,20},{20,16},{24,28},{28,24},{1,5},{5... | collective-permute-start | bytes 2359304 | tf_op jit(solution)/shard_map/ppermute | solution.py:19
  51.8 24.7 %collective-permute-start.8 = (bf16[1536,512]{1,0:T(8,128)(2,1)S(1)}, bf16[1536,512]{1,0:T(8,128)(2,1)S(1)}, u32[]{:S(2)}, u32[]{:S(2)}) collective-permute-start(bf16[1536,512]{1,0:T(8,128)(2,1)S(1)} %get-tuple-element.100), channel_id=1, source_target_pairs={{0,4},{4,0},{8,12},{12,8},{16,20},{20,16},{24,28},{28,24},{1,5},{5... | collective-permute-start | bytes 4718600 | tf_op jit(solution)/shard_map/ppermute | solution.py:19
  52.1 20.0 %collective-permute-start.10 = (bf16[768,512]{1,0:T(8,128)(2,1)S(1)}, bf16[768,512]{1,0:T(8,128)(2,1)S(1)}, u32[]{:S(2)}, u32[]{:S(2)}) collective-permute-start(bf16[768,512]{1,0:T(8,128)(2,1)S(1)} %add.2), channel_id=1, source_target_pairs={{0,1},{1,0},{2,3},{3,2},{4,5},{5,4},{6,7},{7,6},{8,9},{9,8},{10,11... | collective-permute-start | bytes 2359304 | tf_op jit(solution)/shard_map/ppermute | solution.py:23
  53.9 22.7 %collective-permute-start.12 = (bf16[768,512]{1,0:T(8,128)(2,1)S(1)}, bf16[768,512]{1,0:T(8,128)(2,1)S(1)}, u32[]{:S(2)}, u32[]{:S(2)}) collective-permute-start(bf16[768,512]{1,0:T(8,128)(2,1)S(1)} %add.3), channel_id=1, source_target_pairs={{1,2},{2,1},{5,6},{6,5},{9,10},{10,9},{13,14},{14,13},{17,18},{18,... | collective-permute-start | bytes 2359304 | tf_op jit(solution)/shard_map/ppermute | solution.py:23
  54.6 25.5 %collective-permute-start.15 = (bf16[128,4096]{1,0:T(8,128)(2,1)S(1)}, bf16[128,4096]{1,0:T(8,128)(2,1)S(1)}, u32[]{:S(2)}, u32[]{:S(2)}) collective-permute-start(bf16[128,4096]{1,0:T(8,128)(2,1)S(1)} %get-tuple-element.108), channel_id=1, source_target_pairs={{0,8},{4,12},{8,0},{12,4},{16,24},{20,28},{24,16},{28,20},{1,9},{5... | collective-permute-start | bytes 3145736 | tf_op jit(solution)/shard_map/ppermute | solution.py:19
  56.2 25.1 %collective-permute-start.16 = (bf16[128,4096]{1,0:T(8,128)(2,1)S(1)}, bf16[128,4096]{1,0:T(8,128)(2,1)S(1)}, u32[]{:S(2)}, u32[]{:S(2)}) collective-permute-start(bf16[128,4096]{1,0:T(8,128)(2,1)S(1)} %get-tuple-element.109), channel_id=1, source_target_pairs={{0,16},{4,20},{8,24},{12,28},{16,0},{20,4},{24,8},{28,12},{1,17},{... | collective-permute-start | bytes 3145736 | tf_op jit(solution)/shard_map/ppermute | solution.py:19
  72.0 22.5 %collective-permute-start.13 = (bf16[768,512]{1,0:T(8,128)(2,1)S(1)}, bf16[768,512]{1,0:T(8,128)(2,1)S(1)}, u32[]{:S(2)}, u32[]{:S(2)}) collective-permute-start(bf16[768,512]{1,0:T(8,128)(2,1)S(1)} %add.3), channel_id=1, source_target_pairs={{0,2},{3,1},{4,6},{7,5},{8,10},{11,9},{12,14},{15,13},{16,18},{19,... | collective-permute-start | bytes 2359304 | tf_op jit(solution)/shard_map/ppermute | solution.py:23
  76.9 34.8 %collective-permute-start.14 = (bf16[768,512]{1,0:T(8,128)(2,1)S(1)}, bf16[768,512]{1,0:T(8,128)(2,1)S(1)}, u32[]{:S(2)}, u32[]{:S(2)}) collective-permute-start(bf16[768,512]{1,0:T(8,128)(2,1)S(1)} %add_passed.1), channel_id=1, source_target_pairs={{0,1},{1,3},{2,0},{3,2},{4,5},{5,7},{6,4},{7,6},{8,9},{9,11},{10,8... | collective-permute-start | bytes 2359304 | tf_op jit(solution)/shard_map/ppermute | solution.py:23
  83.4 30.0 %collective-permute-start.17 = (bf16[64,4096]{1,0:T(8,128)(2,1)S(1)}, bf16[64,4096]{1,0:T(8,128)(2,1)S(1)}, u32[]{:S(2)}, u32[]{:S(2)}) collective-permute-start(bf16[64,4096]{1,0:T(8,128)(2,1)S(1)} %get-tuple-element.114), channel_id=1, source_target_pairs={{0,24},{4,28},{8,16},{12,20},{16,8},{20,12},{24,0},{28,4},{1,25},{... | collective-permute-start | bytes 1572872 | tf_op jit(solution)/shard_map/ppermute | solution.py:19
  84.1 29.4 %collective-permute-start.18 = (bf16[64,4096]{1,0:T(8,128)(2,1)S(1)}, bf16[64,4096]{1,0:T(8,128)(2,1)S(1)}, u32[]{:S(2)}, u32[]{:S(2)}) collective-permute-start(bf16[64,4096]{1,0:T(8,128)(2,1)S(1)} %get-tuple-element.115), channel_id=1, source_target_pairs={{0,24},{4,28},{8,16},{12,20},{16,8},{20,12},{24,0},{28,4},{1,25},{... | collective-permute-start | bytes 1572872 | tf_op jit(solution)/shard_map/ppermute | solution.py:19
  111.8 1.7 %copy-start.3 = (bf16[1,128,4096]{2,1,0:T(8,128)(2,1)S(1)}, bf16[1,128,4096]{2,1,0:T(8,128)(2,1)}, u32[]{:S(2)}) copy-start(bf16[1,128,4096]{2,1,0:T(8,128)(2,1)} %param.6) | copy-start | bytes 3145732

commit v4 on v3

--- a/solution.py
+++ b/solution.py
@@ -300,11 +300,12 @@
         over = along_dp(middle, [(0, 2), (3, 1)])
         message = add_passed(own3, other34, ends, count)
         last = along_dp(message, [(0, 1), (1, 3), (2, 0), (3, 2)])
-        message, back, gp_far = tie(message, back, gp_far)
     if far:
-        returns = returns_of(0, gp_far, gate_far, gate_weight, w_other, tokens, tokens // 2)
-        back.update({m: [swap(piece, 2 * m) for piece in returns[2 * i : 2 * i + 2]] for i, m in enumerate(far)})
+        returns = returns_of(0, gp_far, gate_far, gate_weight, w_other, tokens, tokens)
+        back.update({m: [swap(piece, 2 * m)] for m, piece in zip(far, returns)})
+    grad_input, grad_attn = finish(cot, mine, gate_near, [back[m] for m in range(1, chips)], width)
     if count == 4:
+        last, grad_input, grad_attn = tie(last, grad_input, grad_attn)
         grad_weight = total(own4, other34, ends, [inner, over, last], count)
     else:
         x_all = jnp.concatenate(x_list, 0)
@@ -316,8 +317,6 @@
             return share[:, :width] + swap(share[:, width:].astype(BF16), 1).astype(F32)
 
         grad_weight = sum_over_line(share_of, count)
-    grad_weight, back, cot = tie(grad_weight, back, cot)
-    grad_input, grad_attn = finish(cot, mine, gate_near, [back[m] for m in range(1, chips)], width)
     return (grad_input[None], grad_attn[None], grad_weight)
 
 

time: 116 us -> 113 us (0.974)
  waiting for transfers between devices: 69.6 us -> 67.1 us
    ppermute x4, waiting for transfers between devices: 40.6 us -> 16.7 us  [along_dp(): return lax.ppermute(x, 'dp', pairs)]
    ppermute x15 -> x14, waiting for transfers between devices: 29 us -> 50.5 us  [swap(): return lax.ppermute(x, 'tensor', [(i, i ^ mask) for i in range(count)])]
    ppermute x15 -> x14, starting transfers between devices: 17.1 us -> 14.7 us  [swap(): return lax.ppermute(x, 'tensor', [(i, i ^ mask) for i in range(count)])]
    ppermute x4, starting transfers between devices: 7.68 us -> 9.93 us  [along_dp(): return lax.ppermute(x, 'dp', pairs)]
  transfers between devices with their start and end apart: 19 -> 18, of which waited for: 12 -> 12; matrix products, arithmetic and copies ran while one was open for 0% -> 0% of each run, Pallas kernels for 11% -> 11%
where the time goes in v4:
time: 113 us
  waiting for transfers between devices  67.1 us (59%)
  starting transfers between devices  24.6 us (22%)
  Pallas kernels  16.6 us (15%)
  local copies, waits for them, and re-layouts  3.59 us (3%)
    ppermute x14, waiting for transfers between devices, swap(): return lax.ppermute(x, 'tensor', [(i, i ^ mask) for i in range(count)])  50.5 us
    ppermute x4, waiting for transfers between devices, along_dp(): return lax.ppermute(x, 'dp', pairs)  16.7 us
    pallas_call x13, Pallas kernels, call(): pl.pallas_call(kernel, in_specs=[spec] * len(operands), out_specs=[spec]...  16.6 us
    ppermute x14, starting transfers between devices, swap(): return lax.ppermute(x, 'tensor', [(i, i ^ mask) for i in range(count)])  14.7 us
    ppermute x4, starting transfers between devices, along_dp(): return lax.ppermute(x, 'dp', pairs)  9.93 us
    unnamed x10, local copies, waits for them, and re-layouts  3.59 us
  transfers between devices with their start and end apart: 18, of which 12 were waited for; matrix products, arithmetic and copies ran while one was open for 0% of the time, Pallas kernels for 11%

profile of v4, /device:TPU:0, one launch (start us, length us, event | category | flops | bytes accessed | tf_op | source)
XLA Modules:
  0.0 112.6 jit_solution(15270352488603421774)
XLA Ops:
  1.1 2.6 %collective-permute-start.4 = (bf16[128,3072]{1,0:T(8,128)(2,1)}, bf16[128,3072]{1,0:T(8,128)(2,1)S(1)}, u32[]{:S(2)}, u32[]{:S(2)}) collective-permute-start(bf16[128,3072]{1,0:T(8,128)(2,1)} %bitcast.5), channel_id=1, source_target_pairs={{0,16},{4,20},{8,24},{12,28},{16,0},{20,4},{24,8},{28,12},{1,17},{... | collective-permute-start | bytes 2359304 | tf_op jit(solution)/shard_map/ppermute | solution.py:19
  3.7 1.5 %collective-permute-start.3 = (bf16[128,3072]{1,0:T(8,128)(2,1)}, bf16[128,3072]{1,0:T(8,128)(2,1)S(1)}, u32[]{:S(2)}, u32[]{:S(2)}) collective-permute-start(bf16[128,3072]{1,0:T(8,128)(2,1)} %bitcast.6), channel_id=1, source_target_pairs={{0,8},{4,12},{8,0},{12,4},{16,24},{20,28},{24,16},{28,20},{1,9},{5... | collective-permute-start | bytes 2359304 | tf_op jit(solution)/shard_map/ppermute | solution.py:19
  5.2 1.2 %copy-done.2 = bf16[1,128,4096]{2,1,0:T(8,128)(2,1)S(1)} copy-done((bf16[1,128,4096]{2,1,0:T(8,128)(2,1)S(1)}, bf16[1,128,4096]{2,1,0:T(8,128)(2,1)}, u32[]{:S(2)}) %copy-start.2) | copy-done | bytes 1048600
  6.5 1.2 %copy-done.4 = bf16[1,128,4096]{2,1,0:T(8,128)(2,1)S(1)} copy-done((bf16[1,128,4096]{2,1,0:T(8,128)(2,1)S(1)}, bf16[1,128,4096]{2,1,0:T(8,128)(2,1)}, u32[]{:S(2)}) %copy-start.4) | copy-done | bytes 1048600
  7.9 1.6 %collective-permute-start.1 = (bf16[128,1024]{1,0:T(8,128)(2,1)S(1)}, bf16[128,1024]{1,0:T(8,128)(2,1)S(1)}, u32[]{:S(2)}, u32[]{:S(2)}) collective-permute-start(bf16[128,1024]{1,0:T(8,128)(2,1)S(1)} %get-tuple-element.60), channel_id=1, source_target_pairs={{0,8},{4,12},{8,0},{12,4},{16,24},{20,28},{24,16},{28,20},{1,9},{5... | collective-permute-start | bytes 786440 | tf_op jit(solution)/shard_map/ppermute | solution.py:19
  9.5 1.5 %collective-permute-start.2 = (bf16[128,1024]{1,0:T(8,128)(2,1)S(1)}, bf16[128,1024]{1,0:T(8,128)(2,1)S(1)}, u32[]{:S(2)}, u32[]{:S(2)}) collective-permute-start(bf16[128,1024]{1,0:T(8,128)(2,1)S(1)} %get-tuple-element.61), channel_id=1, source_target_pairs={{0,16},{4,20},{8,24},{12,28},{16,0},{20,4},{24,8},{28,12},{1,17},{... | collective-permute-start | bytes 786440 | tf_op jit(solution)/shard_map/ppermute | solution.py:19
  11.0 11.3 %collective-permute-done.4.refs_1_.refs_2_ = bf16[128,3072]{1,0:T(8,128)(2,1)S(1)} collective-permute-done((bf16[128,3072]{1,0:T(8,128)(2,1)}, bf16[128,3072]{1,0:T(8,128)(2,1)S(1)}, u32[]{:S(2)}, u32[]{:S(2)}) %collective-permute-start.4) | collective-permute-done | bytes 786464 | tf_op jit(solution)/shard_map/ppermute | solution.py:19
  22.3 2.0 %collective-permute-done.3.refs_0_.refs_1_ = bf16[128,3072]{1,0:T(8,128)(2,1)S(1)} collective-permute-done((bf16[128,3072]{1,0:T(8,128)(2,1)}, bf16[128,3072]{1,0:T(8,128)(2,1)S(1)}, u32[]{:S(2)}, u32[]{:S(2)}) %collective-permute-start.3) | collective-permute-done | bytes 786464 | tf_op jit(solution)/shard_map/ppermute | solution.py:19
  24.3 4.8 %collective-permute-done.1.refs_4_ = bf16[128,1024]{1,0:T(8,128)(2,1)S(1)} collective-permute-done((bf16[128,1024]{1,0:T(8,128)(2,1)S(1)}, bf16[128,1024]{1,0:T(8,128)(2,1)S(1)}, u32[]{:S(2)}, u32[]{:S(2)}) %collective-permute-start.1) | collective-permute-done | bytes 262176 | tf_op jit(solution)/shard_map/ppermute | solution.py:19
  29.6 1.7 %collective-permute-start.6 = (bf16[64,3072]{1,0:T(8,128)(2,1)S(1)}, bf16[64,3072]{1,0:T(8,128)(2,1)S(1)}, u32[]{:S(2)}, u32[]{:S(2)}) collective-permute-start(bf16[64,3072]{1,0:T(8,128)(2,1)S(1)} %get-tuple-element.71), channel_id=1, source_target_pairs={{0,8},{4,12},{8,0},{12,4},{16,24},{20,28},{24,16},{28,20},{1,9},{5... | collective-permute-start | bytes 1179656 | tf_op jit(solution)/shard_map/ppermute | solution.py:19
  31.3 1.5 %collective-permute-start.7 = (bf16[128,1024]{1,0:T(8,128)(2,1)S(1)}, bf16[128,1024]{1,0:T(8,128)(2,1)S(1)}, u32[]{:S(2)}, u32[]{:S(2)}) collective-permute-start(bf16[128,1024]{1,0:T(8,128)(2,1)S(1)} %get-tuple-element.86), channel_id=1, source_target_pairs={{0,24},{4,28},{8,16},{12,20},{16,8},{20,12},{24,0},{28,4},{1,25},{... | collective-permute-start | bytes 786440 | tf_op jit(solution)/shard_map/ppermute | solution.py:19
  32.8 1.1 %copy-done.1 = bf16[1,128,3072]{2,1,0:T(8,128)(2,1)S(1)} copy-done((bf16[1,128,3072]{2,1,0:T(8,128)(2,1)S(1)}, bf16[1,128,3072]{2,1,0:T(8,128)(2,1)}, u32[]{:S(2)}) %copy-start.1) | copy-done | bytes 786456
  33.9 2.7 %gate_terms.2 = (bf16[384,1024]{1,0:T(8,128)(2,1)S(1)}, bf16[384,1024]{1,0:T(8,128)(2,1)S(1)}) custom-call(bf16[128,3072]{1,0:T(8,128)(2,1)S(1)} %bitcast.7, bf16[128,3072]{1,0:T(8,128)(2,1)S(1)} %collective-permute-done.3.refs_0_.refs_1_, bf16[128,3072]{1,0:T(8,128)(2,1)S(1)} %collective-permute-done.4.refs_1_.refs_2_, ...), custom_call_target="tpu_custom_call" | custom-call | tf_op jit(solution)/shard_map/gate_terms/pallas_call | solution.py:32
  36.7 2.6 %returns.2 = (f32[128,3072]{1,0:T(8,128)S(1)}, bf16[128,4096]{1,0:T(8,128)(2,1)S(1)}, bf16[128,4096]{1,0:T(8,128)(2,1)S(1)}) custom-call(bf16[384,1024]{1,0:T(8,128)(2,1)S(1)} %get-tuple-element.89.gp_ref.refs_5_, bf16[384,1024]{1,0:T(8,128)(2,1)S(1)} %get-tuple-element.77.gate_ref.refs_2_, bf16[3072,512]{1,0:T(8,128)(2,1)S(1)} %copy-done, ...), custom_call_target="tpu_custom_call" | custom-call | tf_op jit(solution)/shard_map/returns/pallas_call | solution.py:32
  39.3 1.2 %collective-permute-done.5.refs_0_.refs_3_ = bf16[64,3072]{1,0:T(8,128)(2,1)S(1)} collective-permute-done((bf16[64,3072]{1,0:T(8,128)(2,1)S(1)}, bf16[64,3072]{1,0:T(8,128)(2,1)S(1)}, u32[]{:S(2)}, u32[]{:S(2)}) %collective-permute-start.5) | collective-permute-done | bytes 393248 | tf_op jit(solution)/shard_map/ppermute | solution.py:19
  40.5 1.2 %collective-permute-done.6.refs_1_.refs_4_ = bf16[64,3072]{1,0:T(8,128)(2,1)S(1)} collective-permute-done((bf16[64,3072]{1,0:T(8,128)(2,1)S(1)}, bf16[64,3072]{1,0:T(8,128)(2,1)S(1)}, u32[]{:S(2)}, u32[]{:S(2)}) %collective-permute-start.6) | collective-permute-done | bytes 393248 | tf_op jit(solution)/shard_map/ppermute | solution.py:19
  41.6 4.8 %collective-permute-done.7.refs_2_ = bf16[128,1024]{1,0:T(8,128)(2,1)S(1)} collective-permute-done((bf16[128,1024]{1,0:T(8,128)(2,1)S(1)}, bf16[128,1024]{1,0:T(8,128)(2,1)S(1)}, u32[]{:S(2)}, u32[]{:S(2)}) %collective-permute-start.7) | collective-permute-done | bytes 262176 | tf_op jit(solution)/shard_map/ppermute | solution.py:19
  46.5 1.0 gate_terms.3
  47.5 1.0 weight_shares.2
  48.6 2.7 %weight_shares.3 = (f32[768,512]{1,0:T(8,128)S(1)}, f32[768,512]{1,0:T(8,128)S(1)}, f32[768,512]{1,0:T(8,128)S(1)}, bf16[768,512]{1,0:T(8,128)(2,1)S(1)}, bf16[1536,512]{1,0:T(8,128)(2,1)S(1)}) custom-call(bf16[128,3072]{1,0:T(8,128)(2,1)S(1)} %bitcast.9, bf16[128,3072]{1,0:T(8,128)(2,1)S(1)} %collective-permute-done.3.refs_0_.refs_1_, ...), custom_call_target="tpu_custom_call" | custom-call | tf_op jit(solution)/shard_map/weight_shares/pallas_call | solution.py:32
  52.1 1.6 %collective-permute-start.10 = (bf16[768,512]{1,0:T(8,128)(2,1)S(1)}, bf16[768,512]{1,0:T(8,128)(2,1)S(1)}, u32[]{:S(2)}, u32[]{:S(2)}) collective-permute-start(bf16[768,512]{1,0:T(8,128)(2,1)S(1)} %add.2), channel_id=1, source_target_pairs={{0,1},{1,0},{2,3},{3,2},{4,5},{5,4},{6,7},{7,6},{8,9},{9,8},{10,11... | collective-permute-start | bytes 2359304 | tf_op jit(solution)/shard_map/ppermute | solution.py:23
  54.6 2.1 %returns.3 = bf16[128,4096]{1,0:T(8,128)(2,1)S(1)} custom-call(bf16[128,1024]{1,0:T(8,128)(2,1)S(1)} %get-tuple-element.90.refs_6_.gp_ref, bf16[128,1024]{1,0:T(8,128)(2,1)S(1)} %get-tuple-element.101.gate_ref, bf16[3072,512]{1,0:T(8,128)(2,1)S(1)} %copy-done, bf16[3072,512]{1,0:T(8,128)(2,1)S(1)} %collective-permute-done.refs_7_.w_other_ref.refs_4_), custom_call_target="tpu_custom_call" | custom-call | tf_op jit(solution)/shard_map/returns/pallas_call | solution.py:32
  56.7 1.6 %collective-permute-start.16 = (bf16[128,4096]{1,0:T(8,128)(2,1)S(1)}, bf16[128,4096]{1,0:T(8,128)(2,1)S(1)}, u32[]{:S(2)}, u32[]{:S(2)}) collective-permute-start(bf16[128,4096]{1,0:T(8,128)(2,1)S(1)} %returns.3), channel_id=1, source_target_pairs={{0,24},{4,28},{8,16},{12,20},{16,8},{20,12},{24,0},{28,4},{1,25},{... | collective-permute-start | bytes 3145736 | tf_op jit(solution)/shard_map/ppermute | solution.py:19
  58.9 13.1 %collective-permute-done.10.ends_ref = bf16[768,512]{1,0:T(8,128)(2,1)S(1)} collective-permute-done((bf16[768,512]{1,0:T(8,128)(2,1)S(1)}, bf16[768,512]{1,0:T(8,128)(2,1)S(1)}, u32[]{:S(2)}, u32[]{:S(2)}) %collective-permute-start.10) | collective-permute-done | bytes 786464 | tf_op jit(solution)/shard_map/ppermute | solution.py:23
  73.0 4.6 %collective-permute-start.13 = (bf16[768,512]{1,0:T(8,128)(2,1)S(1)}, bf16[768,512]{1,0:T(8,128)(2,1)S(1)}, u32[]{:S(2)}, u32[]{:S(2)}) collective-permute-start(bf16[768,512]{1,0:T(8,128)(2,1)S(1)} %add_passed.1), channel_id=1, source_target_pairs={{0,1},{1,3},{2,0},{3,2},{4,5},{5,7},{6,4},{7,6},{8,9},{9,11},{10,8... | collective-permute-start | bytes 2359304 | tf_op jit(solution)/shard_map/ppermute | solution.py:23
  77.6 3.0 %collective-permute-start.17 = (bf16[768,512]{1,0:T(8,128)(2,1)S(1)}, bf16[768,512]{1,0:T(8,128)(2,1)S(1)}, u32[]{:S(2)}, u32[]{:S(2)}) collective-permute-start(bf16[768,512]{1,0:T(8,128)(2,1)S(1)} %add.3), channel_id=1, source_target_pairs={{0,2},{3,1},{4,6},{7,5},{8,10},{11,9},{12,14},{15,13},{16,18},{19,... | collective-permute-start | bytes 2359304 | tf_op jit(solution)/shard_map/ppermute | solution.py:23
  80.6 3.2 %collective-permute-done.16.refs_5_ = bf16[128,4096]{1,0:T(8,128)(2,1)S(1)} collective-permute-done((bf16[128,4096]{1,0:T(8,128)(2,1)S(1)}, bf16[128,4096]{1,0:T(8,128)(2,1)S(1)}, u32[]{:S(2)}, u32[]{:S(2)}) %collective-permute-start.16) | collective-permute-done | bytes 1048608 | tf_op jit(solution)/shard_map/ppermute | solution.py:19
  83.7 21.0 %collective-permute-done.14.refs_3_ = bf16[128,4096]{1,0:T(8,128)(2,1)S(1)} collective-permute-done((bf16[128,4096]{1,0:T(8,128)(2,1)S(1)}, bf16[128,4096]{1,0:T(8,128)(2,1)S(1)}, u32[]{:S(2)}, u32[]{:S(2)}) %collective-permute-start.14) | collective-permute-done | bytes 1048608 | tf_op jit(solution)/shard_map/ppermute | solution.py:19
  104.8 0.8 collective-permute-done.15.refs_4_
  105.6 1.8 %finish.1 = (bf16[128,3072]{1,0:T(8,128)(2,1)}, bf16[128,4096]{1,0:T(8,128)(2,1)}) custom-call(bf16[128,4096]{1,0:T(8,128)(2,1)S(1)} %bitcast.11, f32[128,3072]{1,0:T(8,128)S(1)} %get-tuple-element.98.refs_1_, bf16[384,1024]{1,0:T(8,128)(2,1)S(1)} %get-tuple-element.77.gate_ref.refs_2_, bf16[128,4096]{1,0:T(8,128)(2,1)S(1)} %collective-permute-done.14.refs_3_, ...), custom_call_target="tpu_custom_call" | custom-call | tf_op jit(solution)/shard_map/finish/pallas_call | solution.py:32
  107.4 3.5 %collective-permute-done.17.refs_1_ = bf16[768,512]{1,0:T(8,128)(2,1)S(1)} collective-permute-done((bf16[768,512]{1,0:T(8,128)(2,1)S(1)}, bf16[768,512]{1,0:T(8,128)(2,1)S(1)}, u32[]{:S(2)}, u32[]{:S(2)}) %collective-permute-start.17) | collective-permute-done | bytes 786464 | tf_op jit(solution)/shard_map/ppermute | solution.py:23
  110.9 1.7 %total.1 = f32[768,512]{1,0:T(8,128)} custom-call(f32[768,512]{1,0:T(8,128)S(1)} %get-tuple-element.106.own_ref, bf16[1536,512]{1,0:T(8,128)(2,1)S(1)} %collective-permute-done.8.other_ref, bf16[768,512]{1,0:T(8,128)(2,1)S(1)} %collective-permute-done.10.ends_ref, bf16[768,512]{1,0:T(8,128)(2,1)S(1)} %collective-permute-done.12.refs_0_, ...), custom_call_target="tpu_custom_call" | custom-call | tf_op jit(solution)/shard_map/total/pallas_call | solution.py:32
  (27 shorter events, 4.4 us)
Async XLA Ops:
  0.6 7.3 %collective-permute-start = (bf16[3072,512]{1,0:T(8,128)(2,1)}, bf16[3072,512]{1,0:T(8,128)(2,1)S(1)}, u32[]{:S(2)}, u32[]{:S(2)}) collective-permute-start(bf16[3072,512]{1,0:T(8,128)(2,1)} %w_ref.3), channel_id=1, source_target_pairs={{0,4},{4,0},{8,12},{12,8},{16,20},{20,16},{24,28},{28,24},{1,5},{5... | collective-permute-start | bytes 9437192 | tf_op jit(solution)/shard_map/ppermute | solution.py:19
  1.1 21.2 %collective-permute-start.4 = (bf16[128,3072]{1,0:T(8,128)(2,1)}, bf16[128,3072]{1,0:T(8,128)(2,1)S(1)}, u32[]{:S(2)}, u32[]{:S(2)}) collective-permute-start(bf16[128,3072]{1,0:T(8,128)(2,1)} %bitcast.5), channel_id=1, source_target_pairs={{0,16},{4,20},{8,24},{12,28},{16,0},{20,4},{24,8},{28,12},{1,17},{... | collective-permute-start | bytes 2359304 | tf_op jit(solution)/shard_map/ppermute | solution.py:19
  3.7 20.6 %collective-permute-start.3 = (bf16[128,3072]{1,0:T(8,128)(2,1)}, bf16[128,3072]{1,0:T(8,128)(2,1)S(1)}, u32[]{:S(2)}, u32[]{:S(2)}) collective-permute-start(bf16[128,3072]{1,0:T(8,128)(2,1)} %bitcast.6), channel_id=1, source_target_pairs={{0,8},{4,12},{8,0},{12,4},{16,24},{20,28},{24,16},{28,20},{1,9},{5... | collective-permute-start | bytes 2359304 | tf_op jit(solution)/shard_map/ppermute | solution.py:19
  5.2 1.2 %copy-start.2 = (bf16[1,128,4096]{2,1,0:T(8,128)(2,1)S(1)}, bf16[1,128,4096]{2,1,0:T(8,128)(2,1)}, u32[]{:S(2)}) copy-start(bf16[1,128,4096]{2,1,0:T(8,128)(2,1)} %param.6) | copy-start | bytes 3145732
  6.5 1.2 %copy-start.4 = (bf16[1,128,4096]{2,1,0:T(8,128)(2,1)S(1)}, bf16[1,128,4096]{2,1,0:T(8,128)(2,1)}, u32[]{:S(2)}) copy-start(bf16[1,128,4096]{2,1,0:T(8,128)(2,1)} %param.5) | copy-start | bytes 3145732
  7.7 25.1 %copy-start = (bf16[3072,512]{1,0:T(8,128)(2,1)S(1)}, bf16[3072,512]{1,0:T(8,128)(2,1)}, u32[]{:S(2)}) copy-start(bf16[3072,512]{1,0:T(8,128)(2,1)} %w_ref.3) | copy-start | bytes 9437188
  7.9 21.2 %collective-permute-start.1 = (bf16[128,1024]{1,0:T(8,128)(2,1)S(1)}, bf16[128,1024]{1,0:T(8,128)(2,1)S(1)}, u32[]{:S(2)}, u32[]{:S(2)}) collective-permute-start(bf16[128,1024]{1,0:T(8,128)(2,1)S(1)} %get-tuple-element.60), channel_id=1, source_target_pairs={{0,8},{4,12},{8,0},{12,4},{16,24},{20,28},{24,16},{28,20},{1,9},{5... | collective-permute-start | bytes 786440 | tf_op jit(solution)/shard_map/ppermute | solution.py:19
  9.5 19.7 %collective-permute-start.2 = (bf16[128,1024]{1,0:T(8,128)(2,1)S(1)}, bf16[128,1024]{1,0:T(8,128)(2,1)S(1)}, u32[]{:S(2)}, u32[]{:S(2)}) collective-permute-start(bf16[128,1024]{1,0:T(8,128)(2,1)S(1)} %get-tuple-element.61), channel_id=1, source_target_pairs={{0,16},{4,20},{8,24},{12,28},{16,0},{20,4},{24,8},{28,12},{1,17},{... | collective-permute-start | bytes 786440 | tf_op jit(solution)/shard_map/ppermute | solution.py:19
  29.2 11.2 %collective-permute-start.5 = (bf16[64,3072]{1,0:T(8,128)(2,1)S(1)}, bf16[64,3072]{1,0:T(8,128)(2,1)S(1)}, u32[]{:S(2)}, u32[]{:S(2)}) collective-permute-start(bf16[64,3072]{1,0:T(8,128)(2,1)S(1)} %get-tuple-element.70), channel_id=1, source_target_pairs={{0,16},{4,20},{8,24},{12,28},{16,0},{20,4},{24,8},{28,12},{1,17},{... | collective-permute-start | bytes 1179656 | tf_op jit(solution)/shard_map/ppermute | solution.py:19
  29.6 12.1 %collective-permute-start.6 = (bf16[64,3072]{1,0:T(8,128)(2,1)S(1)}, bf16[64,3072]{1,0:T(8,128)(2,1)S(1)}, u32[]{:S(2)}, u32[]{:S(2)}) collective-permute-start(bf16[64,3072]{1,0:T(8,128)(2,1)S(1)} %get-tuple-element.71), channel_id=1, source_target_pairs={{0,8},{4,12},{8,0},{12,4},{16,24},{20,28},{24,16},{28,20},{1,9},{5... | collective-permute-start | bytes 1179656 | tf_op jit(solution)/shard_map/ppermute | solution.py:19
  31.3 15.2 %collective-permute-start.7 = (bf16[128,1024]{1,0:T(8,128)(2,1)S(1)}, bf16[128,1024]{1,0:T(8,128)(2,1)S(1)}, u32[]{:S(2)}, u32[]{:S(2)}) collective-permute-start(bf16[128,1024]{1,0:T(8,128)(2,1)S(1)} %get-tuple-element.86), channel_id=1, source_target_pairs={{0,24},{4,28},{8,16},{12,20},{16,8},{20,12},{24,0},{28,4},{1,25},{... | collective-permute-start | bytes 786440 | tf_op jit(solution)/shard_map/ppermute | solution.py:19
  32.8 1.1 %copy-start.1 = (bf16[1,128,3072]{2,1,0:T(8,128)(2,1)S(1)}, bf16[1,128,3072]{2,1,0:T(8,128)(2,1)}, u32[]{:S(2)}) copy-start(bf16[1,128,3072]{2,1,0:T(8,128)(2,1)} %param.4) | copy-start | bytes 2359300
  48.5 3.4 %collective-permute-start.9 = (bf16[768,512]{1,0:T(8,128)(2,1)S(1)}, bf16[768,512]{1,0:T(8,128)(2,1)S(1)}, u32[]{:S(2)}, u32[]{:S(2)}) collective-permute-start(bf16[768,512]{1,0:T(8,128)(2,1)S(1)} %get-tuple-element.94), channel_id=1, source_target_pairs={{0,4},{4,0},{8,12},{12,8},{16,20},{20,16},{24,28},{28,24},{1,5},{5... | collective-permute-start | bytes 2359304 | tf_op jit(solution)/shard_map/ppermute | solution.py:19
  51.3 2.5 %collective-permute-start.11 = (bf16[768,512]{1,0:T(8,128)(2,1)S(1)}, bf16[768,512]{1,0:T(8,128)(2,1)S(1)}, u32[]{:S(2)}, u32[]{:S(2)}) collective-permute-start(bf16[768,512]{1,0:T(8,128)(2,1)S(1)} %get-tuple-element.96), channel_id=1, source_target_pairs={{0,4},{4,0},{8,12},{12,8},{16,20},{20,16},{24,28},{28,24},{1,5},{5... | collective-permute-start | bytes 2359304 | tf_op jit(solution)/shard_map/ppermute | solution.py:19
  51.8 20.8 %collective-permute-start.8 = (bf16[1536,512]{1,0:T(8,128)(2,1)S(1)}, bf16[1536,512]{1,0:T(8,128)(2,1)S(1)}, u32[]{:S(2)}, u32[]{:S(2)}) collective-permute-start(bf16[1536,512]{1,0:T(8,128)(2,1)S(1)} %get-tuple-element.92), channel_id=1, source_target_pairs={{0,4},{4,0},{8,12},{12,8},{16,20},{20,16},{24,28},{28,24},{1,5},{5... | collective-permute-start | bytes 4718600 | tf_op jit(solution)/shard_map/ppermute | solution.py:19
  52.1 20.0 %collective-permute-start.10 = (bf16[768,512]{1,0:T(8,128)(2,1)S(1)}, bf16[768,512]{1,0:T(8,128)(2,1)S(1)}, u32[]{:S(2)}, u32[]{:S(2)}) collective-permute-start(bf16[768,512]{1,0:T(8,128)(2,1)S(1)} %add.2), channel_id=1, source_target_pairs={{0,1},{1,0},{2,3},{3,2},{4,5},{5,4},{6,7},{7,6},{8,9},{9,8},{10,11... | collective-permute-start | bytes 2359304 | tf_op jit(solution)/shard_map/ppermute | solution.py:23
  53.9 18.7 %collective-permute-start.12 = (bf16[768,512]{1,0:T(8,128)(2,1)S(1)}, bf16[768,512]{1,0:T(8,128)(2,1)S(1)}, u32[]{:S(2)}, u32[]{:S(2)}) collective-permute-start(bf16[768,512]{1,0:T(8,128)(2,1)S(1)} %add.3), channel_id=1, source_target_pairs={{1,2},{2,1},{5,6},{6,5},{9,10},{10,9},{13,14},{14,13},{17,18},{18,... | collective-permute-start | bytes 2359304 | tf_op jit(solution)/shard_map/ppermute | solution.py:23
  56.7 27.0 %collective-permute-start.16 = (bf16[128,4096]{1,0:T(8,128)(2,1)S(1)}, bf16[128,4096]{1,0:T(8,128)(2,1)S(1)}, u32[]{:S(2)}, u32[]{:S(2)}) collective-permute-start(bf16[128,4096]{1,0:T(8,128)(2,1)S(1)} %returns.3), channel_id=1, source_target_pairs={{0,24},{4,28},{8,16},{12,20},{16,8},{20,12},{24,0},{28,4},{1,25},{... | collective-permute-start | bytes 3145736 | tf_op jit(solution)/shard_map/ppermute | solution.py:19
  58.3 46.4 %collective-permute-start.14 = (bf16[128,4096]{1,0:T(8,128)(2,1)S(1)}, bf16[128,4096]{1,0:T(8,128)(2,1)S(1)}, u32[]{:S(2)}, u32[]{:S(2)}) collective-permute-start(bf16[128,4096]{1,0:T(8,128)(2,1)S(1)} %get-tuple-element.99), channel_id=1, source_target_pairs={{0,8},{4,12},{8,0},{12,4},{16,24},{20,28},{24,16},{28,20},{1,9},{5... | collective-permute-start | bytes 3145736 | tf_op jit(solution)/shard_map/ppermute | solution.py:19
  72.0 33.6 %collective-permute-start.15 = (bf16[128,4096]{1,0:T(8,128)(2,1)S(1)}, bf16[128,4096]{1,0:T(8,128)(2,1)S(1)}, u32[]{:S(2)}, u32[]{:S(2)}) collective-permute-start(bf16[128,4096]{1,0:T(8,128)(2,1)S(1)} %get-tuple-element.100), channel_id=1, source_target_pairs={{0,16},{4,20},{8,24},{12,28},{16,0},{20,4},{24,8},{28,12},{1,17},{... | collective-permute-start | bytes 3145736 | tf_op jit(solution)/shard_map/ppermute | solution.py:19
  72.6 33.0 %copy-start.3 = (bf16[1,128,4096]{2,1,0:T(8,128)(2,1)S(1)}, bf16[1,128,4096]{2,1,0:T(8,128)(2,1)}, u32[]{:S(2)}) copy-start(bf16[1,128,4096]{2,1,0:T(8,128)(2,1)} %param.6) | copy-start | bytes 3145732
  73.0 34.5 %collective-permute-start.13 = (bf16[768,512]{1,0:T(8,128)(2,1)S(1)}, bf16[768,512]{1,0:T(8,128)(2,1)S(1)}, u32[]{:S(2)}, u32[]{:S(2)}) collective-permute-start(bf16[768,512]{1,0:T(8,128)(2,1)S(1)} %add_passed.1), channel_id=1, source_target_pairs={{0,1},{1,3},{2,0},{3,2},{4,5},{5,7},{6,4},{7,6},{8,9},{9,11},{10,8... | collective-permute-start | bytes 2359304 | tf_op jit(solution)/shard_map/ppermute | solution.py:23
  77.6 33.4 %collective-permute-start.17 = (bf16[768,512]{1,0:T(8,128)(2,1)S(1)}, bf16[768,512]{1,0:T(8,128)(2,1)S(1)}, u32[]{:S(2)}, u32[]{:S(2)}) collective-permute-start(bf16[768,512]{1,0:T(8,128)(2,1)S(1)} %add.3), channel_id=1, source_target_pairs={{0,2},{3,1},{4,6},{7,5},{8,10},{11,9},{12,14},{15,13},{16,18},{19,... | collective-permute-start | bytes 2359304 | tf_op jit(solution)/shard_map/ppermute | solution.py:23

commit v5 on v2

--- a/solution.py
+++ b/solution.py
@@ -97,6 +97,34 @@
     return call(kernel, "gate_terms", [(shape, BF16)] * 2, *xs, *gas, weight, w_other)
 
 
+def slope_kernel(xs, *refs):
+    w_refs, (gate_ref, slope_ref) = refs[xs : xs + 2], refs[xs + 2 :]
+    x = stack(refs[:xs])
+    width = w_refs[0].shape[1]
+    for i, w_ref in enumerate(w_refs):
+        cols = slice(i * width, (i + 1) * width)
+        gate = jax.nn.sigmoid(jnp.dot(x, w_ref[...], preferred_element_type=F32))
+        gate_ref[:, cols] = gate.astype(BF16)
+        slope_ref[:, cols] = gate * (1.0 - gate)
+
+
+def slope_terms(xs, weight, w_other):
+    shape = (sum(x.shape[0] for x in xs), 2 * weight.shape[1])
+    return call(functools.partial(slope_kernel, len(xs)), "slope_terms", [(shape, BF16), (shape, F32)], *xs, weight, w_other)
+
+
+def apply_kernel(*refs):
+    ga_refs, (slope_ref, gp_ref, other_ref) = refs[:-3], refs[-3:]
+    gp = (stack(ga_refs).astype(F32) * slope_ref[...]).astype(BF16)
+    gp_ref[...] = gp
+    other_ref[...] = gp[:, other_ref.shape[1] :]
+
+
+def apply_slope(gas, slope):
+    total, width = slope.shape
+    return call(apply_kernel, "apply_slope", [((total, width), BF16), ((total, width // 2), BF16)], *gas, slope)
+
+
 def pick(index, table):
     value = jnp.int32(table[-1])
     for i, entry in enumerate(table[:-1]):
@@ -105,7 +133,8 @@
 
 
 def share_kernel(tables, rows, xs, *refs):
-    x_refs, gp_refs, outs = refs[:xs], refs[xs : -2 * len(tables)], refs[-2 * len(tables) :]
+    outs = len(tables) + min(len(tables), 2)
+    x_refs, gp_refs, outs = refs[:xs], refs[xs:-outs], refs[-outs:]
     me = lax.axis_index("dp")
     gp = stack(gp_refs)
     width = outs[0].shape[1]
@@ -113,21 +142,61 @@
         cols = columns_at(pick(me, table), rows)
         x = jnp.concatenate([ref[:, cols] for ref in x_refs], 0)
         share = lax.dot_general(x, gp, ROWS, preferred_element_type=F32)
-        outs[2 * i][...] = share[:, :width]
-        outs[2 * i + 1][...] = share[:, width:].astype(BF16)
+        outs[i][...] = share[:, :width]
+        at = max(i - 1, 0) * rows
+        outs[len(tables) + min(i, 1)][at : at + rows] = share[:, width:].astype(BF16)
 
 
 def weight_shares(tables, xs, gps, count):
     width = gps[0].shape[1] // 2
     rows = xs[0].shape[1] // count
-    shapes = [((rows, width), F32), ((rows, width), BF16)] * len(tables)
+    shapes = [((rows, width), F32)] * len(tables) + [((rows, width), BF16)]
+    if len(tables) > 1:
+        shapes.append((((len(tables) - 1) * rows, width), BF16))
     return call(functools.partial(share_kernel, tables, rows, len(xs)), "weight_shares", shapes, *xs, *gps)
 
 
+def far_share(table, rows, x_refs, gp):
+    cols = columns_at(pick(lax.axis_index("dp"), table), rows)
+    x = jnp.concatenate([ref[:, cols] for ref in x_refs], 0)
+    return lax.dot_general(x, gp, ROWS, preferred_element_type=F32)
+
+
+def first_kernel(table, xs, *refs):
+    x_refs, (gp_ref, arrived_ref, own_ref, other_ref, all_ref, message_ref) = refs[:xs], refs[xs:]
+    rows, width = own_ref.shape
+    half = gp_ref.shape[0]
+    all_ref[:half] = gp_ref[:, :width]
+    all_ref[half:] = arrived_ref[...]
+    share = own_ref[...] + other_ref[...].astype(F32) + far_share(table, rows, x_refs, all_ref[...])
+    message_ref[...] = share.astype(BF16)
+
+
+def first_message(table, xs, gp, arrived, own, other):
+    shapes = [((2 * gp.shape[0], own.shape[1]), BF16), (own.shape, BF16)]
+    return call(functools.partial(first_kernel, table, len(xs)), "first_message", shapes, *xs, gp, arrived, own, other)
+
+
+def far_kernel(tables, xs, others, *refs):
+    count = len(tables)
+    x_refs, gp_ref = refs[:xs], refs[xs]
+    owns, other_refs, outs = refs[xs + 1 :][:count], refs[xs + 1 + count :][:others], refs[-count:]
+    for i, table in enumerate(tables):
+        share = owns[i][...] + far_share(table, owns[i].shape[0], x_refs, gp_ref[...])
+        for ref in other_refs:
+            share = share + ref[...].astype(F32)
+        outs[i][...] = share.astype(outs[i].dtype)
+
+
+def far_shares(tables, xs, gp, owns, others, dtype):
+    shapes = [(own.shape, dtype) for own in owns]
+    kernel = functools.partial(far_kernel, tables, len(xs), len(others))
+    return call(kernel, "far_shares", shapes, *xs, gp, *owns, *others)
+
+
 def return_kernel(own, gp_ref, gate_ref, w_ref, w_other_ref, *outs):
-    width = gp_ref.shape[1] // 2
+    depth, width = w_ref.shape
     tokens = outs[0].shape[0]
-    depth = w_ref.shape[0]
     tile = min(depth, 1024)
     for at in range(0, depth, tile):
         rows = slice(at, at + tile)
@@ -167,6 +236,33 @@
     return call(kernel, "finish", [(mine.shape, BF16), (cot.shape, BF16)], cot, mine, gate, *back)
 
 
+def on_ends(ref, count):
+    me = lax.axis_index("dp")
+    is_end = (me == 0) | (me == count - 1)
+    return jnp.where(is_end, ref[...].astype(F32), 0.0)
+
+
+def pass_kernel(count, kept_ref, other_ref, ends_ref, out_ref):
+    ends = ends_ref[...].astype(F32) - on_ends(ends_ref, count)
+    out_ref[...] = (kept_ref[...] + other_ref[...].astype(F32) + ends).astype(BF16)
+
+
+def add_passed(kept, other, ends, count):
+    return call(functools.partial(pass_kernel, count), "add_passed", [(kept.shape, BF16)], kept, other, ends)[0]
+
+
+def total_kernel(count, own_ref, ends_ref, *refs):
+    total = own_ref[...] + on_ends(ends_ref, count)
+    for ref in refs[:-1]:
+        total = total + ref[...].astype(F32)
+    refs[-1][...] = total
+
+
+def total(own, ends, arrived, count):
+    kernel = functools.partial(total_kernel, count)
+    return call(kernel, "total", [(own.shape, F32)], own, ends, *arrived)[0]
+
+
 def sum_over_line(share_of, count):
     me = lax.axis_index("dp")
     right = left = None
@@ -191,18 +287,17 @@
     near = [1 << bit for bit in range(chips.bit_length() - 1)]
     far = [m for m in range(chips) if m and m not in near]
 
+    first = [0] + near
     xs = {0: [x0]}
     for m in near:
         xs[m] = [swap(x0, 2 * m)]
     w_other = swap(gate_weight, 1)
     ga = products(cot, attn_output[0], chips, width)
     ga, w_other = tie(ga, w_other)
-    ga = [swap(piece, 2 * m) if m else piece for m, piece in enumerate(ga)]
+    ga_near = {m: swap(ga[m], 2 * m) if m else ga[0] for m in first}
 
     pairs = [m for m in far if (m & (m - 1)) in near]
-    held, xs = tie([ga[m] for m in near], xs)
-    for m, piece in zip(near, held):
-        ga[m] = piece
+    ga_near, xs = tie(ga_near, xs)
     if pairs:
         out = halves([xs[bit][0] for m in pairs for bit in (m & -m, m & (m - 1))])
         out, xs = tie(out, xs)
@@ -212,69 +307,59 @@
             xs[m] = [swap(out[i], 2 * (m & (m - 1))), swap(out[i + 1], 2 * (m & -m))]
         else:
             xs[m] = [swap(x0, 2 * m)]
-
-    def terms_of(some):
-        return gate_terms([x for m in some for x in xs[m]], [ga[m] for m in some], gate_weight, w_other)
-
-    first = [0] + near
-    gp_near, gate_near = terms_of(first)
-    mine, *returns = returns_of(1, gp_near, gate_near, gate_weight, w_other, tokens)
-    xs, gp_near, returns = tie(xs, gp_near, returns)
-    gps = [gp_near]
+    ga_far = [swap(ga[m], 2 * m) for m in far]
+
+    x_first = [xs[m][0] for m in first]
+    gp_first, gate_first = gate_terms(x_first, [ga_near[m] for m in first], gate_weight, w_other)
+    if count == 4:
+        to_end, to_middle, passed_on, kept_here = [3, 0, 3, 0], [2, 2, 1, 1], [1, 3, 0, 2], [0, 1, 2, 3]
+        own1, other1 = weight_shares([to_end], x_first, [gp_first], count)
+        other1, gp_first = tie(other1, gp_first)
+        own2, other2 = weight_shares([to_middle], x_first, [gp_first], count)
+        other1, other2 = swap(other1, 1), swap(other2, 1)
+        own3, own4, other3, other4 = weight_shares([passed_on, kept_here], x_first, [gp_first], count)
+        other3, other4 = swap(other3, 1), swap(other4, 1)
+    mine, *returns = returns_of(1, gp_first, gate_first, gate_weight, w_other, tokens)
+    xs, returns = tie(xs, returns)
+    back = {m: swap(piece, 2 * m) for m, piece in zip(near, returns)}
+
     if far:
-        gp_far, gate_far = terms_of(far)
-        gps.append(gp_far)
-    x_list = [x for m in first + far for x in xs[m]]
-
-    back = {m: swap(piece, 2 * m) for m, piece in zip(near, returns)}
-    if count == 4:
-        rows = depth // count
-        own1, other1 = weight_shares([[3, 0, 3, 0]], x_list, gps, count)
-        other1, gps = tie(other1, gps)
-        other1 = swap(other1, 1)
-        own2, other2, own3, other3, own4, other4 = weight_shares(
-            [[2, 2, 1, 1], [1, 3, 0, 2], [0, 1, 2, 3]], x_list, gps, count
-        )
-        other1, other2, other3, other4 = tie(other1, other2, other3, other4)
-        other2 = swap(other2, 1)
-        message = (own1 + other1.astype(F32)).astype(BF16)
-        message, other3, other4 = tie(message, other3, other4)
+        x_far = [x for m in far for x in xs[m]]
+        gate_far, slope = slope_terms(x_far, gate_weight, w_other)
+        x_far = x_far + [swap(x, 1) for x in x_far]
+        gp_far, gp_sent = apply_slope(ga_far, slope)
+        gp_arrived = swap(gp_sent, 1)
+    if count == 4 and far:
+        gp_all, message = first_message(to_end, x_far, gp_far, gp_arrived, own1, other1)
         ends = along_dp(message, [(0, 1), (1, 0), (2, 3), (3, 2)])
-        other3, other4 = swap(other3, 1), swap(other4, 1)
-        middle = (own2 + other2.astype(F32)).astype(BF16)
+        (middle,) = far_shares([to_middle], x_far, gp_all, [own2], [other2], BF16)
         inner = along_dp(middle, [(1, 2), (2, 1)])
+        middle, own3, own4, gp_far, gp_all = tie(middle, own3, own4, gp_far, gp_all)
+        kept, own = far_shares([passed_on, kept_here], x_far, gp_all, [own3, own4], [], F32)
+        ends, inner, kept = tie(ends, inner, kept)
+        over = along_dp(middle, [(0, 2), (3, 1)])
+        last = along_dp(add_passed(kept, other3, ends, count), [(0, 1), (1, 3), (2, 0), (3, 2)])
     if far:
         returns = returns_of(0, gp_far, gate_far, gate_weight, w_other, tokens)
-    if count == 4:
-        kept = own3 + other3.astype(F32)
-        own = own4 + other4.astype(F32)
-        kept, own, middle, ends, inner, returns, back = tie(
-            kept, own, middle, ends, inner, returns, back
-        )
-        me = lax.axis_index("dp")
-        is_end = (me == 0) | (me == count - 1)
-        passed = jnp.where(is_end, 0.0, ends.astype(F32))
-        message = (kept + passed).astype(BF16)
-        own = own + (ends.astype(F32) - passed) + inner.astype(F32)
-        message, own, middle, returns = tie(message, own, middle, returns)
-        last = along_dp(message, [(0, 1), (1, 3), (2, 0), (3, 2)])
-        over = along_dp(middle, [(0, 2), (3, 1)])
-    if far:
         back.update({m: swap(piece, 2 * m) for m, piece in zip(far, returns)})
-    if count == 4:
-        own = own + over.astype(F32)
-    grad_input, grad_attn = finish(cot, mine, gate_near, [back[m] for m in range(1, chips)], width)
-    if count == 4:
-        own, last = tie(own, last)
-        grad_weight = own + last.astype(F32)
+    grad_input, grad_attn = finish(cot, mine, gate_first, [back[m] for m in range(1, chips)], width)
+    if count == 4 and far:
+        last, grad_input, grad_attn = tie(last, grad_input, grad_attn)
+        grad_weight = total(own, ends, [other4, inner, over, last], count)
     else:
-        x_all = jnp.concatenate(x_list, 0)
-        gp_all = jnp.concatenate(gps, 0)
+        rows = depth // count
+        x_first = jnp.concatenate(x_first, 0)
+        x_far = jnp.concatenate(x_far, 0) if far else x_first[:0]
+        gp_all = jnp.concatenate([gp_far[:, :width], gp_arrived], 0) if far else gp_first[:0, :width]
 
         def share_of(k):
-            cols = lax.dynamic_slice_in_dim(x_all, k * (depth // count), depth // count, 1)
-            share = lax.dot_general(cols, gp_all, ROWS, preferred_element_type=F32)
-            return share[:, :width] + swap(share[:, width:].astype(BF16), 1).astype(F32)
+            def term(x, gp):
+                cols = lax.dynamic_slice_in_dim(x, k * rows, rows, 1)
+                return lax.dot_general(cols, gp, ROWS, preferred_element_type=F32)
+
+            share = term(x_first, gp_first)
+            other = swap(share[:, width:].astype(BF16), 1).astype(F32)
+            return share[:, :width] + other + term(x_far, gp_all)
 
         grad_weight = sum_over_line(share_of, count)
     return (grad_input[None], grad_attn[None], grad_weight)

time: 127 us -> 110 us (0.87)
  waiting for transfers between devices: 67.8 us -> 59.9 us
  other arithmetic: 7.84 us -> 0 us
  local copies, waits for them, and re-layouts: 8.52 us -> 3.6 us
  starting transfers between devices: 24.6 us -> 26.8 us
    ppermute x4, waiting for transfers between devices: 32.7 us -> 13.4 us  [along_dp(): return lax.ppermute(x, 'dp', pairs)]
    ppermute x15 -> x18, waiting for transfers between devices: 35.1 us -> 46.6 us  [swap(): return lax.ppermute(x, 'tensor', [(i, i ^ mask) for i in range(count)])]
    add x5 -> x0, other arithmetic: 5.29 us -> none  [the longest x1 1.99 us: on_device(): own = own + (ends.astype(F32) - passed) + inner.astype(F32)]
    unnamed x38 -> x12, local copies, waits for them, and re-layouts: 8.52 us -> 3.6 us
    convert_element_type x2 -> x0, other arithmetic: 2.54 us -> none  [the longest x1 1.4 us: on_device(): message = (own1 + other1.astype(F32)).astype(BF16)]
    ppermute x4, starting transfers between devices: 8.54 us -> 10.6 us  [along_dp(): return lax.ppermute(x, 'dp', pairs)]
    pallas_call x9 -> x16, Pallas kernels: 17.2 us -> 18 us  [call(): pl.pallas_call(kernel, in_specs=[spec] * len(operands), out_specs=[spec]...]
    ppermute x15 -> x18, starting transfers between devices: 16.1 us -> 16.2 us  [swap(): return lax.ppermute(x, 'tensor', [(i, i ^ mask) for i in range(count)])]
  transfers between devices with their start and end apart: 19 -> 22, of which waited for: 10 -> 9; matrix products, arithmetic and copies ran while one was open for 5% -> 0% of each run, Pallas kernels for 9% -> 15%
where the time goes in v5:
time: 110 us; the launch traced here: 109 us
  waiting for transfers between devices  59.9 us (54%)
  starting transfers between devices  26.8 us (24%)
  Pallas kernels  18 us (16%)
  local copies, waits for them, and re-layouts  3.6 us (3%)
    ppermute x18, waiting for transfers between devices, swap(): return lax.ppermute(x, 'tensor', [(i, i ^ mask) for i in range(count)])  46.6 us
    pallas_call x16, Pallas kernels, call(): pl.pallas_call(kernel, in_specs=[spec] * len(operands), out_specs=[spec]...  18 us
    ppermute x18, starting transfers between devices, swap(): return lax.ppermute(x, 'tensor', [(i, i ^ mask) for i in range(count)])  16.2 us
    ppermute x4, waiting for transfers between devices, along_dp(): return lax.ppermute(x, 'dp', pairs)  13.4 us
    ppermute x4, starting transfers between devices, along_dp(): return lax.ppermute(x, 'dp', pairs)  10.6 us
    unnamed x12, local copies, waits for them, and re-layouts  3.6 us
  transfers between devices with their start and end apart: 22, of which 9 were waited for; matrix products, arithmetic and copies ran while one was open for 0% of the time, Pallas kernels for 15%

profile of v5, /device:TPU:0, one launch (start us, length us, event | category | flops | bytes accessed | tf_op | source)
XLA Modules:
  0.0 109.2 jit_solution(2614505966759441884)
XLA Ops:
  1.1 2.6 %collective-permute-start.4 = (bf16[128,3072]{1,0:T(8,128)(2,1)}, bf16[128,3072]{1,0:T(8,128)(2,1)S(1)}, u32[]{:S(2)}, u32[]{:S(2)}) collective-permute-start(bf16[128,3072]{1,0:T(8,128)(2,1)} %bitcast.5), channel_id=1, source_target_pairs={{0,16},{4,20},{8,24},{12,28},{16,0},{20,4},{24,8},{28,12},{1,17},{... | collective-permute-start | bytes 2359304 | tf_op jit(solution)/shard_map/ppermute | solution.py:19
  3.7 1.5 %collective-permute-start.3 = (bf16[128,3072]{1,0:T(8,128)(2,1)}, bf16[128,3072]{1,0:T(8,128)(2,1)S(1)}, u32[]{:S(2)}, u32[]{:S(2)}) collective-permute-start(bf16[128,3072]{1,0:T(8,128)(2,1)} %bitcast.6), channel_id=1, source_target_pairs={{0,8},{4,12},{8,0},{12,4},{16,24},{20,28},{24,16},{28,20},{1,9},{5... | collective-permute-start | bytes 2359304 | tf_op jit(solution)/shard_map/ppermute | solution.py:19
  5.2 1.2 %copy-done.3 = bf16[1,128,4096]{2,1,0:T(8,128)(2,1)S(1)} copy-done((bf16[1,128,4096]{2,1,0:T(8,128)(2,1)S(1)}, bf16[1,128,4096]{2,1,0:T(8,128)(2,1)}, u32[]{:S(2)}) %copy-start.3) | copy-done | bytes 1048600
  6.5 1.2 %copy-done.5 = bf16[1,128,4096]{2,1,0:T(8,128)(2,1)S(1)} copy-done((bf16[1,128,4096]{2,1,0:T(8,128)(2,1)S(1)}, bf16[1,128,4096]{2,1,0:T(8,128)(2,1)}, u32[]{:S(2)}) %copy-start.5) | copy-done | bytes 1048600
  7.9 1.6 %collective-permute-start.1 = (bf16[128,1024]{1,0:T(8,128)(2,1)S(1)}, bf16[128,1024]{1,0:T(8,128)(2,1)S(1)}, u32[]{:S(2)}, u32[]{:S(2)}) collective-permute-start(bf16[128,1024]{1,0:T(8,128)(2,1)S(1)} %get-tuple-element.70), channel_id=1, source_target_pairs={{0,8},{4,12},{8,0},{12,4},{16,24},{20,28},{24,16},{28,20},{1,9},{5... | collective-permute-start | bytes 786440 | tf_op jit(solution)/shard_map/ppermute | solution.py:19
  9.5 1.5 %collective-permute-start.2 = (bf16[128,1024]{1,0:T(8,128)(2,1)S(1)}, bf16[128,1024]{1,0:T(8,128)(2,1)S(1)}, u32[]{:S(2)}, u32[]{:S(2)}) collective-permute-start(bf16[128,1024]{1,0:T(8,128)(2,1)S(1)} %get-tuple-element.71), channel_id=1, source_target_pairs={{0,16},{4,20},{8,24},{12,28},{16,0},{20,4},{24,8},{28,12},{1,17},{... | collective-permute-start | bytes 786440 | tf_op jit(solution)/shard_map/ppermute | solution.py:19
  11.0 11.3 %collective-permute-done.4.refs_1_.refs_2_ = bf16[128,3072]{1,0:T(8,128)(2,1)S(1)} collective-permute-done((bf16[128,3072]{1,0:T(8,128)(2,1)}, bf16[128,3072]{1,0:T(8,128)(2,1)S(1)}, u32[]{:S(2)}, u32[]{:S(2)}) %collective-permute-start.4) | collective-permute-done | bytes 786464 | tf_op jit(solution)/shard_map/ppermute | solution.py:19
  22.3 2.0 %collective-permute-done.3.refs_0_.refs_1_ = bf16[128,3072]{1,0:T(8,128)(2,1)S(1)} collective-permute-done((bf16[128,3072]{1,0:T(8,128)(2,1)}, bf16[128,3072]{1,0:T(8,128)(2,1)S(1)}, u32[]{:S(2)}, u32[]{:S(2)}) %collective-permute-start.3) | collective-permute-done | bytes 786464 | tf_op jit(solution)/shard_map/ppermute | solution.py:19
  24.3 4.8 %collective-permute-done.1.refs_4_ = bf16[128,1024]{1,0:T(8,128)(2,1)S(1)} collective-permute-done((bf16[128,1024]{1,0:T(8,128)(2,1)S(1)}, bf16[128,1024]{1,0:T(8,128)(2,1)S(1)}, u32[]{:S(2)}, u32[]{:S(2)}) %collective-permute-start.1) | collective-permute-done | bytes 262176 | tf_op jit(solution)/shard_map/ppermute | solution.py:19
  29.6 1.7 %collective-permute-start.6 = (bf16[64,3072]{1,0:T(8,128)(2,1)S(1)}, bf16[64,3072]{1,0:T(8,128)(2,1)S(1)}, u32[]{:S(2)}, u32[]{:S(2)}) collective-permute-start(bf16[64,3072]{1,0:T(8,128)(2,1)S(1)} %get-tuple-element.81), channel_id=1, source_target_pairs={{0,8},{4,12},{8,0},{12,4},{16,24},{20,28},{24,16},{28,20},{1,9},{5... | collective-permute-start | bytes 1179656 | tf_op jit(solution)/shard_map/ppermute | solution.py:19
  31.3 1.1 %copy-done.1 = bf16[1,128,3072]{2,1,0:T(8,128)(2,1)S(1)} copy-done((bf16[1,128,3072]{2,1,0:T(8,128)(2,1)S(1)}, bf16[1,128,3072]{2,1,0:T(8,128)(2,1)}, u32[]{:S(2)}) %copy-start.1) | copy-done | bytes 786456
  32.4 2.7 %gate_terms.1 = (bf16[384,1024]{1,0:T(8,128)(2,1)S(1)}, bf16[384,1024]{1,0:T(8,128)(2,1)S(1)}) custom-call(bf16[128,3072]{1,0:T(8,128)(2,1)S(1)} %bitcast.7, bf16[128,3072]{1,0:T(8,128)(2,1)S(1)} %collective-permute-done.3.refs_0_.refs_1_, bf16[128,3072]{1,0:T(8,128)(2,1)S(1)} %collective-permute-done.4.refs_1_.refs_2_, ...), custom_call_target="tpu_custom_call" | custom-call | tf_op jit(solution)/shard_map/gate_terms/pallas_call | solution.py:32
  35.2 1.0 weight_shares.3
  36.3 1.0 weight_shares.4
  37.9 1.5 %collective-permute-start.9 = (bf16[128,1024]{1,0:T(8,128)(2,1)S(1)}, bf16[128,1024]{1,0:T(8,128)(2,1)S(1)}, u32[]{:S(2)}, u32[]{:S(2)}) collective-permute-start(bf16[128,1024]{1,0:T(8,128)(2,1)S(1)} %get-tuple-element.94), channel_id=1, source_target_pairs={{0,24},{4,28},{8,16},{12,20},{16,8},{20,12},{24,0},{28,4},{1,25},{... | collective-permute-start | bytes 786440 | tf_op jit(solution)/shard_map/ppermute | solution.py:19
  39.4 2.6 %returns.2 = (f32[128,3072]{1,0:T(8,128)S(1)}, bf16[128,4096]{1,0:T(8,128)(2,1)S(1)}, bf16[128,4096]{1,0:T(8,128)(2,1)S(1)}) custom-call(bf16[384,1024]{1,0:T(8,128)(2,1)S(1)} %get-tuple-element.88.refs_3_.gp_ref, bf16[384,1024]{1,0:T(8,128)(2,1)S(1)} %get-tuple-element.89.gate_ref.refs_2_, bf16[3072,512]{1,0:T(8,128)(2,1)S(1)} %copy-done, ...), custom_call_target="tpu_custom_call" | custom-call | tf_op jit(solution)/shard_map/returns/pallas_call | solution.py:32
  42.6 1.0 slope_terms.1
  43.6 3.5 %collective-permute-done.9.refs_0_ = bf16[128,1024]{1,0:T(8,128)(2,1)S(1)} collective-permute-done((bf16[128,1024]{1,0:T(8,128)(2,1)S(1)}, bf16[128,1024]{1,0:T(8,128)(2,1)S(1)}, u32[]{:S(2)}, u32[]{:S(2)}) %collective-permute-start.9) | collective-permute-done | bytes 262176 | tf_op jit(solution)/shard_map/ppermute | solution.py:19
  47.2 1.3 %collective-permute-done.10.refs_5_ = bf16[128,512]{1,0:T(8,128)(2,1)S(1)} collective-permute-done((bf16[128,512]{1,0:T(8,128)(2,1)S(1)}, bf16[128,512]{1,0:T(8,128)(2,1)S(1)}, u32[]{:S(2)}, u32[]{:S(2)}) %collective-permute-start.10) | collective-permute-done | bytes 131104 | tf_op jit(solution)/shard_map/ppermute | solution.py:19
  49.0 1.6 %collective-permute-start.12 = (bf16[768,512]{1,0:T(8,128)(2,1)S(1)}, bf16[768,512]{1,0:T(8,128)(2,1)S(1)}, u32[]{:S(2)}, u32[]{:S(2)}) collective-permute-start(bf16[768,512]{1,0:T(8,128)(2,1)S(1)} %get-tuple-element.100), channel_id=1, source_target_pairs={{0,1},{1,0},{2,3},{3,2},{4,5},{5,4},{6,7},{7,6},{8,9},{9,8},{10,11... | collective-permute-start | bytes 2359304 | tf_op jit(solution)/shard_map/ppermute | solution.py:23
  52.8 1.8 %weight_shares.5 = (f32[768,512]{1,0:T(8,128)S(1)}, f32[768,512]{1,0:T(8,128)S(1)}, bf16[768,512]{1,0:T(8,128)(2,1)S(1)}, bf16[768,512]{1,0:T(8,128)(2,1)S(1)}) custom-call(bf16[128,3072]{1,0:T(8,128)(2,1)S(1)} %bitcast.10, bf16[128,3072]{1,0:T(8,128)(2,1)S(1)} %collective-permute-done.3.refs_0_.refs_1_, ...), custom_call_target="tpu_custom_call" | custom-call | tf_op jit(solution)/shard_map/weight_shares/pallas_call | solution.py:32
  54.8 1.2 %collective-permute-start.18 = (bf16[128,4096]{1,0:T(8,128)(2,1)S(1)}, bf16[128,4096]{1,0:T(8,128)(2,1)S(1)}, u32[]{:S(2)}, u32[]{:S(2)}) collective-permute-start(bf16[128,4096]{1,0:T(8,128)(2,1)S(1)} %get-tuple-element.115), channel_id=1, source_target_pairs={{0,16},{4,20},{8,24},{12,28},{16,0},{20,4},{24,8},{28,12},{1,17},{... | collective-permute-start | bytes 3145736 | tf_op jit(solution)/shard_map/ppermute | solution.py:19
  56.0 2.1 %returns.3 = bf16[128,4096]{1,0:T(8,128)(2,1)S(1)} custom-call(bf16[128,1024]{1,0:T(8,128)(2,1)S(1)} %get-tuple-element.116.refs_4_.gp_ref, bf16[128,1024]{1,0:T(8,128)(2,1)S(1)} %get-tuple-element.117.gate_ref, bf16[3072,512]{1,0:T(8,128)(2,1)S(1)} %copy-done, bf16[3072,512]{1,0:T(8,128)(2,1)S(1)} %collective-permute-done.refs_7_.w_other_ref.refs_3_), custom_call_target="tpu_custom_call" | custom-call | tf_op jit(solution)/shard_map/returns/pallas_call | solution.py:32
  58.1 10.5 %collective-permute-done.12.ends_ref = bf16[768,512]{1,0:T(8,128)(2,1)S(1)} collective-permute-done((bf16[768,512]{1,0:T(8,128)(2,1)S(1)}, bf16[768,512]{1,0:T(8,128)(2,1)S(1)}, u32[]{:S(2)}, u32[]{:S(2)}) %collective-permute-start.12) | collective-permute-done | bytes 786464 | tf_op jit(solution)/shard_map/ppermute | solution.py:23
  68.6 1.5 %collective-permute-start.19 = (bf16[128,4096]{1,0:T(8,128)(2,1)S(1)}, bf16[128,4096]{1,0:T(8,128)(2,1)S(1)}, u32[]{:S(2)}, u32[]{:S(2)}) collective-permute-start(bf16[128,4096]{1,0:T(8,128)(2,1)S(1)} %returns.3), channel_id=1, source_target_pairs={{0,24},{4,28},{8,16},{12,20},{16,8},{20,12},{24,0},{28,4},{1,25},{... | collective-permute-start | bytes 3145736 | tf_op jit(solution)/shard_map/ppermute | solution.py:19
  71.1 3.5 %collective-permute-start.16 = (bf16[768,512]{1,0:T(8,128)(2,1)S(1)}, bf16[768,512]{1,0:T(8,128)(2,1)S(1)}, u32[]{:S(2)}, u32[]{:S(2)}) collective-permute-start(bf16[768,512]{1,0:T(8,128)(2,1)S(1)} %add_passed.1), channel_id=1, source_target_pairs={{0,1},{1,3},{2,0},{3,2},{4,5},{5,7},{6,4},{7,6},{8,9},{9,11},{10,8... | collective-permute-start | bytes 2359304 | tf_op jit(solution)/shard_map/ppermute | solution.py:23
  74.7 2.0 %collective-permute-done.17.refs_3_ = bf16[128,4096]{1,0:T(8,128)(2,1)S(1)} collective-permute-done((bf16[128,4096]{1,0:T(8,128)(2,1)S(1)}, bf16[128,4096]{1,0:T(8,128)(2,1)S(1)}, u32[]{:S(2)}, u32[]{:S(2)}) %collective-permute-start.17) | collective-permute-done | bytes 1048608 | tf_op jit(solution)/shard_map/ppermute | solution.py:19
  76.6 4.5 %collective-permute-start.21 = (bf16[768,512]{1,0:T(8,128)(2,1)S(1)}, bf16[768,512]{1,0:T(8,128)(2,1)S(1)}, u32[]{:S(2)}, u32[]{:S(2)}) collective-permute-start(bf16[768,512]{1,0:T(8,128)(2,1)S(1)} %far_shares.2), channel_id=1, source_target_pairs={{0,2},{3,1},{4,6},{7,5},{8,10},{11,9},{12,14},{15,13},{16,18},{19,... | collective-permute-start | bytes 2359304 | tf_op jit(solution)/shard_map/ppermute | solution.py:23
  81.2 21.6 %collective-permute-done.18.refs_4_ = bf16[128,4096]{1,0:T(8,128)(2,1)S(1)} collective-permute-done((bf16[128,4096]{1,0:T(8,128)(2,1)S(1)}, bf16[128,4096]{1,0:T(8,128)(2,1)S(1)}, u32[]{:S(2)}, u32[]{:S(2)}) %collective-permute-start.18) | collective-permute-done | bytes 1048608 | tf_op jit(solution)/shard_map/ppermute | solution.py:19
  102.8 1.8 %finish.1 = (bf16[128,3072]{1,0:T(8,128)(2,1)}, bf16[128,4096]{1,0:T(8,128)(2,1)}) custom-call(bf16[128,4096]{1,0:T(8,128)(2,1)S(1)} %bitcast.12, f32[128,3072]{1,0:T(8,128)S(1)} %get-tuple-element.113.refs_1_, bf16[384,1024]{1,0:T(8,128)(2,1)S(1)} %get-tuple-element.89.gate_ref.refs_2_, bf16[128,4096]{1,0:T(8,128)(2,1)S(1)} %collective-permute-done.17.refs_3_, ...), custom_call_target="tpu_custom_call" | custom-call | tf_op jit(solution)/shard_map/finish/pallas_call | solution.py:32
  104.6 2.9 %collective-permute-done.21.refs_2_ = bf16[768,512]{1,0:T(8,128)(2,1)S(1)} collective-permute-done((bf16[768,512]{1,0:T(8,128)(2,1)S(1)}, bf16[768,512]{1,0:T(8,128)(2,1)S(1)}, u32[]{:S(2)}, u32[]{:S(2)}) %collective-permute-start.21) | collective-permute-done | bytes 786464 | tf_op jit(solution)/shard_map/ppermute | solution.py:23
  107.5 1.7 %total.1 = f32[768,512]{1,0:T(8,128)} custom-call(f32[768,512]{1,0:T(8,128)S(1)} %get-tuple-element.122.own_ref, bf16[768,512]{1,0:T(8,128)(2,1)S(1)} %collective-permute-done.12.ends_ref, bf16[768,512]{1,0:T(8,128)(2,1)S(1)} %collective-permute-done.20.refs_0_, bf16[768,512]{1,0:T(8,128)(2,1)S(1)} %collective-permute-done.14.refs_1_, ...), custom_call_target="tpu_custom_call" | custom-call | tf_op jit(solution)/shard_map/total/pallas_call | solution.py:32
  (40 shorter events, 6.2 us)
Async XLA Ops:
  0.6 7.3 %collective-permute-start = (bf16[3072,512]{1,0:T(8,128)(2,1)}, bf16[3072,512]{1,0:T(8,128)(2,1)S(1)}, u32[]{:S(2)}, u32[]{:S(2)}) collective-permute-start(bf16[3072,512]{1,0:T(8,128)(2,1)} %w_ref.3), channel_id=1, source_target_pairs={{0,4},{4,0},{8,12},{12,8},{16,20},{20,16},{24,28},{28,24},{1,5},{5... | collective-permute-start | bytes 9437192 | tf_op jit(solution)/shard_map/ppermute | solution.py:19
  1.1 21.2 %collective-permute-start.4 = (bf16[128,3072]{1,0:T(8,128)(2,1)}, bf16[128,3072]{1,0:T(8,128)(2,1)S(1)}, u32[]{:S(2)}, u32[]{:S(2)}) collective-permute-start(bf16[128,3072]{1,0:T(8,128)(2,1)} %bitcast.5), channel_id=1, source_target_pairs={{0,16},{4,20},{8,24},{12,28},{16,0},{20,4},{24,8},{28,12},{1,17},{... | collective-permute-start | bytes 2359304 | tf_op jit(solution)/shard_map/ppermute | solution.py:19
  3.7 20.6 %collective-permute-start.3 = (bf16[128,3072]{1,0:T(8,128)(2,1)}, bf16[128,3072]{1,0:T(8,128)(2,1)S(1)}, u32[]{:S(2)}, u32[]{:S(2)}) collective-permute-start(bf16[128,3072]{1,0:T(8,128)(2,1)} %bitcast.6), channel_id=1, source_target_pairs={{0,8},{4,12},{8,0},{12,4},{16,24},{20,28},{24,16},{28,20},{1,9},{5... | collective-permute-start | bytes 2359304 | tf_op jit(solution)/shard_map/ppermute | solution.py:19
  5.2 1.2 %copy-start.3 = (bf16[1,128,4096]{2,1,0:T(8,128)(2,1)S(1)}, bf16[1,128,4096]{2,1,0:T(8,128)(2,1)}, u32[]{:S(2)}) copy-start(bf16[1,128,4096]{2,1,0:T(8,128)(2,1)} %param.6) | copy-start | bytes 3145732
  6.5 1.2 %copy-start.5 = (bf16[1,128,4096]{2,1,0:T(8,128)(2,1)S(1)}, bf16[1,128,4096]{2,1,0:T(8,128)(2,1)}, u32[]{:S(2)}) copy-start(bf16[1,128,4096]{2,1,0:T(8,128)(2,1)} %param.5) | copy-start | bytes 3145732
  7.7 23.6 %copy-start = (bf16[3072,512]{1,0:T(8,128)(2,1)S(1)}, bf16[3072,512]{1,0:T(8,128)(2,1)}, u32[]{:S(2)}) copy-start(bf16[3072,512]{1,0:T(8,128)(2,1)} %w_ref.3) | copy-start | bytes 9437188
  7.9 21.2 %collective-permute-start.1 = (bf16[128,1024]{1,0:T(8,128)(2,1)S(1)}, bf16[128,1024]{1,0:T(8,128)(2,1)S(1)}, u32[]{:S(2)}, u32[]{:S(2)}) collective-permute-start(bf16[128,1024]{1,0:T(8,128)(2,1)S(1)} %get-tuple-element.70), channel_id=1, source_target_pairs={{0,8},{4,12},{8,0},{12,4},{16,24},{20,28},{24,16},{28,20},{1,9},{5... | collective-permute-start | bytes 786440 | tf_op jit(solution)/shard_map/ppermute | solution.py:19
  9.5 19.7 %collective-permute-start.2 = (bf16[128,1024]{1,0:T(8,128)(2,1)S(1)}, bf16[128,1024]{1,0:T(8,128)(2,1)S(1)}, u32[]{:S(2)}, u32[]{:S(2)}) collective-permute-start(bf16[128,1024]{1,0:T(8,128)(2,1)S(1)} %get-tuple-element.71), channel_id=1, source_target_pairs={{0,16},{4,20},{8,24},{12,28},{16,0},{20,4},{24,8},{28,12},{1,17},{... | collective-permute-start | bytes 786440 | tf_op jit(solution)/shard_map/ppermute | solution.py:19
  29.2 12.8 %collective-permute-start.5 = (bf16[64,3072]{1,0:T(8,128)(2,1)S(1)}, bf16[64,3072]{1,0:T(8,128)(2,1)S(1)}, u32[]{:S(2)}, u32[]{:S(2)}) collective-permute-start(bf16[64,3072]{1,0:T(8,128)(2,1)S(1)} %get-tuple-element.80), channel_id=1, source_target_pairs={{0,16},{4,20},{8,24},{12,28},{16,0},{20,4},{24,8},{28,12},{1,17},{... | collective-permute-start | bytes 1179656 | tf_op jit(solution)/shard_map/ppermute | solution.py:19
  29.6 12.4 %collective-permute-start.6 = (bf16[64,3072]{1,0:T(8,128)(2,1)S(1)}, bf16[64,3072]{1,0:T(8,128)(2,1)S(1)}, u32[]{:S(2)}, u32[]{:S(2)}) collective-permute-start(bf16[64,3072]{1,0:T(8,128)(2,1)S(1)} %get-tuple-element.81), channel_id=1, source_target_pairs={{0,8},{4,12},{8,0},{12,4},{16,24},{20,28},{24,16},{28,20},{1,9},{5... | collective-permute-start | bytes 1179656 | tf_op jit(solution)/shard_map/ppermute | solution.py:19
  31.3 1.1 %copy-start.1 = (bf16[1,128,3072]{2,1,0:T(8,128)(2,1)S(1)}, bf16[1,128,3072]{2,1,0:T(8,128)(2,1)}, u32[]{:S(2)}) copy-start(bf16[1,128,3072]{2,1,0:T(8,128)(2,1)} %param.4) | copy-start | bytes 2359300
  36.2 12.3 %collective-permute-start.11 = (bf16[768,512]{1,0:T(8,128)(2,1)S(1)}, bf16[768,512]{1,0:T(8,128)(2,1)S(1)}, u32[]{:S(2)}, u32[]{:S(2)}) collective-permute-start(bf16[768,512]{1,0:T(8,128)(2,1)S(1)} %get-tuple-element.99), channel_id=1, source_target_pairs={{0,4},{4,0},{8,12},{12,8},{16,20},{20,16},{24,28},{28,24},{1,5},{5... | collective-permute-start | bytes 2359304 | tf_op jit(solution)/shard_map/ppermute | solution.py:19
  37.3 14.2 %collective-permute-start.13 = (bf16[768,512]{1,0:T(8,128)(2,1)S(1)}, bf16[768,512]{1,0:T(8,128)(2,1)S(1)}, u32[]{:S(2)}, u32[]{:S(2)}) collective-permute-start(bf16[768,512]{1,0:T(8,128)(2,1)S(1)} %get-tuple-element.103), channel_id=1, source_target_pairs={{0,4},{4,0},{8,12},{12,8},{16,20},{20,16},{24,28},{28,24},{1,5},{5... | collective-permute-start | bytes 2359304 | tf_op jit(solution)/shard_map/ppermute | solution.py:19
  37.9 9.2 %collective-permute-start.9 = (bf16[128,1024]{1,0:T(8,128)(2,1)S(1)}, bf16[128,1024]{1,0:T(8,128)(2,1)S(1)}, u32[]{:S(2)}, u32[]{:S(2)}) collective-permute-start(bf16[128,1024]{1,0:T(8,128)(2,1)S(1)} %get-tuple-element.94), channel_id=1, source_target_pairs={{0,24},{4,28},{8,16},{12,20},{16,8},{20,12},{24,0},{28,4},{1,25},{... | collective-permute-start | bytes 786440 | tf_op jit(solution)/shard_map/ppermute | solution.py:19
  42.0 6.5 %collective-permute-start.7 = (bf16[64,3072]{1,0:T(8,128)(2,1)S(1)}, bf16[64,3072]{1,0:T(8,128)(2,1)S(1)}, u32[]{:S(2)}, u32[]{:S(2)}) collective-permute-start(bf16[64,3072]{1,0:T(8,128)(2,1)S(1)} %collective-permute-done.5.refs_0_), channel_id=1, source_target_pairs={{0,4},{4,0},{8,12},{12,8},{16,20},{20,16},{24,28},{28,24},{1,5},{5... | collective-permute-start | bytes 1179656 | tf_op jit(solution)/shard_map/ppermute | solution.py:19
  42.1 6.4 %collective-permute-start.8 = (bf16[64,3072]{1,0:T(8,128)(2,1)S(1)}, bf16[64,3072]{1,0:T(8,128)(2,1)S(1)}, u32[]{:S(2)}, u32[]{:S(2)}) collective-permute-start(bf16[64,3072]{1,0:T(8,128)(2,1)S(1)} %collective-permute-done.6.refs_1_), channel_id=1, source_target_pairs={{0,4},{4,0},{8,12},{12,8},{16,20},{20,16},{24,28},{28,24},{1,5},{5... | collective-permute-start | bytes 1179656 | tf_op jit(solution)/shard_map/ppermute | solution.py:19
  47.1 1.4 %collective-permute-start.10 = (bf16[128,512]{1,0:T(8,128)(2,1)S(1)}, bf16[128,512]{1,0:T(8,128)(2,1)S(1)}, u32[]{:S(2)}, u32[]{:S(2)}) collective-permute-start(bf16[128,512]{1,0:T(8,128)(2,1)S(1)} %get-tuple-element.97), channel_id=1, source_target_pairs={{0,4},{4,0},{8,12},{12,8},{16,20},{20,16},{24,28},{28,24},{1,5},{5... | collective-permute-start | bytes 393224 | tf_op jit(solution)/shard_map/ppermute | solution.py:19
  49.0 19.7 %collective-permute-start.12 = (bf16[768,512]{1,0:T(8,128)(2,1)S(1)}, bf16[768,512]{1,0:T(8,128)(2,1)S(1)}, u32[]{:S(2)}, u32[]{:S(2)}) collective-permute-start(bf16[768,512]{1,0:T(8,128)(2,1)S(1)} %get-tuple-element.100), channel_id=1, source_target_pairs={{0,1},{1,0},{2,3},{3,2},{4,5},{5,4},{6,7},{7,6},{8,9},{9,8},{10,11... | collective-permute-start | bytes 2359304 | tf_op jit(solution)/shard_map/ppermute | solution.py:23
  50.6 26.0 %collective-permute-start.17 = (bf16[128,4096]{1,0:T(8,128)(2,1)S(1)}, bf16[128,4096]{1,0:T(8,128)(2,1)S(1)}, u32[]{:S(2)}, u32[]{:S(2)}) collective-permute-start(bf16[128,4096]{1,0:T(8,128)(2,1)S(1)} %get-tuple-element.114), channel_id=1, source_target_pairs={{0,8},{4,12},{8,0},{12,4},{16,24},{20,28},{24,16},{28,20},{1,9},{5... | collective-permute-start | bytes 3145736 | tf_op jit(solution)/shard_map/ppermute | solution.py:19
  51.5 1.3 %copy-start.2 = (bf16[1,128,3072]{2,1,0:T(8,128)(2,1)S(1)}, bf16[1,128,3072]{2,1,0:T(8,128)(2,1)}, u32[]{:S(2)}) copy-start(bf16[1,128,3072]{2,1,0:T(8,128)(2,1)} %param.4) | copy-start | bytes 2359300
  51.9 18.8 %collective-permute-start.14 = (bf16[768,512]{1,0:T(8,128)(2,1)S(1)}, bf16[768,512]{1,0:T(8,128)(2,1)S(1)}, u32[]{:S(2)}, u32[]{:S(2)}) collective-permute-start(bf16[768,512]{1,0:T(8,128)(2,1)S(1)} %far_shares.2), channel_id=1, source_target_pairs={{1,2},{2,1},{5,6},{6,5},{9,10},{10,9},{13,14},{14,13},{17,18},{18,... | collective-permute-start | bytes 2359304 | tf_op jit(solution)/shard_map/ppermute | solution.py:23
  54.7 16.1 %collective-permute-start.15 = (bf16[768,512]{1,0:T(8,128)(2,1)S(1)}, bf16[768,512]{1,0:T(8,128)(2,1)S(1)}, u32[]{:S(2)}, u32[]{:S(2)}) collective-permute-start(bf16[768,512]{1,0:T(8,128)(2,1)S(1)} %get-tuple-element.111), channel_id=1, source_target_pairs={{0,4},{4,0},{8,12},{12,8},{16,20},{20,16},{24,28},{28,24},{1,5},{5... | collective-permute-start | bytes 2359304 | tf_op jit(solution)/shard_map/ppermute | solution.py:19
  54.8 48.0 %collective-permute-start.18 = (bf16[128,4096]{1,0:T(8,128)(2,1)S(1)}, bf16[128,4096]{1,0:T(8,128)(2,1)S(1)}, u32[]{:S(2)}, u32[]{:S(2)}) collective-permute-start(bf16[128,4096]{1,0:T(8,128)(2,1)S(1)} %get-tuple-element.115), channel_id=1, source_target_pairs={{0,16},{4,20},{8,24},{12,28},{16,0},{20,4},{24,8},{28,12},{1,17},{... | collective-permute-start | bytes 3145736 | tf_op jit(solution)/shard_map/ppermute | solution.py:19
  68.6 34.2 %collective-permute-start.19 = (bf16[128,4096]{1,0:T(8,128)(2,1)S(1)}, bf16[128,4096]{1,0:T(8,128)(2,1)S(1)}, u32[]{:S(2)}, u32[]{:S(2)}) collective-permute-start(bf16[128,4096]{1,0:T(8,128)(2,1)S(1)} %returns.3), channel_id=1, source_target_pairs={{0,24},{4,28},{8,16},{12,20},{16,8},{20,12},{24,0},{28,4},{1,25},{... | collective-permute-start | bytes 3145736 | tf_op jit(solution)/shard_map/ppermute | solution.py:19
  70.8 32.1 %copy-start.4 = (bf16[1,128,4096]{2,1,0:T(8,128)(2,1)S(1)}, bf16[1,128,4096]{2,1,0:T(8,128)(2,1)}, u32[]{:S(2)}) copy-start(bf16[1,128,4096]{2,1,0:T(8,128)(2,1)} %param.6) | copy-start | bytes 3145732
  71.1 33.5 %collective-permute-start.16 = (bf16[768,512]{1,0:T(8,128)(2,1)S(1)}, bf16[768,512]{1,0:T(8,128)(2,1)S(1)}, u32[]{:S(2)}, u32[]{:S(2)}) collective-permute-start(bf16[768,512]{1,0:T(8,128)(2,1)S(1)} %add_passed.1), channel_id=1, source_target_pairs={{0,1},{1,3},{2,0},{3,2},{4,5},{5,7},{6,4},{7,6},{8,9},{9,11},{10,8... | collective-permute-start | bytes 2359304 | tf_op jit(solution)/shard_map/ppermute | solution.py:23
  74.7 29.9 %collective-permute-start.20 = (bf16[768,512]{1,0:T(8,128)(2,1)S(1)}, bf16[768,512]{1,0:T(8,128)(2,1)S(1)}, u32[]{:S(2)}, u32[]{:S(2)}) collective-permute-start(bf16[768,512]{1,0:T(8,128)(2,1)S(1)} %get-tuple-element.123), channel_id=1, source_target_pairs={{0,4},{4,0},{8,12},{12,8},{16,20},{20,16},{24,28},{28,24},{1,5},{5... | collective-permute-start | bytes 2359304 | tf_op jit(solution)/shard_map/ppermute | solution.py:19
  76.6 30.8 %collective-permute-start.21 = (bf16[768,512]{1,0:T(8,128)(2,1)S(1)}, bf16[768,512]{1,0:T(8,128)(2,1)S(1)}, u32[]{:S(2)}, u32[]{:S(2)}) collective-permute-start(bf16[768,512]{1,0:T(8,128)(2,1)S(1)} %far_shares.2), channel_id=1, source_target_pairs={{0,2},{3,1},{4,6},{7,5},{8,10},{11,9},{12,14},{15,13},{16,18},{19,... | collective-permute-start | bytes 2359304 | tf_op jit(solution)/shard_map/ppermute | solution.py:23

commit v6 on v5

--- a/solution.py
+++ b/solution.py
@@ -63,6 +63,14 @@
 def products(cot, att, chips, width):
     kernel = functools.partial(product_kernel, width)
     return call(kernel, "products", [((cot.shape[0], 2 * width), BF16)] * chips, cot, att)
+
+
+def hold_kernel(x_ref, out_ref):
+    out_ref[...] = x_ref[...]
+
+
+def hold(x):
+    return call(hold_kernel, "hold", [(x.shape, x.dtype)], x)[0]
 
 
 def half_kernel(pairs, *refs):
@@ -297,7 +305,8 @@
     ga_near = {m: swap(ga[m], 2 * m) if m else ga[0] for m in first}
 
     pairs = [m for m in far if (m & (m - 1)) in near]
-    ga_near, xs = tie(ga_near, xs)
+    held = hold(gate_weight)
+    ga, xs, gate_weight = tie(ga, xs, held)
     if pairs:
         out = halves([xs[bit][0] for m in pairs for bit in (m & -m, m & (m - 1))])
         out, xs = tie(out, xs)
@@ -320,12 +329,12 @@
         own3, own4, other3, other4 = weight_shares([passed_on, kept_here], x_first, [gp_first], count)
         other3, other4 = swap(other3, 1), swap(other4, 1)
     mine, *returns = returns_of(1, gp_first, gate_first, gate_weight, w_other, tokens)
-    xs, returns = tie(xs, returns)
     back = {m: swap(piece, 2 * m) for m, piece in zip(near, returns)}
 
     if far:
         x_far = [x for m in far for x in xs[m]]
-        gate_far, slope = slope_terms(x_far, gate_weight, w_other)
+        x_after, mine = tie(x_far, mine)
+        gate_far, slope = slope_terms(x_after, gate_weight, w_other)
         x_far = x_far + [swap(x, 1) for x in x_far]
         gp_far, gp_sent = apply_slope(ga_far, slope)
         gp_arrived = swap(gp_sent, 1)
@@ -336,6 +345,7 @@
         inner = along_dp(middle, [(1, 2), (2, 1)])
         middle, own3, own4, gp_far, gp_all = tie(middle, own3, own4, gp_far, gp_all)
         kept, own = far_shares([passed_on, kept_here], x_far, gp_all, [own3, own4], [], F32)
+        kept, gp_far = tie(kept, gp_far)
         ends, inner, kept = tie(ends, inner, kept)
         over = along_dp(middle, [(0, 2), (3, 1)])
         last = along_dp(add_passed(kept, other3, ends, count), [(0, 1), (1, 3), (2, 0), (3, 2)])

time: 110 us -> 107 us (0.973)
  waiting for transfers between devices: 59.9 us -> 55.9 us
    ppermute x18, waiting for transfers between devices: 46.6 us -> 43.1 us  [swap(): return lax.ppermute(x, 'tensor', [(i, i ^ mask) for i in range(count)])]
    unnamed x12 -> x10, local copies, waits for them, and re-layouts: 3.6 us -> 4.35 us
    pallas_call x16 -> x17, Pallas kernels: 18 us -> 18.2 us  [call(): pl.pallas_call(kernel, in_specs=[spec] * len(operands), out_specs=[spec]...]
  transfers between devices with their start and end apart: 22 -> 22, of which waited for: 9 -> 11; matrix products, arithmetic and copies ran while one was open for 0% -> 0% of each run, Pallas kernels for 15% -> 16%
where the time goes in v6:
time: 107 us; the launch traced here: 106 us
  waiting for transfers between devices  55.9 us (52%)
  starting transfers between devices  27.1 us (25%)
  Pallas kernels  18.2 us (17%)
  local copies, waits for them, and re-layouts  4.35 us (4%)
    ppermute x18, waiting for transfers between devices, swap(): return lax.ppermute(x, 'tensor', [(i, i ^ mask) for i in range(count)])  43.1 us
    pallas_call x17, Pallas kernels, call(): pl.pallas_call(kernel, in_specs=[spec] * len(operands), out_specs=[spec]...  18.2 us
    ppermute x18, starting transfers between devices, swap(): return lax.ppermute(x, 'tensor', [(i, i ^ mask) for i in range(count)])  16.2 us
    ppermute x4, waiting for transfers between devices, along_dp(): return lax.ppermute(x, 'dp', pairs)  12.8 us
    ppermute x4, starting transfers between devices, along_dp(): return lax.ppermute(x, 'dp', pairs)  10.9 us
    unnamed x10, local copies, waits for them, and re-layouts  4.35 us
  transfers between devices with their start and end apart: 22, of which 11 were waited for; matrix products, arithmetic and copies ran while one was open for 0% of the time, Pallas kernels for 16%

profile of v6, /device:TPU:0, one launch (start us, length us, event | category | flops | bytes accessed | tf_op | source)
XLA Modules:
  0.0 106.3 jit_solution(4549294657864029784)
XLA Ops:
  1.1 2.6 %collective-permute-start.1 = (bf16[128,3072]{1,0:T(8,128)(2,1)}, bf16[128,3072]{1,0:T(8,128)(2,1)S(1)}, u32[]{:S(2)}, u32[]{:S(2)}) collective-permute-start(bf16[128,3072]{1,0:T(8,128)(2,1)} %bitcast.5), channel_id=1, source_target_pairs={{0,8},{4,12},{8,0},{12,4},{16,24},{20,28},{24,16},{28,20},{1,9},{5... | collective-permute-start | bytes 2359304 | tf_op jit(solution)/shard_map/ppermute | solution.py:19
  3.7 1.5 %collective-permute-start.2 = (bf16[128,3072]{1,0:T(8,128)(2,1)}, bf16[128,3072]{1,0:T(8,128)(2,1)S(1)}, u32[]{:S(2)}, u32[]{:S(2)}) collective-permute-start(bf16[128,3072]{1,0:T(8,128)(2,1)} %bitcast.6), channel_id=1, source_target_pairs={{0,16},{4,20},{8,24},{12,28},{16,0},{20,4},{24,8},{28,12},{1,17},{... | collective-permute-start | bytes 2359304 | tf_op jit(solution)/shard_map/ppermute | solution.py:19
  5.2 1.2 %copy-done.1 = bf16[1,128,4096]{2,1,0:T(8,128)(2,1)S(1)} copy-done((bf16[1,128,4096]{2,1,0:T(8,128)(2,1)S(1)}, bf16[1,128,4096]{2,1,0:T(8,128)(2,1)}, u32[]{:S(2)}) %copy-start.1) | copy-done | bytes 1048600
  6.5 1.2 %copy-done.4 = bf16[1,128,4096]{2,1,0:T(8,128)(2,1)S(1)} copy-done((bf16[1,128,4096]{2,1,0:T(8,128)(2,1)S(1)}, bf16[1,128,4096]{2,1,0:T(8,128)(2,1)}, u32[]{:S(2)}) %copy-start.4) | copy-done | bytes 1048600
  7.9 1.6 %collective-permute-start.8 = (bf16[128,1024]{1,0:T(8,128)(2,1)S(1)}, bf16[128,1024]{1,0:T(8,128)(2,1)S(1)}, u32[]{:S(2)}, u32[]{:S(2)}) collective-permute-start(bf16[128,1024]{1,0:T(8,128)(2,1)S(1)} %get-tuple-element.70), channel_id=1, source_target_pairs={{0,8},{4,12},{8,0},{12,4},{16,24},{20,28},{24,16},{28,20},{1,9},{5... | collective-permute-start | bytes 786440 | tf_op jit(solution)/shard_map/ppermute | solution.py:19
  9.5 1.5 %collective-permute-start.9 = (bf16[128,1024]{1,0:T(8,128)(2,1)S(1)}, bf16[128,1024]{1,0:T(8,128)(2,1)S(1)}, u32[]{:S(2)}, u32[]{:S(2)}) collective-permute-start(bf16[128,1024]{1,0:T(8,128)(2,1)S(1)} %get-tuple-element.71), channel_id=1, source_target_pairs={{0,16},{4,20},{8,24},{12,28},{16,0},{20,4},{24,8},{28,12},{1,17},{... | collective-permute-start | bytes 786440 | tf_op jit(solution)/shard_map/ppermute | solution.py:19
  11.0 1.9 %copy-done.3 = bf16[3072,512]{1,0:T(8,128)(2,1)S(1)} copy-done((bf16[3072,512]{1,0:T(8,128)(2,1)S(1)}, bf16[3072,512]{1,0:T(8,128)(2,1)}, u32[]{:S(2)}) %copy-start.3) | copy-done | bytes 3145752
  13.1 9.2 %collective-permute-done.1.refs_0_.refs_1_ = bf16[128,3072]{1,0:T(8,128)(2,1)S(1)} collective-permute-done((bf16[128,3072]{1,0:T(8,128)(2,1)}, bf16[128,3072]{1,0:T(8,128)(2,1)S(1)}, u32[]{:S(2)}, u32[]{:S(2)}) %collective-permute-start.1) | collective-permute-done | bytes 786464 | tf_op jit(solution)/shard_map/ppermute | solution.py:19
  22.3 2.0 %collective-permute-done.2.refs_1_.refs_2_ = bf16[128,3072]{1,0:T(8,128)(2,1)S(1)} collective-permute-done((bf16[128,3072]{1,0:T(8,128)(2,1)}, bf16[128,3072]{1,0:T(8,128)(2,1)S(1)}, u32[]{:S(2)}, u32[]{:S(2)}) %collective-permute-start.2) | collective-permute-done | bytes 786464 | tf_op jit(solution)/shard_map/ppermute | solution.py:19
  24.4 1.6 %collective-permute-start.3 = (bf16[64,3072]{1,0:T(8,128)(2,1)S(1)}, bf16[64,3072]{1,0:T(8,128)(2,1)S(1)}, u32[]{:S(2)}, u32[]{:S(2)}) collective-permute-start(bf16[64,3072]{1,0:T(8,128)(2,1)S(1)} %get-tuple-element.78), channel_id=1, source_target_pairs={{0,16},{4,20},{8,24},{12,28},{16,0},{20,4},{24,8},{28,12},{1,17},{... | collective-permute-start | bytes 1179656 | tf_op jit(solution)/shard_map/ppermute | solution.py:19
  26.5 1.5 %collective-permute-done.8.refs_4_ = bf16[128,1024]{1,0:T(8,128)(2,1)S(1)} collective-permute-done((bf16[128,1024]{1,0:T(8,128)(2,1)S(1)}, bf16[128,1024]{1,0:T(8,128)(2,1)S(1)}, u32[]{:S(2)}, u32[]{:S(2)}) %collective-permute-start.8) | collective-permute-done | bytes 262176 | tf_op jit(solution)/shard_map/ppermute | solution.py:19
  27.9 2.0 %collective-permute-done.9.refs_5_ = bf16[128,1024]{1,0:T(8,128)(2,1)S(1)} collective-permute-done((bf16[128,1024]{1,0:T(8,128)(2,1)S(1)}, bf16[128,1024]{1,0:T(8,128)(2,1)S(1)}, u32[]{:S(2)}, u32[]{:S(2)}) %collective-permute-start.9) | collective-permute-done | bytes 262176 | tf_op jit(solution)/shard_map/ppermute | solution.py:19
  29.9 2.7 %gate_terms.1 = (bf16[384,1024]{1,0:T(8,128)(2,1)S(1)}, bf16[384,1024]{1,0:T(8,128)(2,1)S(1)}) custom-call(bf16[128,3072]{1,0:T(8,128)(2,1)S(1)} %bitcast.7, bf16[128,3072]{1,0:T(8,128)(2,1)S(1)} %collective-permute-done.1.refs_0_.refs_1_, bf16[128,3072]{1,0:T(8,128)(2,1)S(1)} %collective-permute-done.2.refs_1_.refs_2_, ...), custom_call_target="tpu_custom_call" | custom-call | tf_op jit(solution)/shard_map/gate_terms/pallas_call | solution.py:32
  32.7 1.0 weight_shares.3
  33.8 1.0 weight_shares.4
  35.4 1.5 %collective-permute-start.7 = (bf16[128,1024]{1,0:T(8,128)(2,1)S(1)}, bf16[128,1024]{1,0:T(8,128)(2,1)S(1)}, u32[]{:S(2)}, u32[]{:S(2)}) collective-permute-start(bf16[128,1024]{1,0:T(8,128)(2,1)S(1)} %get-tuple-element.80), channel_id=1, source_target_pairs={{0,24},{4,28},{8,16},{12,20},{16,8},{20,12},{24,0},{28,4},{1,25},{... | collective-permute-start | bytes 786440 | tf_op jit(solution)/shard_map/ppermute | solution.py:19
  38.1 2.6 %returns.2 = (f32[128,3072]{1,0:T(8,128)S(1)}, bf16[128,4096]{1,0:T(8,128)(2,1)S(1)}, bf16[128,4096]{1,0:T(8,128)(2,1)S(1)}) custom-call(bf16[384,1024]{1,0:T(8,128)(2,1)S(1)} %get-tuple-element.88.refs_3_.gp_ref, bf16[384,1024]{1,0:T(8,128)(2,1)S(1)} %get-tuple-element.89.gate_ref.refs_2_, bf16[3072,512]{1,0:T(8,128)(2,1)S(1)} %hold.1.refs_6_.w_ref.refs_2_, ...), custom_call_target="tpu_custom_call" | custom-call | tf_op jit(solution)/shard_map/returns/pallas_call | solution.py:32
  41.7 2.8 %collective-permute-done.7.refs_0_ = bf16[128,1024]{1,0:T(8,128)(2,1)S(1)} collective-permute-done((bf16[128,1024]{1,0:T(8,128)(2,1)S(1)}, bf16[128,1024]{1,0:T(8,128)(2,1)S(1)}, u32[]{:S(2)}, u32[]{:S(2)}) %collective-permute-start.7) | collective-permute-done | bytes 262176 | tf_op jit(solution)/shard_map/ppermute | solution.py:19
  44.7 1.3 %collective-permute-done.10.refs_5_ = bf16[128,512]{1,0:T(8,128)(2,1)S(1)} collective-permute-done((bf16[128,512]{1,0:T(8,128)(2,1)S(1)}, bf16[128,512]{1,0:T(8,128)(2,1)S(1)}, u32[]{:S(2)}, u32[]{:S(2)}) %collective-permute-start.10) | collective-permute-done | bytes 131104 | tf_op jit(solution)/shard_map/ppermute | solution.py:19
  46.5 1.6 %collective-permute-start.12 = (bf16[768,512]{1,0:T(8,128)(2,1)S(1)}, bf16[768,512]{1,0:T(8,128)(2,1)S(1)}, u32[]{:S(2)}, u32[]{:S(2)}) collective-permute-start(bf16[768,512]{1,0:T(8,128)(2,1)S(1)} %get-tuple-element.98), channel_id=1, source_target_pairs={{0,1},{1,0},{2,3},{3,2},{4,5},{5,4},{6,7},{7,6},{8,9},{9,8},{10,11... | collective-permute-start | bytes 2359304 | tf_op jit(solution)/shard_map/ppermute | solution.py:23
  49.9 1.8 %weight_shares.5 = (f32[768,512]{1,0:T(8,128)S(1)}, f32[768,512]{1,0:T(8,128)S(1)}, bf16[768,512]{1,0:T(8,128)(2,1)S(1)}, bf16[768,512]{1,0:T(8,128)(2,1)S(1)}) custom-call(bf16[128,3072]{1,0:T(8,128)(2,1)S(1)} %bitcast.10, bf16[128,3072]{1,0:T(8,128)(2,1)S(1)} %collective-permute-done.1.refs_0_.refs_1_, ...), custom_call_target="tpu_custom_call" | custom-call | tf_op jit(solution)/shard_map/weight_shares/pallas_call | solution.py:32
  51.9 1.6 %collective-permute-start.18 = (bf16[128,4096]{1,0:T(8,128)(2,1)S(1)}, bf16[128,4096]{1,0:T(8,128)(2,1)S(1)}, u32[]{:S(2)}, u32[]{:S(2)}) collective-permute-start(bf16[128,4096]{1,0:T(8,128)(2,1)S(1)} %get-tuple-element.115), channel_id=1, source_target_pairs={{0,16},{4,20},{8,24},{12,28},{16,0},{20,4},{24,8},{28,12},{1,17},{... | collective-permute-start | bytes 3145736 | tf_op jit(solution)/shard_map/ppermute | solution.py:19
  54.1 2.1 %returns.3 = bf16[128,4096]{1,0:T(8,128)(2,1)S(1)} custom-call(bf16[128,1024]{1,0:T(8,128)(2,1)S(1)} %get-tuple-element.116.refs_4_.gp_ref, bf16[128,1024]{1,0:T(8,128)(2,1)S(1)} %get-tuple-element.117.gate_ref, bf16[3072,512]{1,0:T(8,128)(2,1)S(1)} %hold.1.refs_6_.w_ref.refs_2_, bf16[3072,512]{1,0:T(8,128)(2,1)S(1)} %collective-permute-done.refs_7_.w_other_ref.refs_3_), custom_call_target="tpu_custom_call" | custom-call | tf_op jit(solution)/shard_map/returns/pallas_call | solution.py:32
  56.2 9.9 %collective-permute-done.12.ends_ref = bf16[768,512]{1,0:T(8,128)(2,1)S(1)} collective-permute-done((bf16[768,512]{1,0:T(8,128)(2,1)S(1)}, bf16[768,512]{1,0:T(8,128)(2,1)S(1)}, u32[]{:S(2)}, u32[]{:S(2)}) %collective-permute-start.12) | collective-permute-done | bytes 786464 | tf_op jit(solution)/shard_map/ppermute | solution.py:23
  66.1 1.5 %collective-permute-start.19 = (bf16[128,4096]{1,0:T(8,128)(2,1)S(1)}, bf16[128,4096]{1,0:T(8,128)(2,1)S(1)}, u32[]{:S(2)}, u32[]{:S(2)}) collective-permute-start(bf16[128,4096]{1,0:T(8,128)(2,1)S(1)} %returns.3), channel_id=1, source_target_pairs={{0,24},{4,28},{8,16},{12,20},{16,8},{20,12},{24,0},{28,4},{1,25},{... | collective-permute-start | bytes 3145736 | tf_op jit(solution)/shard_map/ppermute | solution.py:19
  67.9 3.9 %collective-permute-start.16 = (bf16[768,512]{1,0:T(8,128)(2,1)S(1)}, bf16[768,512]{1,0:T(8,128)(2,1)S(1)}, u32[]{:S(2)}, u32[]{:S(2)}) collective-permute-start(bf16[768,512]{1,0:T(8,128)(2,1)S(1)} %add_passed.1), channel_id=1, source_target_pairs={{0,1},{1,3},{2,0},{3,2},{4,5},{5,7},{6,4},{7,6},{8,9},{9,11},{10,8... | collective-permute-start | bytes 2359304 | tf_op jit(solution)/shard_map/ppermute | solution.py:23
  71.8 2.3 %collective-permute-done.17.refs_3_ = bf16[128,4096]{1,0:T(8,128)(2,1)S(1)} collective-permute-done((bf16[128,4096]{1,0:T(8,128)(2,1)S(1)}, bf16[128,4096]{1,0:T(8,128)(2,1)S(1)}, u32[]{:S(2)}, u32[]{:S(2)}) %collective-permute-start.17) | collective-permute-done | bytes 1048608 | tf_op jit(solution)/shard_map/ppermute | solution.py:19
  74.1 4.5 %collective-permute-start.21 = (bf16[768,512]{1,0:T(8,128)(2,1)S(1)}, bf16[768,512]{1,0:T(8,128)(2,1)S(1)}, u32[]{:S(2)}, u32[]{:S(2)}) collective-permute-start(bf16[768,512]{1,0:T(8,128)(2,1)S(1)} %far_shares.2), channel_id=1, source_target_pairs={{0,2},{3,1},{4,6},{7,5},{8,10},{11,9},{12,14},{15,13},{16,18},{19,... | collective-permute-start | bytes 2359304 | tf_op jit(solution)/shard_map/ppermute | solution.py:23
  78.7 21.2 %collective-permute-done.18.refs_4_ = bf16[128,4096]{1,0:T(8,128)(2,1)S(1)} collective-permute-done((bf16[128,4096]{1,0:T(8,128)(2,1)S(1)}, bf16[128,4096]{1,0:T(8,128)(2,1)S(1)}, u32[]{:S(2)}, u32[]{:S(2)}) %collective-permute-start.18) | collective-permute-done | bytes 1048608 | tf_op jit(solution)/shard_map/ppermute | solution.py:19
  99.9 1.8 %finish.1 = (bf16[128,3072]{1,0:T(8,128)(2,1)}, bf16[128,4096]{1,0:T(8,128)(2,1)}) custom-call(bf16[128,4096]{1,0:T(8,128)(2,1)S(1)} %bitcast.12, f32[128,3072]{1,0:T(8,128)S(1)} %get-tuple-element.113.refs_1_, bf16[384,1024]{1,0:T(8,128)(2,1)S(1)} %get-tuple-element.89.gate_ref.refs_2_, bf16[128,4096]{1,0:T(8,128)(2,1)S(1)} %collective-permute-done.17.refs_3_, ...), custom_call_target="tpu_custom_call" | custom-call | tf_op jit(solution)/shard_map/finish/pallas_call | solution.py:32
  101.7 2.9 %collective-permute-done.21.refs_2_ = bf16[768,512]{1,0:T(8,128)(2,1)S(1)} collective-permute-done((bf16[768,512]{1,0:T(8,128)(2,1)S(1)}, bf16[768,512]{1,0:T(8,128)(2,1)S(1)}, u32[]{:S(2)}, u32[]{:S(2)}) %collective-permute-start.21) | collective-permute-done | bytes 786464 | tf_op jit(solution)/shard_map/ppermute | solution.py:23
  104.6 1.7 %total.1 = f32[768,512]{1,0:T(8,128)} custom-call(f32[768,512]{1,0:T(8,128)S(1)} %get-tuple-element.122.own_ref, bf16[768,512]{1,0:T(8,128)(2,1)S(1)} %collective-permute-done.12.ends_ref, bf16[768,512]{1,0:T(8,128)(2,1)S(1)} %collective-permute-done.20.refs_0_, bf16[768,512]{1,0:T(8,128)(2,1)S(1)} %collective-permute-done.14.refs_1_, ...), custom_call_target="tpu_custom_call" | custom-call | tf_op jit(solution)/shard_map/total/pallas_call | solution.py:32
  (39 shorter events, 7.9 us)
Async XLA Ops:
  0.6 7.3 %collective-permute-start = (bf16[3072,512]{1,0:T(8,128)(2,1)}, bf16[3072,512]{1,0:T(8,128)(2,1)S(1)}, u32[]{:S(2)}, u32[]{:S(2)}) collective-permute-start(bf16[3072,512]{1,0:T(8,128)(2,1)} %x_ref.1), channel_id=1, source_target_pairs={{0,4},{4,0},{8,12},{12,8},{16,20},{20,16},{24,28},{28,24},{1,5},{5... | collective-permute-start | bytes 9437192 | tf_op jit(solution)/shard_map/ppermute | solution.py:19
  1.1 21.2 %collective-permute-start.1 = (bf16[128,3072]{1,0:T(8,128)(2,1)}, bf16[128,3072]{1,0:T(8,128)(2,1)S(1)}, u32[]{:S(2)}, u32[]{:S(2)}) collective-permute-start(bf16[128,3072]{1,0:T(8,128)(2,1)} %bitcast.5), channel_id=1, source_target_pairs={{0,8},{4,12},{8,0},{12,4},{16,24},{20,28},{24,16},{28,20},{1,9},{5... | collective-permute-start | bytes 2359304 | tf_op jit(solution)/shard_map/ppermute | solution.py:19
  3.7 20.6 %collective-permute-start.2 = (bf16[128,3072]{1,0:T(8,128)(2,1)}, bf16[128,3072]{1,0:T(8,128)(2,1)S(1)}, u32[]{:S(2)}, u32[]{:S(2)}) collective-permute-start(bf16[128,3072]{1,0:T(8,128)(2,1)} %bitcast.6), channel_id=1, source_target_pairs={{0,16},{4,20},{8,24},{12,28},{16,0},{20,4},{24,8},{28,12},{1,17},{... | collective-permute-start | bytes 2359304 | tf_op jit(solution)/shard_map/ppermute | solution.py:19
  5.2 1.2 %copy-start.1 = (bf16[1,128,4096]{2,1,0:T(8,128)(2,1)S(1)}, bf16[1,128,4096]{2,1,0:T(8,128)(2,1)}, u32[]{:S(2)}) copy-start(bf16[1,128,4096]{2,1,0:T(8,128)(2,1)} %param.6) | copy-start | bytes 3145732
  6.5 1.2 %copy-start.4 = (bf16[1,128,4096]{2,1,0:T(8,128)(2,1)S(1)}, bf16[1,128,4096]{2,1,0:T(8,128)(2,1)}, u32[]{:S(2)}) copy-start(bf16[1,128,4096]{2,1,0:T(8,128)(2,1)} %param.5) | copy-start | bytes 3145732
  7.9 20.0 %collective-permute-start.8 = (bf16[128,1024]{1,0:T(8,128)(2,1)S(1)}, bf16[128,1024]{1,0:T(8,128)(2,1)S(1)}, u32[]{:S(2)}, u32[]{:S(2)}) collective-permute-start(bf16[128,1024]{1,0:T(8,128)(2,1)S(1)} %get-tuple-element.70), channel_id=1, source_target_pairs={{0,8},{4,12},{8,0},{12,4},{16,24},{20,28},{24,16},{28,20},{1,9},{5... | collective-permute-start | bytes 786440 | tf_op jit(solution)/shard_map/ppermute | solution.py:19
  9.5 20.4 %collective-permute-start.9 = (bf16[128,1024]{1,0:T(8,128)(2,1)S(1)}, bf16[128,1024]{1,0:T(8,128)(2,1)S(1)}, u32[]{:S(2)}, u32[]{:S(2)}) collective-permute-start(bf16[128,1024]{1,0:T(8,128)(2,1)S(1)} %get-tuple-element.71), channel_id=1, source_target_pairs={{0,16},{4,20},{8,24},{12,28},{16,0},{20,4},{24,8},{28,12},{1,17},{... | collective-permute-start | bytes 786440 | tf_op jit(solution)/shard_map/ppermute | solution.py:19
  11.0 1.9 %copy-start.3 = (bf16[3072,512]{1,0:T(8,128)(2,1)S(1)}, bf16[3072,512]{1,0:T(8,128)(2,1)}, u32[]{:S(2)}) copy-start(bf16[3072,512]{1,0:T(8,128)(2,1)} %x_ref.1) | copy-start | bytes 9437188
  13.1 16.8 %copy-start = (bf16[1,128,3072]{2,1,0:T(8,128)(2,1)S(1)}, bf16[1,128,3072]{2,1,0:T(8,128)(2,1)}, u32[]{:S(2)}) copy-start(bf16[1,128,3072]{2,1,0:T(8,128)(2,1)} %param.4) | copy-start | bytes 2359300
  24.4 13.2 %collective-permute-start.3 = (bf16[64,3072]{1,0:T(8,128)(2,1)S(1)}, bf16[64,3072]{1,0:T(8,128)(2,1)S(1)}, u32[]{:S(2)}, u32[]{:S(2)}) collective-permute-start(bf16[64,3072]{1,0:T(8,128)(2,1)S(1)} %get-tuple-element.78), channel_id=1, source_target_pairs={{0,16},{4,20},{8,24},{12,28},{16,0},{20,4},{24,8},{28,12},{1,17},{... | collective-permute-start | bytes 1179656 | tf_op jit(solution)/shard_map/ppermute | solution.py:19
  25.9 11.6 %collective-permute-start.4 = (bf16[64,3072]{1,0:T(8,128)(2,1)S(1)}, bf16[64,3072]{1,0:T(8,128)(2,1)S(1)}, u32[]{:S(2)}, u32[]{:S(2)}) collective-permute-start(bf16[64,3072]{1,0:T(8,128)(2,1)S(1)} %get-tuple-element.79), channel_id=1, source_target_pairs={{0,8},{4,12},{8,0},{12,4},{16,24},{20,28},{24,16},{28,20},{1,9},{5... | collective-permute-start | bytes 1179656 | tf_op jit(solution)/shard_map/ppermute | solution.py:19
  33.7 12.3 %collective-permute-start.11 = (bf16[768,512]{1,0:T(8,128)(2,1)S(1)}, bf16[768,512]{1,0:T(8,128)(2,1)S(1)}, u32[]{:S(2)}, u32[]{:S(2)}) collective-permute-start(bf16[768,512]{1,0:T(8,128)(2,1)S(1)} %get-tuple-element.97), channel_id=1, source_target_pairs={{0,4},{4,0},{8,12},{12,8},{16,20},{20,16},{24,28},{28,24},{1,5},{5... | collective-permute-start | bytes 2359304 | tf_op jit(solution)/shard_map/ppermute | solution.py:19
  34.8 13.8 %collective-permute-start.13 = (bf16[768,512]{1,0:T(8,128)(2,1)S(1)}, bf16[768,512]{1,0:T(8,128)(2,1)S(1)}, u32[]{:S(2)}, u32[]{:S(2)}) collective-permute-start(bf16[768,512]{1,0:T(8,128)(2,1)S(1)} %get-tuple-element.101), channel_id=1, source_target_pairs={{0,4},{4,0},{8,12},{12,8},{16,20},{20,16},{24,28},{28,24},{1,5},{5... | collective-permute-start | bytes 2359304 | tf_op jit(solution)/shard_map/ppermute | solution.py:19
  35.4 9.2 %collective-permute-start.7 = (bf16[128,1024]{1,0:T(8,128)(2,1)S(1)}, bf16[128,1024]{1,0:T(8,128)(2,1)S(1)}, u32[]{:S(2)}, u32[]{:S(2)}) collective-permute-start(bf16[128,1024]{1,0:T(8,128)(2,1)S(1)} %get-tuple-element.80), channel_id=1, source_target_pairs={{0,24},{4,28},{8,16},{12,20},{16,8},{20,12},{24,0},{28,4},{1,25},{... | collective-permute-start | bytes 786440 | tf_op jit(solution)/shard_map/ppermute | solution.py:19
  37.6 8.4 %collective-permute-start.5 = (bf16[64,3072]{1,0:T(8,128)(2,1)S(1)}, bf16[64,3072]{1,0:T(8,128)(2,1)S(1)}, u32[]{:S(2)}, u32[]{:S(2)}) collective-permute-start(bf16[64,3072]{1,0:T(8,128)(2,1)S(1)} %collective-permute-done.3.refs_0_), channel_id=1, source_target_pairs={{0,4},{4,0},{8,12},{12,8},{16,20},{20,16},{24,28},{28,24},{1,5},{5... | collective-permute-start | bytes 1179656 | tf_op jit(solution)/shard_map/ppermute | solution.py:19
  37.6 8.4 %collective-permute-start.6 = (bf16[64,3072]{1,0:T(8,128)(2,1)S(1)}, bf16[64,3072]{1,0:T(8,128)(2,1)S(1)}, u32[]{:S(2)}, u32[]{:S(2)}) collective-permute-start(bf16[64,3072]{1,0:T(8,128)(2,1)S(1)} %collective-permute-done.4.refs_1_), channel_id=1, source_target_pairs={{0,4},{4,0},{8,12},{12,8},{16,20},{20,16},{24,28},{28,24},{1,5},{5... | collective-permute-start | bytes 1179656 | tf_op jit(solution)/shard_map/ppermute | solution.py:19
  44.6 1.4 %collective-permute-start.10 = (bf16[128,512]{1,0:T(8,128)(2,1)S(1)}, bf16[128,512]{1,0:T(8,128)(2,1)S(1)}, u32[]{:S(2)}, u32[]{:S(2)}) collective-permute-start(bf16[128,512]{1,0:T(8,128)(2,1)S(1)} %get-tuple-element.95), channel_id=1, source_target_pairs={{0,4},{4,0},{8,12},{12,8},{16,20},{20,16},{24,28},{28,24},{1,5},{5... | collective-permute-start | bytes 393224 | tf_op jit(solution)/shard_map/ppermute | solution.py:19
  46.5 19.7 %collective-permute-start.12 = (bf16[768,512]{1,0:T(8,128)(2,1)S(1)}, bf16[768,512]{1,0:T(8,128)(2,1)S(1)}, u32[]{:S(2)}, u32[]{:S(2)}) collective-permute-start(bf16[768,512]{1,0:T(8,128)(2,1)S(1)} %get-tuple-element.98), channel_id=1, source_target_pairs={{0,1},{1,0},{2,3},{3,2},{4,5},{5,4},{6,7},{7,6},{8,9},{9,8},{10,11... | collective-permute-start | bytes 2359304 | tf_op jit(solution)/shard_map/ppermute | solution.py:23
  48.1 26.0 %collective-permute-start.17 = (bf16[128,4096]{1,0:T(8,128)(2,1)S(1)}, bf16[128,4096]{1,0:T(8,128)(2,1)S(1)}, u32[]{:S(2)}, u32[]{:S(2)}) collective-permute-start(bf16[128,4096]{1,0:T(8,128)(2,1)S(1)} %get-tuple-element.114), channel_id=1, source_target_pairs={{0,8},{4,12},{8,0},{12,4},{16,24},{20,28},{24,16},{28,20},{1,9},{5... | collective-permute-start | bytes 3145736 | tf_op jit(solution)/shard_map/ppermute | solution.py:19
  49.0 18.6 %collective-permute-start.14 = (bf16[768,512]{1,0:T(8,128)(2,1)S(1)}, bf16[768,512]{1,0:T(8,128)(2,1)S(1)}, u32[]{:S(2)}, u32[]{:S(2)}) collective-permute-start(bf16[768,512]{1,0:T(8,128)(2,1)S(1)} %far_shares.2), channel_id=1, source_target_pairs={{1,2},{2,1},{5,6},{6,5},{9,10},{10,9},{13,14},{14,13},{17,18},{18,... | collective-permute-start | bytes 2359304 | tf_op jit(solution)/shard_map/ppermute | solution.py:23
  51.8 15.8 %collective-permute-start.15 = (bf16[768,512]{1,0:T(8,128)(2,1)S(1)}, bf16[768,512]{1,0:T(8,128)(2,1)S(1)}, u32[]{:S(2)}, u32[]{:S(2)}) collective-permute-start(bf16[768,512]{1,0:T(8,128)(2,1)S(1)} %get-tuple-element.111), channel_id=1, source_target_pairs={{0,4},{4,0},{8,12},{12,8},{16,20},{20,16},{24,28},{28,24},{1,5},{5... | collective-permute-start | bytes 2359304 | tf_op jit(solution)/shard_map/ppermute | solution.py:19
  51.9 48.0 %collective-permute-start.18 = (bf16[128,4096]{1,0:T(8,128)(2,1)S(1)}, bf16[128,4096]{1,0:T(8,128)(2,1)S(1)}, u32[]{:S(2)}, u32[]{:S(2)}) collective-permute-start(bf16[128,4096]{1,0:T(8,128)(2,1)S(1)} %get-tuple-element.115), channel_id=1, source_target_pairs={{0,16},{4,20},{8,24},{12,28},{16,0},{20,4},{24,8},{28,12},{1,17},{... | collective-permute-start | bytes 3145736 | tf_op jit(solution)/shard_map/ppermute | solution.py:19
  56.2 43.7 %copy-start.2 = (bf16[1,128,4096]{2,1,0:T(8,128)(2,1)S(1)}, bf16[1,128,4096]{2,1,0:T(8,128)(2,1)}, u32[]{:S(2)}) copy-start(bf16[1,128,4096]{2,1,0:T(8,128)(2,1)} %param.6) | copy-start | bytes 3145732
  66.1 33.8 %collective-permute-start.19 = (bf16[128,4096]{1,0:T(8,128)(2,1)S(1)}, bf16[128,4096]{1,0:T(8,128)(2,1)S(1)}, u32[]{:S(2)}, u32[]{:S(2)}) collective-permute-start(bf16[128,4096]{1,0:T(8,128)(2,1)S(1)} %returns.3), channel_id=1, source_target_pairs={{0,24},{4,28},{8,16},{12,20},{16,8},{20,12},{24,0},{28,4},{1,25},{... | collective-permute-start | bytes 3145736 | tf_op jit(solution)/shard_map/ppermute | solution.py:19
  67.9 33.8 %collective-permute-start.16 = (bf16[768,512]{1,0:T(8,128)(2,1)S(1)}, bf16[768,512]{1,0:T(8,128)(2,1)S(1)}, u32[]{:S(2)}, u32[]{:S(2)}) collective-permute-start(bf16[768,512]{1,0:T(8,128)(2,1)S(1)} %add_passed.1), channel_id=1, source_target_pairs={{0,1},{1,3},{2,0},{3,2},{4,5},{5,7},{6,4},{7,6},{8,9},{9,11},{10,8... | collective-permute-start | bytes 2359304 | tf_op jit(solution)/shard_map/ppermute | solution.py:23
  71.8 29.9 %collective-permute-start.20 = (bf16[768,512]{1,0:T(8,128)(2,1)S(1)}, bf16[768,512]{1,0:T(8,128)(2,1)S(1)}, u32[]{:S(2)}, u32[]{:S(2)}) collective-permute-start(bf16[768,512]{1,0:T(8,128)(2,1)S(1)} %get-tuple-element.123), channel_id=1, source_target_pairs={{0,4},{4,0},{8,12},{12,8},{16,20},{20,16},{24,28},{28,24},{1,5},{5... | collective-permute-start | bytes 2359304 | tf_op jit(solution)/shard_map/ppermute | solution.py:19
  74.1 30.5 %collective-permute-start.21 = (bf16[768,512]{1,0:T(8,128)(2,1)S(1)}, bf16[768,512]{1,0:T(8,128)(2,1)S(1)}, u32[]{:S(2)}, u32[]{:S(2)}) collective-permute-start(bf16[768,512]{1,0:T(8,128)(2,1)S(1)} %far_shares.2), channel_id=1, source_target_pairs={{0,2},{3,1},{4,6},{7,5},{8,10},{11,9},{12,14},{15,13},{16,18},{19,... | collective-permute-start | bytes 2359304 | tf_op jit(solution)/shard_map/ppermute | solution.py:23

commit v7 on v6

--- a/solution.py
+++ b/solution.py
@@ -170,19 +170,23 @@
     return lax.dot_general(x, gp, ROWS, preferred_element_type=F32)
 
 
-def first_kernel(table, xs, *refs):
-    x_refs, (gp_ref, arrived_ref, own_ref, other_ref, all_ref, message_ref) = refs[:xs], refs[xs:]
-    rows, width = own_ref.shape
+def first_kernel(tables, xs, *refs):
+    count = len(tables)
+    x_refs, (gp_ref, arrived_ref), refs = refs[:xs], refs[xs : xs + 2], refs[xs + 2 :]
+    owns, others, (all_ref, *outs) = refs[:count], refs[count : 2 * count], refs[2 * count :]
+    rows, width = owns[0].shape
     half = gp_ref.shape[0]
     all_ref[:half] = gp_ref[:, :width]
     all_ref[half:] = arrived_ref[...]
-    share = own_ref[...] + other_ref[...].astype(F32) + far_share(table, rows, x_refs, all_ref[...])
-    message_ref[...] = share.astype(BF16)
-
-
-def first_message(table, xs, gp, arrived, own, other):
-    shapes = [((2 * gp.shape[0], own.shape[1]), BF16), (own.shape, BF16)]
-    return call(functools.partial(first_kernel, table, len(xs)), "first_message", shapes, *xs, gp, arrived, own, other)
+    for table, own_ref, other_ref, out_ref in zip(tables, owns, others, outs):
+        share = own_ref[...] + other_ref[...].astype(F32) + far_share(table, rows, x_refs, all_ref[...])
+        out_ref[...] = share.astype(BF16)
+
+
+def first_messages(tables, xs, gp, arrived, owns, others):
+    shapes = [((2 * gp.shape[0], owns[0].shape[1]), BF16)] + [(own.shape, BF16) for own in owns]
+    kernel = functools.partial(first_kernel, tables, len(xs))
+    return call(kernel, "first_messages", shapes, *xs, gp, arrived, *owns, *others)
 
 
 def far_kernel(tables, xs, others, *refs):
@@ -306,7 +310,7 @@
 
     pairs = [m for m in far if (m & (m - 1)) in near]
     held = hold(gate_weight)
-    ga, xs, gate_weight = tie(ga, xs, held)
+    ga, xs, gate_weight, w_other = tie(ga, xs, held, w_other)
     if pairs:
         out = halves([xs[bit][0] for m in pairs for bit in (m & -m, m & (m - 1))])
         out, xs = tie(out, xs)
@@ -339,9 +343,10 @@
         gp_far, gp_sent = apply_slope(ga_far, slope)
         gp_arrived = swap(gp_sent, 1)
     if count == 4 and far:
-        gp_all, message = first_message(to_end, x_far, gp_far, gp_arrived, own1, other1)
+        gp_all, message, middle = first_messages(
+            [to_end, to_middle], x_far, gp_far, gp_arrived, [own1, own2], [other1, other2]
+        )
         ends = along_dp(message, [(0, 1), (1, 0), (2, 3), (3, 2)])
-        (middle,) = far_shares([to_middle], x_far, gp_all, [own2], [other2], BF16)
         inner = along_dp(middle, [(1, 2), (2, 1)])
         middle, own3, own4, gp_far, gp_all = tie(middle, own3, own4, gp_far, gp_all)
         kept, own = far_shares([passed_on, kept_here], x_far, gp_all, [own3, own4], [], F32)

time: 107 us -> 107 us (level)
    pallas_call x17 -> x16, Pallas kernels: 18.2 us -> 18 us  [call(): pl.pallas_call(kernel, in_specs=[spec] * len(operands), out_specs=[spec]...]
  transfers between devices with their start and end apart: 22 -> 22, of which waited for: 11 -> 11; matrix products, arithmetic and copies ran while one was open for 0% -> 0% of each run, Pallas kernels for 16% -> 15%
where the time goes in v7:
time: 107 us; the launch traced here: 106 us
  waiting for transfers between devices  56.3 us (53%)
  starting transfers between devices  26.6 us (25%)
  Pallas kernels  18 us (17%)
  local copies, waits for them, and re-layouts  4.35 us (4%)
    ppermute x18, waiting for transfers between devices, swap(): return lax.ppermute(x, 'tensor', [(i, i ^ mask) for i in range(count)])  43.1 us
    pallas_call x16, Pallas kernels, call(): pl.pallas_call(kernel, in_specs=[spec] * len(operands), out_specs=[spec]...  18 us
    ppermute x18, starting transfers between devices, swap(): return lax.ppermute(x, 'tensor', [(i, i ^ mask) for i in range(count)])  16.1 us
    ppermute x4, waiting for transfers between devices, along_dp(): return lax.ppermute(x, 'dp', pairs)  13.2 us
    ppermute x4, starting transfers between devices, along_dp(): return lax.ppermute(x, 'dp', pairs)  10.5 us
    unnamed x10, local copies, waits for them, and re-layouts  4.35 us
  transfers between devices with their start and end apart: 22, of which 11 were waited for; matrix products, arithmetic and copies ran while one was open for 0% of the time, Pallas kernels for 15%

profile of v7, /device:TPU:0, one launch (start us, length us, event | category | flops | bytes accessed | tf_op | source)
XLA Modules:
  0.0 106.1 jit_solution(6081546644548357416)
XLA Ops:
  1.1 2.6 %collective-permute-start.1 = (bf16[128,3072]{1,0:T(8,128)(2,1)}, bf16[128,3072]{1,0:T(8,128)(2,1)S(1)}, u32[]{:S(2)}, u32[]{:S(2)}) collective-permute-start(bf16[128,3072]{1,0:T(8,128)(2,1)} %bitcast.5), channel_id=1, source_target_pairs={{0,8},{4,12},{8,0},{12,4},{16,24},{20,28},{24,16},{28,20},{1,9},{5... | collective-permute-start | bytes 2359304 | tf_op jit(solution)/shard_map/ppermute | solution.py:19
  3.7 1.5 %collective-permute-start.2 = (bf16[128,3072]{1,0:T(8,128)(2,1)}, bf16[128,3072]{1,0:T(8,128)(2,1)S(1)}, u32[]{:S(2)}, u32[]{:S(2)}) collective-permute-start(bf16[128,3072]{1,0:T(8,128)(2,1)} %bitcast.6), channel_id=1, source_target_pairs={{0,16},{4,20},{8,24},{12,28},{16,0},{20,4},{24,8},{28,12},{1,17},{... | collective-permute-start | bytes 2359304 | tf_op jit(solution)/shard_map/ppermute | solution.py:19
  5.2 1.2 %copy-done.1 = bf16[1,128,4096]{2,1,0:T(8,128)(2,1)S(1)} copy-done((bf16[1,128,4096]{2,1,0:T(8,128)(2,1)S(1)}, bf16[1,128,4096]{2,1,0:T(8,128)(2,1)}, u32[]{:S(2)}) %copy-start.1) | copy-done | bytes 1048600
  6.5 1.2 %copy-done.4 = bf16[1,128,4096]{2,1,0:T(8,128)(2,1)S(1)} copy-done((bf16[1,128,4096]{2,1,0:T(8,128)(2,1)S(1)}, bf16[1,128,4096]{2,1,0:T(8,128)(2,1)}, u32[]{:S(2)}) %copy-start.4) | copy-done | bytes 1048600
  7.9 1.6 %collective-permute-start.8 = (bf16[128,1024]{1,0:T(8,128)(2,1)S(1)}, bf16[128,1024]{1,0:T(8,128)(2,1)S(1)}, u32[]{:S(2)}, u32[]{:S(2)}) collective-permute-start(bf16[128,1024]{1,0:T(8,128)(2,1)S(1)} %get-tuple-element.72), channel_id=1, source_target_pairs={{0,8},{4,12},{8,0},{12,4},{16,24},{20,28},{24,16},{28,20},{1,9},{5... | collective-permute-start | bytes 786440 | tf_op jit(solution)/shard_map/ppermute | solution.py:19
  9.5 1.5 %collective-permute-start.9 = (bf16[128,1024]{1,0:T(8,128)(2,1)S(1)}, bf16[128,1024]{1,0:T(8,128)(2,1)S(1)}, u32[]{:S(2)}, u32[]{:S(2)}) collective-permute-start(bf16[128,1024]{1,0:T(8,128)(2,1)S(1)} %get-tuple-element.73), channel_id=1, source_target_pairs={{0,16},{4,20},{8,24},{12,28},{16,0},{20,4},{24,8},{28,12},{1,17},{... | collective-permute-start | bytes 786440 | tf_op jit(solution)/shard_map/ppermute | solution.py:19
  11.0 1.9 %copy-done.3 = bf16[3072,512]{1,0:T(8,128)(2,1)S(1)} copy-done((bf16[3072,512]{1,0:T(8,128)(2,1)S(1)}, bf16[3072,512]{1,0:T(8,128)(2,1)}, u32[]{:S(2)}) %copy-start.3) | copy-done | bytes 3145752
  13.1 9.2 %collective-permute-done.1.refs_0_.refs_1_ = bf16[128,3072]{1,0:T(8,128)(2,1)S(1)} collective-permute-done((bf16[128,3072]{1,0:T(8,128)(2,1)}, bf16[128,3072]{1,0:T(8,128)(2,1)S(1)}, u32[]{:S(2)}, u32[]{:S(2)}) %collective-permute-start.1) | collective-permute-done | bytes 786464 | tf_op jit(solution)/shard_map/ppermute | solution.py:19
  22.3 2.0 %collective-permute-done.2.refs_1_.refs_2_ = bf16[128,3072]{1,0:T(8,128)(2,1)S(1)} collective-permute-done((bf16[128,3072]{1,0:T(8,128)(2,1)}, bf16[128,3072]{1,0:T(8,128)(2,1)S(1)}, u32[]{:S(2)}, u32[]{:S(2)}) %collective-permute-start.2) | collective-permute-done | bytes 786464 | tf_op jit(solution)/shard_map/ppermute | solution.py:19
  24.4 1.6 %collective-permute-start.3 = (bf16[64,3072]{1,0:T(8,128)(2,1)S(1)}, bf16[64,3072]{1,0:T(8,128)(2,1)S(1)}, u32[]{:S(2)}, u32[]{:S(2)}) collective-permute-start(bf16[64,3072]{1,0:T(8,128)(2,1)S(1)} %get-tuple-element.81), channel_id=1, source_target_pairs={{0,16},{4,20},{8,24},{12,28},{16,0},{20,4},{24,8},{28,12},{1,17},{... | collective-permute-start | bytes 1179656 | tf_op jit(solution)/shard_map/ppermute | solution.py:19
  26.5 1.5 %collective-permute-done.8.refs_4_ = bf16[128,1024]{1,0:T(8,128)(2,1)S(1)} collective-permute-done((bf16[128,1024]{1,0:T(8,128)(2,1)S(1)}, bf16[128,1024]{1,0:T(8,128)(2,1)S(1)}, u32[]{:S(2)}, u32[]{:S(2)}) %collective-permute-start.8) | collective-permute-done | bytes 262176 | tf_op jit(solution)/shard_map/ppermute | solution.py:19
  27.9 2.0 %collective-permute-done.9.refs_5_ = bf16[128,1024]{1,0:T(8,128)(2,1)S(1)} collective-permute-done((bf16[128,1024]{1,0:T(8,128)(2,1)S(1)}, bf16[128,1024]{1,0:T(8,128)(2,1)S(1)}, u32[]{:S(2)}, u32[]{:S(2)}) %collective-permute-start.9) | collective-permute-done | bytes 262176 | tf_op jit(solution)/shard_map/ppermute | solution.py:19
  29.9 2.7 %gate_terms.1 = (bf16[384,1024]{1,0:T(8,128)(2,1)S(1)}, bf16[384,1024]{1,0:T(8,128)(2,1)S(1)}) custom-call(bf16[128,3072]{1,0:T(8,128)(2,1)S(1)} %bitcast.7, bf16[128,3072]{1,0:T(8,128)(2,1)S(1)} %collective-permute-done.1.refs_0_.refs_1_, bf16[128,3072]{1,0:T(8,128)(2,1)S(1)} %collective-permute-done.2.refs_1_.refs_2_, ...), custom_call_target="tpu_custom_call" | custom-call | tf_op jit(solution)/shard_map/gate_terms/pallas_call | solution.py:32
  32.7 1.0 weight_shares.3
  33.7 1.0 weight_shares.4
  35.3 1.5 %collective-permute-start.7 = (bf16[128,1024]{1,0:T(8,128)(2,1)S(1)}, bf16[128,1024]{1,0:T(8,128)(2,1)S(1)}, u32[]{:S(2)}, u32[]{:S(2)}) collective-permute-start(bf16[128,1024]{1,0:T(8,128)(2,1)S(1)} %get-tuple-element.83), channel_id=1, source_target_pairs={{0,24},{4,28},{8,16},{12,20},{16,8},{20,12},{24,0},{28,4},{1,25},{... | collective-permute-start | bytes 786440 | tf_op jit(solution)/shard_map/ppermute | solution.py:19
  38.1 2.6 %returns.2 = (f32[128,3072]{1,0:T(8,128)S(1)}, bf16[128,4096]{1,0:T(8,128)(2,1)S(1)}, bf16[128,4096]{1,0:T(8,128)(2,1)S(1)}) custom-call(bf16[384,1024]{1,0:T(8,128)(2,1)S(1)} %get-tuple-element.91.refs_3_.gp_ref, bf16[384,1024]{1,0:T(8,128)(2,1)S(1)} %get-tuple-element.92.gate_ref.refs_2_, bf16[3072,512]{1,0:T(8,128)(2,1)S(1)} %hold.1.refs_6_.w_ref.refs_2_, ...), custom_call_target="tpu_custom_call" | custom-call | tf_op jit(solution)/shard_map/returns/pallas_call | solution.py:32
  41.7 2.8 %collective-permute-done.7.refs_0_ = bf16[128,1024]{1,0:T(8,128)(2,1)S(1)} collective-permute-done((bf16[128,1024]{1,0:T(8,128)(2,1)S(1)}, bf16[128,1024]{1,0:T(8,128)(2,1)S(1)}, u32[]{:S(2)}, u32[]{:S(2)}) %collective-permute-start.7) | collective-permute-done | bytes 262176 | tf_op jit(solution)/shard_map/ppermute | solution.py:19
  44.6 1.3 %collective-permute-done.10.refs_5_ = bf16[128,512]{1,0:T(8,128)(2,1)S(1)} collective-permute-done((bf16[128,512]{1,0:T(8,128)(2,1)S(1)}, bf16[128,512]{1,0:T(8,128)(2,1)S(1)}, u32[]{:S(2)}, u32[]{:S(2)}) %collective-permute-start.10) | collective-permute-done | bytes 131104 | tf_op jit(solution)/shard_map/ppermute | solution.py:19
  46.6 1.6 %collective-permute-start.13 = (bf16[768,512]{1,0:T(8,128)(2,1)S(1)}, bf16[768,512]{1,0:T(8,128)(2,1)S(1)}, u32[]{:S(2)}, u32[]{:S(2)}) collective-permute-start(bf16[768,512]{1,0:T(8,128)(2,1)S(1)} %get-tuple-element.103), channel_id=1, source_target_pairs={{0,1},{1,0},{2,3},{3,2},{4,5},{5,4},{6,7},{7,6},{8,9},{9,8},{10,11... | collective-permute-start | bytes 2359304 | tf_op jit(solution)/shard_map/ppermute | solution.py:23
  49.7 1.8 %weight_shares.5 = (f32[768,512]{1,0:T(8,128)S(1)}, f32[768,512]{1,0:T(8,128)S(1)}, bf16[768,512]{1,0:T(8,128)(2,1)S(1)}, bf16[768,512]{1,0:T(8,128)(2,1)S(1)}) custom-call(bf16[128,3072]{1,0:T(8,128)(2,1)S(1)} %bitcast.10, bf16[128,3072]{1,0:T(8,128)(2,1)S(1)} %collective-permute-done.1.refs_0_.refs_1_, ...), custom_call_target="tpu_custom_call" | custom-call | tf_op jit(solution)/shard_map/weight_shares/pallas_call | solution.py:32
  51.6 1.6 %collective-permute-start.18 = (bf16[128,4096]{1,0:T(8,128)(2,1)S(1)}, bf16[128,4096]{1,0:T(8,128)(2,1)S(1)}, u32[]{:S(2)}, u32[]{:S(2)}) collective-permute-start(bf16[128,4096]{1,0:T(8,128)(2,1)S(1)} %get-tuple-element.119), channel_id=1, source_target_pairs={{0,16},{4,20},{8,24},{12,28},{16,0},{20,4},{24,8},{28,12},{1,17},{... | collective-permute-start | bytes 3145736 | tf_op jit(solution)/shard_map/ppermute | solution.py:19
  53.8 2.1 %returns.3 = bf16[128,4096]{1,0:T(8,128)(2,1)S(1)} custom-call(bf16[128,1024]{1,0:T(8,128)(2,1)S(1)} %get-tuple-element.120.refs_4_.gp_ref, bf16[128,1024]{1,0:T(8,128)(2,1)S(1)} %get-tuple-element.121.gate_ref, bf16[3072,512]{1,0:T(8,128)(2,1)S(1)} %hold.1.refs_6_.w_ref.refs_2_, bf16[3072,512]{1,0:T(8,128)(2,1)S(1)} %collective-permute-done.refs_7_.w_other_ref.refs_3_), custom_call_target="tpu_custom_call" | custom-call | tf_op jit(solution)/shard_map/returns/pallas_call | solution.py:32
  56.0 10.3 %collective-permute-done.13.ends_ref = bf16[768,512]{1,0:T(8,128)(2,1)S(1)} collective-permute-done((bf16[768,512]{1,0:T(8,128)(2,1)S(1)}, bf16[768,512]{1,0:T(8,128)(2,1)S(1)}, u32[]{:S(2)}, u32[]{:S(2)}) %collective-permute-start.13) | collective-permute-done | bytes 786464 | tf_op jit(solution)/shard_map/ppermute | solution.py:23
  66.3 1.5 %collective-permute-start.19 = (bf16[128,4096]{1,0:T(8,128)(2,1)S(1)}, bf16[128,4096]{1,0:T(8,128)(2,1)S(1)}, u32[]{:S(2)}, u32[]{:S(2)}) collective-permute-start(bf16[128,4096]{1,0:T(8,128)(2,1)S(1)} %returns.3), channel_id=1, source_target_pairs={{0,24},{4,28},{8,16},{12,20},{16,8},{20,12},{24,0},{28,4},{1,25},{... | collective-permute-start | bytes 3145736 | tf_op jit(solution)/shard_map/ppermute | solution.py:19
  68.1 3.4 %collective-permute-start.16 = (bf16[768,512]{1,0:T(8,128)(2,1)S(1)}, bf16[768,512]{1,0:T(8,128)(2,1)S(1)}, u32[]{:S(2)}, u32[]{:S(2)}) collective-permute-start(bf16[768,512]{1,0:T(8,128)(2,1)S(1)} %add_passed.1), channel_id=1, source_target_pairs={{0,1},{1,3},{2,0},{3,2},{4,5},{5,7},{6,4},{7,6},{8,9},{9,11},{10,8... | collective-permute-start | bytes 2359304 | tf_op jit(solution)/shard_map/ppermute | solution.py:23
  71.5 2.8 %collective-permute-done.17.refs_3_ = bf16[128,4096]{1,0:T(8,128)(2,1)S(1)} collective-permute-done((bf16[128,4096]{1,0:T(8,128)(2,1)S(1)}, bf16[128,4096]{1,0:T(8,128)(2,1)S(1)}, u32[]{:S(2)}, u32[]{:S(2)}) %collective-permute-start.17) | collective-permute-done | bytes 1048608 | tf_op jit(solution)/shard_map/ppermute | solution.py:19
  74.3 4.5 %collective-permute-start.21 = (bf16[768,512]{1,0:T(8,128)(2,1)S(1)}, bf16[768,512]{1,0:T(8,128)(2,1)S(1)}, u32[]{:S(2)}, u32[]{:S(2)}) collective-permute-start(bf16[768,512]{1,0:T(8,128)(2,1)S(1)} %get-tuple-element.129), channel_id=1, source_target_pairs={{0,2},{3,1},{4,6},{7,5},{8,10},{11,9},{12,14},{15,13},{16,18},{19,... | collective-permute-start | bytes 2359304 | tf_op jit(solution)/shard_map/ppermute | solution.py:23
  78.8 20.8 %collective-permute-done.18.refs_4_ = bf16[128,4096]{1,0:T(8,128)(2,1)S(1)} collective-permute-done((bf16[128,4096]{1,0:T(8,128)(2,1)S(1)}, bf16[128,4096]{1,0:T(8,128)(2,1)S(1)}, u32[]{:S(2)}, u32[]{:S(2)}) %collective-permute-start.18) | collective-permute-done | bytes 1048608 | tf_op jit(solution)/shard_map/ppermute | solution.py:19
  99.7 1.8 %finish.1 = (bf16[128,3072]{1,0:T(8,128)(2,1)}, bf16[128,4096]{1,0:T(8,128)(2,1)}) custom-call(bf16[128,4096]{1,0:T(8,128)(2,1)S(1)} %bitcast.12, f32[128,3072]{1,0:T(8,128)S(1)} %get-tuple-element.117.refs_1_, bf16[384,1024]{1,0:T(8,128)(2,1)S(1)} %get-tuple-element.92.gate_ref.refs_2_, bf16[128,4096]{1,0:T(8,128)(2,1)S(1)} %collective-permute-done.17.refs_3_, ...), custom_call_target="tpu_custom_call" | custom-call | tf_op jit(solution)/shard_map/finish/pallas_call | solution.py:32
  101.5 2.9 %collective-permute-done.21.refs_2_ = bf16[768,512]{1,0:T(8,128)(2,1)S(1)} collective-permute-done((bf16[768,512]{1,0:T(8,128)(2,1)S(1)}, bf16[768,512]{1,0:T(8,128)(2,1)S(1)}, u32[]{:S(2)}, u32[]{:S(2)}) %collective-permute-start.21) | collective-permute-done | bytes 786464 | tf_op jit(solution)/shard_map/ppermute | solution.py:23
  104.4 1.7 %total.1 = f32[768,512]{1,0:T(8,128)} custom-call(f32[768,512]{1,0:T(8,128)S(1)} %get-tuple-element.126.own_ref, bf16[768,512]{1,0:T(8,128)(2,1)S(1)} %collective-permute-done.13.ends_ref, bf16[768,512]{1,0:T(8,128)(2,1)S(1)} %collective-permute-done.20.refs_0_, bf16[768,512]{1,0:T(8,128)(2,1)S(1)} %collective-permute-done.14.refs_1_, ...), custom_call_target="tpu_custom_call" | custom-call | tf_op jit(solution)/shard_map/total/pallas_call | solution.py:32
  (38 shorter events, 7.7 us)
Async XLA Ops:
  0.6 7.3 %collective-permute-start = (bf16[3072,512]{1,0:T(8,128)(2,1)}, bf16[3072,512]{1,0:T(8,128)(2,1)S(1)}, u32[]{:S(2)}, u32[]{:S(2)}) collective-permute-start(bf16[3072,512]{1,0:T(8,128)(2,1)} %x_ref.1), channel_id=1, source_target_pairs={{0,4},{4,0},{8,12},{12,8},{16,20},{20,16},{24,28},{28,24},{1,5},{5... | collective-permute-start | bytes 9437192 | tf_op jit(solution)/shard_map/ppermute | solution.py:19
  1.1 21.2 %collective-permute-start.1 = (bf16[128,3072]{1,0:T(8,128)(2,1)}, bf16[128,3072]{1,0:T(8,128)(2,1)S(1)}, u32[]{:S(2)}, u32[]{:S(2)}) collective-permute-start(bf16[128,3072]{1,0:T(8,128)(2,1)} %bitcast.5), channel_id=1, source_target_pairs={{0,8},{4,12},{8,0},{12,4},{16,24},{20,28},{24,16},{28,20},{1,9},{5... | collective-permute-start | bytes 2359304 | tf_op jit(solution)/shard_map/ppermute | solution.py:19
  3.7 20.6 %collective-permute-start.2 = (bf16[128,3072]{1,0:T(8,128)(2,1)}, bf16[128,3072]{1,0:T(8,128)(2,1)S(1)}, u32[]{:S(2)}, u32[]{:S(2)}) collective-permute-start(bf16[128,3072]{1,0:T(8,128)(2,1)} %bitcast.6), channel_id=1, source_target_pairs={{0,16},{4,20},{8,24},{12,28},{16,0},{20,4},{24,8},{28,12},{1,17},{... | collective-permute-start | bytes 2359304 | tf_op jit(solution)/shard_map/ppermute | solution.py:19
  5.2 1.2 %copy-start.1 = (bf16[1,128,4096]{2,1,0:T(8,128)(2,1)S(1)}, bf16[1,128,4096]{2,1,0:T(8,128)(2,1)}, u32[]{:S(2)}) copy-start(bf16[1,128,4096]{2,1,0:T(8,128)(2,1)} %param.6) | copy-start | bytes 3145732
  6.5 1.2 %copy-start.4 = (bf16[1,128,4096]{2,1,0:T(8,128)(2,1)S(1)}, bf16[1,128,4096]{2,1,0:T(8,128)(2,1)}, u32[]{:S(2)}) copy-start(bf16[1,128,4096]{2,1,0:T(8,128)(2,1)} %param.5) | copy-start | bytes 3145732
  7.9 20.0 %collective-permute-start.8 = (bf16[128,1024]{1,0:T(8,128)(2,1)S(1)}, bf16[128,1024]{1,0:T(8,128)(2,1)S(1)}, u32[]{:S(2)}, u32[]{:S(2)}) collective-permute-start(bf16[128,1024]{1,0:T(8,128)(2,1)S(1)} %get-tuple-element.72), channel_id=1, source_target_pairs={{0,8},{4,12},{8,0},{12,4},{16,24},{20,28},{24,16},{28,20},{1,9},{5... | collective-permute-start | bytes 786440 | tf_op jit(solution)/shard_map/ppermute | solution.py:19
  9.5 20.4 %collective-permute-start.9 = (bf16[128,1024]{1,0:T(8,128)(2,1)S(1)}, bf16[128,1024]{1,0:T(8,128)(2,1)S(1)}, u32[]{:S(2)}, u32[]{:S(2)}) collective-permute-start(bf16[128,1024]{1,0:T(8,128)(2,1)S(1)} %get-tuple-element.73), channel_id=1, source_target_pairs={{0,16},{4,20},{8,24},{12,28},{16,0},{20,4},{24,8},{28,12},{1,17},{... | collective-permute-start | bytes 786440 | tf_op jit(solution)/shard_map/ppermute | solution.py:19
  11.0 1.9 %copy-start.3 = (bf16[3072,512]{1,0:T(8,128)(2,1)S(1)}, bf16[3072,512]{1,0:T(8,128)(2,1)}, u32[]{:S(2)}) copy-start(bf16[3072,512]{1,0:T(8,128)(2,1)} %x_ref.1) | copy-start | bytes 9437188
  13.1 16.8 %copy-start = (bf16[1,128,3072]{2,1,0:T(8,128)(2,1)S(1)}, bf16[1,128,3072]{2,1,0:T(8,128)(2,1)}, u32[]{:S(2)}) copy-start(bf16[1,128,3072]{2,1,0:T(8,128)(2,1)} %param.4) | copy-start | bytes 2359300
  24.4 13.2 %collective-permute-start.3 = (bf16[64,3072]{1,0:T(8,128)(2,1)S(1)}, bf16[64,3072]{1,0:T(8,128)(2,1)S(1)}, u32[]{:S(2)}, u32[]{:S(2)}) collective-permute-start(bf16[64,3072]{1,0:T(8,128)(2,1)S(1)} %get-tuple-element.81), channel_id=1, source_target_pairs={{0,16},{4,20},{8,24},{12,28},{16,0},{20,4},{24,8},{28,12},{1,17},{... | collective-permute-start | bytes 1179656 | tf_op jit(solution)/shard_map/ppermute | solution.py:19
  25.9 11.6 %collective-permute-start.4 = (bf16[64,3072]{1,0:T(8,128)(2,1)S(1)}, bf16[64,3072]{1,0:T(8,128)(2,1)S(1)}, u32[]{:S(2)}, u32[]{:S(2)}) collective-permute-start(bf16[64,3072]{1,0:T(8,128)(2,1)S(1)} %get-tuple-element.82), channel_id=1, source_target_pairs={{0,8},{4,12},{8,0},{12,4},{16,24},{20,28},{24,16},{28,20},{1,9},{5... | collective-permute-start | bytes 1179656 | tf_op jit(solution)/shard_map/ppermute | solution.py:19
  34.7 11.2 %collective-permute-start.11 = (bf16[768,512]{1,0:T(8,128)(2,1)S(1)}, bf16[768,512]{1,0:T(8,128)(2,1)S(1)}, u32[]{:S(2)}, u32[]{:S(2)}) collective-permute-start(bf16[768,512]{1,0:T(8,128)(2,1)S(1)} %get-tuple-element.101), channel_id=1, source_target_pairs={{0,4},{4,0},{8,12},{12,8},{16,20},{20,16},{24,28},{28,24},{1,5},{5... | collective-permute-start | bytes 2359304 | tf_op jit(solution)/shard_map/ppermute | solution.py:19
  34.8 11.2 %collective-permute-start.12 = (bf16[768,512]{1,0:T(8,128)(2,1)S(1)}, bf16[768,512]{1,0:T(8,128)(2,1)S(1)}, u32[]{:S(2)}, u32[]{:S(2)}) collective-permute-start(bf16[768,512]{1,0:T(8,128)(2,1)S(1)} %get-tuple-element.102), channel_id=1, source_target_pairs={{0,4},{4,0},{8,12},{12,8},{16,20},{20,16},{24,28},{28,24},{1,5},{5... | collective-permute-start | bytes 2359304 | tf_op jit(solution)/shard_map/ppermute | solution.py:19
  35.3 9.2 %collective-permute-start.7 = (bf16[128,1024]{1,0:T(8,128)(2,1)S(1)}, bf16[128,1024]{1,0:T(8,128)(2,1)S(1)}, u32[]{:S(2)}, u32[]{:S(2)}) collective-permute-start(bf16[128,1024]{1,0:T(8,128)(2,1)S(1)} %get-tuple-element.83), channel_id=1, source_target_pairs={{0,24},{4,28},{8,16},{12,20},{16,8},{20,12},{24,0},{28,4},{1,25},{... | collective-permute-start | bytes 786440 | tf_op jit(solution)/shard_map/ppermute | solution.py:19
  37.6 8.4 %collective-permute-start.5 = (bf16[64,3072]{1,0:T(8,128)(2,1)S(1)}, bf16[64,3072]{1,0:T(8,128)(2,1)S(1)}, u32[]{:S(2)}, u32[]{:S(2)}) collective-permute-start(bf16[64,3072]{1,0:T(8,128)(2,1)S(1)} %collective-permute-done.3.refs_0_), channel_id=1, source_target_pairs={{0,4},{4,0},{8,12},{12,8},{16,20},{20,16},{24,28},{28,24},{1,5},{5... | collective-permute-start | bytes 1179656 | tf_op jit(solution)/shard_map/ppermute | solution.py:19
  37.6 8.4 %collective-permute-start.6 = (bf16[64,3072]{1,0:T(8,128)(2,1)S(1)}, bf16[64,3072]{1,0:T(8,128)(2,1)S(1)}, u32[]{:S(2)}, u32[]{:S(2)}) collective-permute-start(bf16[64,3072]{1,0:T(8,128)(2,1)S(1)} %collective-permute-done.4.refs_1_), channel_id=1, source_target_pairs={{0,4},{4,0},{8,12},{12,8},{16,20},{20,16},{24,28},{28,24},{1,5},{5... | collective-permute-start | bytes 1179656 | tf_op jit(solution)/shard_map/ppermute | solution.py:19
  44.5 1.4 %collective-permute-start.10 = (bf16[128,512]{1,0:T(8,128)(2,1)S(1)}, bf16[128,512]{1,0:T(8,128)(2,1)S(1)}, u32[]{:S(2)}, u32[]{:S(2)}) collective-permute-start(bf16[128,512]{1,0:T(8,128)(2,1)S(1)} %get-tuple-element.98), channel_id=1, source_target_pairs={{0,4},{4,0},{8,12},{12,8},{16,20},{20,16},{24,28},{28,24},{1,5},{5... | collective-permute-start | bytes 393224 | tf_op jit(solution)/shard_map/ppermute | solution.py:19
  46.6 19.7 %collective-permute-start.13 = (bf16[768,512]{1,0:T(8,128)(2,1)S(1)}, bf16[768,512]{1,0:T(8,128)(2,1)S(1)}, u32[]{:S(2)}, u32[]{:S(2)}) collective-permute-start(bf16[768,512]{1,0:T(8,128)(2,1)S(1)} %get-tuple-element.103), channel_id=1, source_target_pairs={{0,1},{1,0},{2,3},{3,2},{4,5},{5,4},{6,7},{7,6},{8,9},{9,8},{10,11... | collective-permute-start | bytes 2359304 | tf_op jit(solution)/shard_map/ppermute | solution.py:23
  48.3 26.0 %collective-permute-start.17 = (bf16[128,4096]{1,0:T(8,128)(2,1)S(1)}, bf16[128,4096]{1,0:T(8,128)(2,1)S(1)}, u32[]{:S(2)}, u32[]{:S(2)}) collective-permute-start(bf16[128,4096]{1,0:T(8,128)(2,1)S(1)} %get-tuple-element.118), channel_id=1, source_target_pairs={{0,8},{4,12},{8,0},{12,4},{16,24},{20,28},{24,16},{28,20},{1,9},{5... | collective-permute-start | bytes 3145736 | tf_op jit(solution)/shard_map/ppermute | solution.py:19
  48.8 19.0 %collective-permute-start.14 = (bf16[768,512]{1,0:T(8,128)(2,1)S(1)}, bf16[768,512]{1,0:T(8,128)(2,1)S(1)}, u32[]{:S(2)}, u32[]{:S(2)}) collective-permute-start(bf16[768,512]{1,0:T(8,128)(2,1)S(1)} %get-tuple-element.129), channel_id=1, source_target_pairs={{1,2},{2,1},{5,6},{6,5},{9,10},{10,9},{13,14},{14,13},{17,18},{18,... | collective-permute-start | bytes 2359304 | tf_op jit(solution)/shard_map/ppermute | solution.py:23
  51.5 16.3 %collective-permute-start.15 = (bf16[768,512]{1,0:T(8,128)(2,1)S(1)}, bf16[768,512]{1,0:T(8,128)(2,1)S(1)}, u32[]{:S(2)}, u32[]{:S(2)}) collective-permute-start(bf16[768,512]{1,0:T(8,128)(2,1)S(1)} %get-tuple-element.115), channel_id=1, source_target_pairs={{0,4},{4,0},{8,12},{12,8},{16,20},{20,16},{24,28},{28,24},{1,5},{5... | collective-permute-start | bytes 2359304 | tf_op jit(solution)/shard_map/ppermute | solution.py:19
  51.6 48.0 %collective-permute-start.18 = (bf16[128,4096]{1,0:T(8,128)(2,1)S(1)}, bf16[128,4096]{1,0:T(8,128)(2,1)S(1)}, u32[]{:S(2)}, u32[]{:S(2)}) collective-permute-start(bf16[128,4096]{1,0:T(8,128)(2,1)S(1)} %get-tuple-element.119), channel_id=1, source_target_pairs={{0,16},{4,20},{8,24},{12,28},{16,0},{20,4},{24,8},{28,12},{1,17},{... | collective-permute-start | bytes 3145736 | tf_op jit(solution)/shard_map/ppermute | solution.py:19
  56.0 43.7 %copy-start.2 = (bf16[1,128,4096]{2,1,0:T(8,128)(2,1)S(1)}, bf16[1,128,4096]{2,1,0:T(8,128)(2,1)}, u32[]{:S(2)}) copy-start(bf16[1,128,4096]{2,1,0:T(8,128)(2,1)} %param.6) | copy-start | bytes 3145732
  66.3 33.4 %collective-permute-start.19 = (bf16[128,4096]{1,0:T(8,128)(2,1)S(1)}, bf16[128,4096]{1,0:T(8,128)(2,1)S(1)}, u32[]{:S(2)}, u32[]{:S(2)}) collective-permute-start(bf16[128,4096]{1,0:T(8,128)(2,1)S(1)} %returns.3), channel_id=1, source_target_pairs={{0,24},{4,28},{8,16},{12,20},{16,8},{20,12},{24,0},{28,4},{1,25},{... | collective-permute-start | bytes 3145736 | tf_op jit(solution)/shard_map/ppermute | solution.py:19
  68.1 33.3 %collective-permute-start.16 = (bf16[768,512]{1,0:T(8,128)(2,1)S(1)}, bf16[768,512]{1,0:T(8,128)(2,1)S(1)}, u32[]{:S(2)}, u32[]{:S(2)}) collective-permute-start(bf16[768,512]{1,0:T(8,128)(2,1)S(1)} %add_passed.1), channel_id=1, source_target_pairs={{0,1},{1,3},{2,0},{3,2},{4,5},{5,7},{6,4},{7,6},{8,9},{9,11},{10,8... | collective-permute-start | bytes 2359304 | tf_op jit(solution)/shard_map/ppermute | solution.py:23
  71.5 29.9 %collective-permute-start.20 = (bf16[768,512]{1,0:T(8,128)(2,1)S(1)}, bf16[768,512]{1,0:T(8,128)(2,1)S(1)}, u32[]{:S(2)}, u32[]{:S(2)}) collective-permute-start(bf16[768,512]{1,0:T(8,128)(2,1)S(1)} %get-tuple-element.127), channel_id=1, source_target_pairs={{0,4},{4,0},{8,12},{12,8},{16,20},{20,16},{24,28},{28,24},{1,5},{5... | collective-permute-start | bytes 2359304 | tf_op jit(solution)/shard_map/ppermute | solution.py:19
  74.3 30.1 %collective-permute-start.21 = (bf16[768,512]{1,0:T(8,128)(2,1)S(1)}, bf16[768,512]{1,0:T(8,128)(2,1)S(1)}, u32[]{:S(2)}, u32[]{:S(2)}) collective-permute-start(bf16[768,512]{1,0:T(8,128)(2,1)S(1)} %get-tuple-element.129), channel_id=1, source_target_pairs={{0,2},{3,1},{4,6},{7,5},{8,10},{11,9},{12,14},{15,13},{16,18},{19,... | collective-permute-start | bytes 2359304 | tf_op jit(solution)/shard_map/ppermute | solution.py:23

commit v8 on v7

--- a/solution.py
+++ b/solution.py
@@ -248,14 +248,14 @@
     return call(kernel, "finish", [(mine.shape, BF16), (cot.shape, BF16)], cot, mine, gate, *back)
 
 
-def on_ends(ref, count):
+def on_ends(value, count):
     me = lax.axis_index("dp")
     is_end = (me == 0) | (me == count - 1)
-    return jnp.where(is_end, ref[...].astype(F32), 0.0)
+    return jnp.where(is_end, value.astype(F32), 0.0)
 
 
 def pass_kernel(count, kept_ref, other_ref, ends_ref, out_ref):
-    ends = ends_ref[...].astype(F32) - on_ends(ends_ref, count)
+    ends = ends_ref[...].astype(F32) - on_ends(ends_ref[...], count)
     out_ref[...] = (kept_ref[...] + other_ref[...].astype(F32) + ends).astype(BF16)
 
 
@@ -263,16 +263,34 @@
     return call(functools.partial(pass_kernel, count), "add_passed", [(kept.shape, BF16)], kept, other, ends)[0]
 
 
-def total_kernel(count, own_ref, ends_ref, *refs):
-    total = own_ref[...] + on_ends(ends_ref, count)
-    for ref in refs[:-1]:
-        total = total + ref[...].astype(F32)
-    refs[-1][...] = total
+def total_kernel(count, parts, own_ref, ends_ref, *refs):
+    arrived, (out_ref, sums, sent) = refs[:-3], refs[-3:]
+    rows = own_ref.shape[0] // parts
+    copies = []
+    for i in range(parts):
+        block = slice(i * rows, (i + 1) * rows)
+        total = own_ref[block] + on_ends(ends_ref[block], count)
+        for ref in arrived:
+            total = total + ref[block].astype(F32)
+        sums[block] = total
+        copies.append(pltpu.make_async_copy(sums.at[pl.ds(i * rows, rows)], out_ref.at[pl.ds(i * rows, rows)], sent.at[i]))
+        copies[-1].start()
+    for copy in copies:
+        copy.wait()
 
 
 def total(own, ends, arrived, count):
-    kernel = functools.partial(total_kernel, count)
-    return call(kernel, "total", [(own.shape, F32)], own, ends, *arrived)[0]
+    parts = 4
+    operands = [pltpu.with_memory_space_constraint(x, pltpu.VMEM) for x in (own, ends, *arrived)]
+    return pl.pallas_call(
+        functools.partial(total_kernel, count, parts),
+        in_specs=[pl.BlockSpec(memory_space=pltpu.VMEM)] * len(operands),
+        out_specs=pl.BlockSpec(memory_space=pl.ANY),
+        out_shape=jax.ShapeDtypeStruct(own.shape, F32),
+        scratch_shapes=[pltpu.VMEM(own.shape, F32), pltpu.SemaphoreType.DMA((parts,))],
+        compiler_params=pltpu.CompilerParams(vmem_limit_bytes=LIMIT),
+        name="total",
+    )(*operands)
 
 
 def sum_over_line(share_of, count):

time: 107 us -> 106 us (level)
    pallas_call x16 -> x15, Pallas kernels: 18 us -> 16.3 us  [call(): pl.pallas_call(kernel, in_specs=[spec] * len(operands), out_specs=[spec]...]
    pallas_call x0 -> x1, Pallas kernels: none -> 1.35 us  [total(): pl.pallas_call(functools.partial(total_kernel, count, parts), in_specs=[p...]
where the time goes in v8:
time: 106 us
  waiting for transfers between devices  56.3 us (53%)
  starting transfers between devices  26.6 us (25%)
  Pallas kernels  17.7 us (17%)
  local copies, waits for them, and re-layouts  4.35 us (4%)
    ppermute x18, waiting for transfers between devices, swap(): return lax.ppermute(x, 'tensor', [(i, i ^ mask) for i in range(count)])  43.1 us
    pallas_call x15, Pallas kernels, call(): pl.pallas_call(kernel, in_specs=[spec] * len(operands), out_specs=[spec]...  16.3 us
    ppermute x18, starting transfers between devices, swap(): return lax.ppermute(x, 'tensor', [(i, i ^ mask) for i in range(count)])  16.1 us
    ppermute x4, waiting for transfers between devices, along_dp(): return lax.ppermute(x, 'dp', pairs)  13.2 us
    ppermute x4, starting transfers between devices, along_dp(): return lax.ppermute(x, 'dp', pairs)  10.5 us
    unnamed x10, local copies, waits for them, and re-layouts  4.35 us
  transfers between devices with their start and end apart: 22, of which 11 were waited for; matrix products, arithmetic and copies ran while one was open for 0% of the time, Pallas kernels for 15%

profile of v8, /device:TPU:0, one launch (start us, length us, event | category | flops | bytes accessed | tf_op | source)
XLA Modules:
  0.0 105.9 jit_solution(7945702331591930514)
XLA Ops:
  1.1 2.6 %collective-permute-start.1 = (bf16[128,3072]{1,0:T(8,128)(2,1)}, bf16[128,3072]{1,0:T(8,128)(2,1)S(1)}, u32[]{:S(2)}, u32[]{:S(2)}) collective-permute-start(bf16[128,3072]{1,0:T(8,128)(2,1)} %bitcast.5), channel_id=1, source_target_pairs={{0,8},{4,12},{8,0},{12,4},{16,24},{20,28},{24,16},{28,20},{1,9},{5... | collective-permute-start | bytes 2359304 | tf_op jit(solution)/shard_map/ppermute | solution.py:19
  3.7 1.5 %collective-permute-start.2 = (bf16[128,3072]{1,0:T(8,128)(2,1)}, bf16[128,3072]{1,0:T(8,128)(2,1)S(1)}, u32[]{:S(2)}, u32[]{:S(2)}) collective-permute-start(bf16[128,3072]{1,0:T(8,128)(2,1)} %bitcast.6), channel_id=1, source_target_pairs={{0,16},{4,20},{8,24},{12,28},{16,0},{20,4},{24,8},{28,12},{1,17},{... | collective-permute-start | bytes 2359304 | tf_op jit(solution)/shard_map/ppermute | solution.py:19
  5.2 1.2 %copy-done.1 = bf16[1,128,4096]{2,1,0:T(8,128)(2,1)S(1)} copy-done((bf16[1,128,4096]{2,1,0:T(8,128)(2,1)S(1)}, bf16[1,128,4096]{2,1,0:T(8,128)(2,1)}, u32[]{:S(2)}) %copy-start.1) | copy-done | bytes 1048600
  6.5 1.2 %copy-done.4 = bf16[1,128,4096]{2,1,0:T(8,128)(2,1)S(1)} copy-done((bf16[1,128,4096]{2,1,0:T(8,128)(2,1)S(1)}, bf16[1,128,4096]{2,1,0:T(8,128)(2,1)}, u32[]{:S(2)}) %copy-start.4) | copy-done | bytes 1048600
  7.9 1.6 %collective-permute-start.8 = (bf16[128,1024]{1,0:T(8,128)(2,1)S(1)}, bf16[128,1024]{1,0:T(8,128)(2,1)S(1)}, u32[]{:S(2)}, u32[]{:S(2)}) collective-permute-start(bf16[128,1024]{1,0:T(8,128)(2,1)S(1)} %get-tuple-element.72), channel_id=1, source_target_pairs={{0,8},{4,12},{8,0},{12,4},{16,24},{20,28},{24,16},{28,20},{1,9},{5... | collective-permute-start | bytes 786440 | tf_op jit(solution)/shard_map/ppermute | solution.py:19
  9.5 1.5 %collective-permute-start.9 = (bf16[128,1024]{1,0:T(8,128)(2,1)S(1)}, bf16[128,1024]{1,0:T(8,128)(2,1)S(1)}, u32[]{:S(2)}, u32[]{:S(2)}) collective-permute-start(bf16[128,1024]{1,0:T(8,128)(2,1)S(1)} %get-tuple-element.73), channel_id=1, source_target_pairs={{0,16},{4,20},{8,24},{12,28},{16,0},{20,4},{24,8},{28,12},{1,17},{... | collective-permute-start | bytes 786440 | tf_op jit(solution)/shard_map/ppermute | solution.py:19
  11.0 1.9 %copy-done.3 = bf16[3072,512]{1,0:T(8,128)(2,1)S(1)} copy-done((bf16[3072,512]{1,0:T(8,128)(2,1)S(1)}, bf16[3072,512]{1,0:T(8,128)(2,1)}, u32[]{:S(2)}) %copy-start.3) | copy-done | bytes 3145752
  13.1 9.2 %collective-permute-done.1.refs_0_.refs_1_ = bf16[128,3072]{1,0:T(8,128)(2,1)S(1)} collective-permute-done((bf16[128,3072]{1,0:T(8,128)(2,1)}, bf16[128,3072]{1,0:T(8,128)(2,1)S(1)}, u32[]{:S(2)}, u32[]{:S(2)}) %collective-permute-start.1) | collective-permute-done | bytes 786464 | tf_op jit(solution)/shard_map/ppermute | solution.py:19
  22.3 2.0 %collective-permute-done.2.refs_1_.refs_2_ = bf16[128,3072]{1,0:T(8,128)(2,1)S(1)} collective-permute-done((bf16[128,3072]{1,0:T(8,128)(2,1)}, bf16[128,3072]{1,0:T(8,128)(2,1)S(1)}, u32[]{:S(2)}, u32[]{:S(2)}) %collective-permute-start.2) | collective-permute-done | bytes 786464 | tf_op jit(solution)/shard_map/ppermute | solution.py:19
  24.4 1.6 %collective-permute-start.3 = (bf16[64,3072]{1,0:T(8,128)(2,1)S(1)}, bf16[64,3072]{1,0:T(8,128)(2,1)S(1)}, u32[]{:S(2)}, u32[]{:S(2)}) collective-permute-start(bf16[64,3072]{1,0:T(8,128)(2,1)S(1)} %get-tuple-element.81), channel_id=1, source_target_pairs={{0,16},{4,20},{8,24},{12,28},{16,0},{20,4},{24,8},{28,12},{1,17},{... | collective-permute-start | bytes 1179656 | tf_op jit(solution)/shard_map/ppermute | solution.py:19
  26.5 1.5 %collective-permute-done.8.refs_4_ = bf16[128,1024]{1,0:T(8,128)(2,1)S(1)} collective-permute-done((bf16[128,1024]{1,0:T(8,128)(2,1)S(1)}, bf16[128,1024]{1,0:T(8,128)(2,1)S(1)}, u32[]{:S(2)}, u32[]{:S(2)}) %collective-permute-start.8) | collective-permute-done | bytes 262176 | tf_op jit(solution)/shard_map/ppermute | solution.py:19
  27.9 2.0 %collective-permute-done.9.refs_5_ = bf16[128,1024]{1,0:T(8,128)(2,1)S(1)} collective-permute-done((bf16[128,1024]{1,0:T(8,128)(2,1)S(1)}, bf16[128,1024]{1,0:T(8,128)(2,1)S(1)}, u32[]{:S(2)}, u32[]{:S(2)}) %collective-permute-start.9) | collective-permute-done | bytes 262176 | tf_op jit(solution)/shard_map/ppermute | solution.py:19
  29.9 2.7 %gate_terms.1 = (bf16[384,1024]{1,0:T(8,128)(2,1)S(1)}, bf16[384,1024]{1,0:T(8,128)(2,1)S(1)}) custom-call(bf16[128,3072]{1,0:T(8,128)(2,1)S(1)} %bitcast.7, bf16[128,3072]{1,0:T(8,128)(2,1)S(1)} %collective-permute-done.1.refs_0_.refs_1_, bf16[128,3072]{1,0:T(8,128)(2,1)S(1)} %collective-permute-done.2.refs_1_.refs_2_, ...), custom_call_target="tpu_custom_call" | custom-call | tf_op jit(solution)/shard_map/gate_terms/pallas_call | solution.py:32
  32.7 1.0 weight_shares.3
  33.7 1.0 weight_shares.4
  35.3 1.5 %collective-permute-start.7 = (bf16[128,1024]{1,0:T(8,128)(2,1)S(1)}, bf16[128,1024]{1,0:T(8,128)(2,1)S(1)}, u32[]{:S(2)}, u32[]{:S(2)}) collective-permute-start(bf16[128,1024]{1,0:T(8,128)(2,1)S(1)} %get-tuple-element.83), channel_id=1, source_target_pairs={{0,24},{4,28},{8,16},{12,20},{16,8},{20,12},{24,0},{28,4},{1,25},{... | collective-permute-start | bytes 786440 | tf_op jit(solution)/shard_map/ppermute | solution.py:19
  38.1 2.6 %returns.2 = (f32[128,3072]{1,0:T(8,128)S(1)}, bf16[128,4096]{1,0:T(8,128)(2,1)S(1)}, bf16[128,4096]{1,0:T(8,128)(2,1)S(1)}) custom-call(bf16[384,1024]{1,0:T(8,128)(2,1)S(1)} %get-tuple-element.91.refs_3_.gp_ref, bf16[384,1024]{1,0:T(8,128)(2,1)S(1)} %get-tuple-element.92.gate_ref.refs_2_, bf16[3072,512]{1,0:T(8,128)(2,1)S(1)} %hold.1.refs_6_.w_ref.refs_2_, ...), custom_call_target="tpu_custom_call" | custom-call | tf_op jit(solution)/shard_map/returns/pallas_call | solution.py:32
  41.7 2.8 %collective-permute-done.7.refs_0_ = bf16[128,1024]{1,0:T(8,128)(2,1)S(1)} collective-permute-done((bf16[128,1024]{1,0:T(8,128)(2,1)S(1)}, bf16[128,1024]{1,0:T(8,128)(2,1)S(1)}, u32[]{:S(2)}, u32[]{:S(2)}) %collective-permute-start.7) | collective-permute-done | bytes 262176 | tf_op jit(solution)/shard_map/ppermute | solution.py:19
  44.6 1.3 %collective-permute-done.10.refs_5_ = bf16[128,512]{1,0:T(8,128)(2,1)S(1)} collective-permute-done((bf16[128,512]{1,0:T(8,128)(2,1)S(1)}, bf16[128,512]{1,0:T(8,128)(2,1)S(1)}, u32[]{:S(2)}, u32[]{:S(2)}) %collective-permute-start.10) | collective-permute-done | bytes 131104 | tf_op jit(solution)/shard_map/ppermute | solution.py:19
  46.6 1.6 %collective-permute-start.13 = (bf16[768,512]{1,0:T(8,128)(2,1)S(1)}, bf16[768,512]{1,0:T(8,128)(2,1)S(1)}, u32[]{:S(2)}, u32[]{:S(2)}) collective-permute-start(bf16[768,512]{1,0:T(8,128)(2,1)S(1)} %get-tuple-element.103), channel_id=1, source_target_pairs={{0,1},{1,0},{2,3},{3,2},{4,5},{5,4},{6,7},{7,6},{8,9},{9,8},{10,11... | collective-permute-start | bytes 2359304 | tf_op jit(solution)/shard_map/ppermute | solution.py:23
  49.7 1.8 %weight_shares.5 = (f32[768,512]{1,0:T(8,128)S(1)}, f32[768,512]{1,0:T(8,128)S(1)}, bf16[768,512]{1,0:T(8,128)(2,1)S(1)}, bf16[768,512]{1,0:T(8,128)(2,1)S(1)}) custom-call(bf16[128,3072]{1,0:T(8,128)(2,1)S(1)} %bitcast.10, bf16[128,3072]{1,0:T(8,128)(2,1)S(1)} %collective-permute-done.1.refs_0_.refs_1_, ...), custom_call_target="tpu_custom_call" | custom-call | tf_op jit(solution)/shard_map/weight_shares/pallas_call | solution.py:32
  51.6 1.6 %collective-permute-start.18 = (bf16[128,4096]{1,0:T(8,128)(2,1)S(1)}, bf16[128,4096]{1,0:T(8,128)(2,1)S(1)}, u32[]{:S(2)}, u32[]{:S(2)}) collective-permute-start(bf16[128,4096]{1,0:T(8,128)(2,1)S(1)} %get-tuple-element.119), channel_id=1, source_target_pairs={{0,16},{4,20},{8,24},{12,28},{16,0},{20,4},{24,8},{28,12},{1,17},{... | collective-permute-start | bytes 3145736 | tf_op jit(solution)/shard_map/ppermute | solution.py:19
  53.8 2.1 %returns.3 = bf16[128,4096]{1,0:T(8,128)(2,1)S(1)} custom-call(bf16[128,1024]{1,0:T(8,128)(2,1)S(1)} %get-tuple-element.120.refs_4_.gp_ref, bf16[128,1024]{1,0:T(8,128)(2,1)S(1)} %get-tuple-element.121.gate_ref, bf16[3072,512]{1,0:T(8,128)(2,1)S(1)} %hold.1.refs_6_.w_ref.refs_2_, bf16[3072,512]{1,0:T(8,128)(2,1)S(1)} %collective-permute-done.refs_7_.w_other_ref.refs_3_), custom_call_target="tpu_custom_call" | custom-call | tf_op jit(solution)/shard_map/returns/pallas_call | solution.py:32
  56.0 10.3 %collective-permute-done.13.ends_ref = bf16[768,512]{1,0:T(8,128)(2,1)S(1)} collective-permute-done((bf16[768,512]{1,0:T(8,128)(2,1)S(1)}, bf16[768,512]{1,0:T(8,128)(2,1)S(1)}, u32[]{:S(2)}, u32[]{:S(2)}) %collective-permute-start.13) | collective-permute-done | bytes 786464 | tf_op jit(solution)/shard_map/ppermute | solution.py:23
  66.3 1.5 %collective-permute-start.19 = (bf16[128,4096]{1,0:T(8,128)(2,1)S(1)}, bf16[128,4096]{1,0:T(8,128)(2,1)S(1)}, u32[]{:S(2)}, u32[]{:S(2)}) collective-permute-start(bf16[128,4096]{1,0:T(8,128)(2,1)S(1)} %returns.3), channel_id=1, source_target_pairs={{0,24},{4,28},{8,16},{12,20},{16,8},{20,12},{24,0},{28,4},{1,25},{... | collective-permute-start | bytes 3145736 | tf_op jit(solution)/shard_map/ppermute | solution.py:19
  68.1 3.4 %collective-permute-start.16 = (bf16[768,512]{1,0:T(8,128)(2,1)S(1)}, bf16[768,512]{1,0:T(8,128)(2,1)S(1)}, u32[]{:S(2)}, u32[]{:S(2)}) collective-permute-start(bf16[768,512]{1,0:T(8,128)(2,1)S(1)} %add_passed.1), channel_id=1, source_target_pairs={{0,1},{1,3},{2,0},{3,2},{4,5},{5,7},{6,4},{7,6},{8,9},{9,11},{10,8... | collective-permute-start | bytes 2359304 | tf_op jit(solution)/shard_map/ppermute | solution.py:23
  71.5 2.8 %collective-permute-done.17.refs_3_ = bf16[128,4096]{1,0:T(8,128)(2,1)S(1)} collective-permute-done((bf16[128,4096]{1,0:T(8,128)(2,1)S(1)}, bf16[128,4096]{1,0:T(8,128)(2,1)S(1)}, u32[]{:S(2)}, u32[]{:S(2)}) %collective-permute-start.17) | collective-permute-done | bytes 1048608 | tf_op jit(solution)/shard_map/ppermute | solution.py:19
  74.3 4.5 %collective-permute-start.21 = (bf16[768,512]{1,0:T(8,128)(2,1)S(1)}, bf16[768,512]{1,0:T(8,128)(2,1)S(1)}, u32[]{:S(2)}, u32[]{:S(2)}) collective-permute-start(bf16[768,512]{1,0:T(8,128)(2,1)S(1)} %get-tuple-element.129), channel_id=1, source_target_pairs={{0,2},{3,1},{4,6},{7,5},{8,10},{11,9},{12,14},{15,13},{16,18},{19,... | collective-permute-start | bytes 2359304 | tf_op jit(solution)/shard_map/ppermute | solution.py:23
  78.8 20.8 %collective-permute-done.18.refs_4_ = bf16[128,4096]{1,0:T(8,128)(2,1)S(1)} collective-permute-done((bf16[128,4096]{1,0:T(8,128)(2,1)S(1)}, bf16[128,4096]{1,0:T(8,128)(2,1)S(1)}, u32[]{:S(2)}, u32[]{:S(2)}) %collective-permute-start.18) | collective-permute-done | bytes 1048608 | tf_op jit(solution)/shard_map/ppermute | solution.py:19
  99.7 1.8 %finish.1 = (bf16[128,3072]{1,0:T(8,128)(2,1)}, bf16[128,4096]{1,0:T(8,128)(2,1)}) custom-call(bf16[128,4096]{1,0:T(8,128)(2,1)S(1)} %bitcast.12, f32[128,3072]{1,0:T(8,128)S(1)} %get-tuple-element.117.refs_1_, bf16[384,1024]{1,0:T(8,128)(2,1)S(1)} %get-tuple-element.92.gate_ref.refs_2_, bf16[128,4096]{1,0:T(8,128)(2,1)S(1)} %collective-permute-done.17.refs_3_, ...), custom_call_target="tpu_custom_call" | custom-call | tf_op jit(solution)/shard_map/finish/pallas_call | solution.py:32
  101.5 2.9 %collective-permute-done.21.refs_2_ = bf16[768,512]{1,0:T(8,128)(2,1)S(1)} collective-permute-done((bf16[768,512]{1,0:T(8,128)(2,1)S(1)}, bf16[768,512]{1,0:T(8,128)(2,1)S(1)}, u32[]{:S(2)}, u32[]{:S(2)}) %collective-permute-start.21) | collective-permute-done | bytes 786464 | tf_op jit(solution)/shard_map/ppermute | solution.py:23
  104.4 1.3 %total.1 = f32[768,512]{1,0:T(8,128)} custom-call(f32[768,512]{1,0:T(8,128)S(1)} %get-tuple-element.126.own_ref, bf16[768,512]{1,0:T(8,128)(2,1)S(1)} %collective-permute-done.13.ends_ref, bf16[768,512]{1,0:T(8,128)(2,1)S(1)} %collective-permute-done.20.refs_0_, bf16[768,512]{1,0:T(8,128)(2,1)S(1)} %collective-permute-done.14.refs_1_, ...), custom_call_target="tpu_custom_call" | custom-call | tf_op jit(solution)/shard_map/total/pallas_call | solution.py:285
  (38 shorter events, 7.7 us)
Async XLA Ops:
  0.6 7.3 %collective-permute-start = (bf16[3072,512]{1,0:T(8,128)(2,1)}, bf16[3072,512]{1,0:T(8,128)(2,1)S(1)}, u32[]{:S(2)}, u32[]{:S(2)}) collective-permute-start(bf16[3072,512]{1,0:T(8,128)(2,1)} %x_ref.1), channel_id=1, source_target_pairs={{0,4},{4,0},{8,12},{12,8},{16,20},{20,16},{24,28},{28,24},{1,5},{5... | collective-permute-start | bytes 9437192 | tf_op jit(solution)/shard_map/ppermute | solution.py:19
  1.1 21.2 %collective-permute-start.1 = (bf16[128,3072]{1,0:T(8,128)(2,1)}, bf16[128,3072]{1,0:T(8,128)(2,1)S(1)}, u32[]{:S(2)}, u32[]{:S(2)}) collective-permute-start(bf16[128,3072]{1,0:T(8,128)(2,1)} %bitcast.5), channel_id=1, source_target_pairs={{0,8},{4,12},{8,0},{12,4},{16,24},{20,28},{24,16},{28,20},{1,9},{5... | collective-permute-start | bytes 2359304 | tf_op jit(solution)/shard_map/ppermute | solution.py:19
  3.7 20.6 %collective-permute-start.2 = (bf16[128,3072]{1,0:T(8,128)(2,1)}, bf16[128,3072]{1,0:T(8,128)(2,1)S(1)}, u32[]{:S(2)}, u32[]{:S(2)}) collective-permute-start(bf16[128,3072]{1,0:T(8,128)(2,1)} %bitcast.6), channel_id=1, source_target_pairs={{0,16},{4,20},{8,24},{12,28},{16,0},{20,4},{24,8},{28,12},{1,17},{... | collective-permute-start | bytes 2359304 | tf_op jit(solution)/shard_map/ppermute | solution.py:19
  5.2 1.2 %copy-start.1 = (bf16[1,128,4096]{2,1,0:T(8,128)(2,1)S(1)}, bf16[1,128,4096]{2,1,0:T(8,128)(2,1)}, u32[]{:S(2)}) copy-start(bf16[1,128,4096]{2,1,0:T(8,128)(2,1)} %param.6) | copy-start | bytes 3145732
  6.5 1.2 %copy-start.4 = (bf16[1,128,4096]{2,1,0:T(8,128)(2,1)S(1)}, bf16[1,128,4096]{2,1,0:T(8,128)(2,1)}, u32[]{:S(2)}) copy-start(bf16[1,128,4096]{2,1,0:T(8,128)(2,1)} %param.5) | copy-start | bytes 3145732
  7.9 20.0 %collective-permute-start.8 = (bf16[128,1024]{1,0:T(8,128)(2,1)S(1)}, bf16[128,1024]{1,0:T(8,128)(2,1)S(1)}, u32[]{:S(2)}, u32[]{:S(2)}) collective-permute-start(bf16[128,1024]{1,0:T(8,128)(2,1)S(1)} %get-tuple-element.72), channel_id=1, source_target_pairs={{0,8},{4,12},{8,0},{12,4},{16,24},{20,28},{24,16},{28,20},{1,9},{5... | collective-permute-start | bytes 786440 | tf_op jit(solution)/shard_map/ppermute | solution.py:19
  9.5 20.4 %collective-permute-start.9 = (bf16[128,1024]{1,0:T(8,128)(2,1)S(1)}, bf16[128,1024]{1,0:T(8,128)(2,1)S(1)}, u32[]{:S(2)}, u32[]{:S(2)}) collective-permute-start(bf16[128,1024]{1,0:T(8,128)(2,1)S(1)} %get-tuple-element.73), channel_id=1, source_target_pairs={{0,16},{4,20},{8,24},{12,28},{16,0},{20,4},{24,8},{28,12},{1,17},{... | collective-permute-start | bytes 786440 | tf_op jit(solution)/shard_map/ppermute | solution.py:19
  11.0 1.9 %copy-start.3 = (bf16[3072,512]{1,0:T(8,128)(2,1)S(1)}, bf16[3072,512]{1,0:T(8,128)(2,1)}, u32[]{:S(2)}) copy-start(bf16[3072,512]{1,0:T(8,128)(2,1)} %x_ref.1) | copy-start | bytes 9437188
  13.1 16.8 %copy-start = (bf16[1,128,3072]{2,1,0:T(8,128)(2,1)S(1)}, bf16[1,128,3072]{2,1,0:T(8,128)(2,1)}, u32[]{:S(2)}) copy-start(bf16[1,128,3072]{2,1,0:T(8,128)(2,1)} %param.4) | copy-start | bytes 2359300
  24.4 13.2 %collective-permute-start.3 = (bf16[64,3072]{1,0:T(8,128)(2,1)S(1)}, bf16[64,3072]{1,0:T(8,128)(2,1)S(1)}, u32[]{:S(2)}, u32[]{:S(2)}) collective-permute-start(bf16[64,3072]{1,0:T(8,128)(2,1)S(1)} %get-tuple-element.81), channel_id=1, source_target_pairs={{0,16},{4,20},{8,24},{12,28},{16,0},{20,4},{24,8},{28,12},{1,17},{... | collective-permute-start | bytes 1179656 | tf_op jit(solution)/shard_map/ppermute | solution.py:19
  25.9 11.6 %collective-permute-start.4 = (bf16[64,3072]{1,0:T(8,128)(2,1)S(1)}, bf16[64,3072]{1,0:T(8,128)(2,1)S(1)}, u32[]{:S(2)}, u32[]{:S(2)}) collective-permute-start(bf16[64,3072]{1,0:T(8,128)(2,1)S(1)} %get-tuple-element.82), channel_id=1, source_target_pairs={{0,8},{4,12},{8,0},{12,4},{16,24},{20,28},{24,16},{28,20},{1,9},{5... | collective-permute-start | bytes 1179656 | tf_op jit(solution)/shard_map/ppermute | solution.py:19
  34.7 11.2 %collective-permute-start.11 = (bf16[768,512]{1,0:T(8,128)(2,1)S(1)}, bf16[768,512]{1,0:T(8,128)(2,1)S(1)}, u32[]{:S(2)}, u32[]{:S(2)}) collective-permute-start(bf16[768,512]{1,0:T(8,128)(2,1)S(1)} %get-tuple-element.101), channel_id=1, source_target_pairs={{0,4},{4,0},{8,12},{12,8},{16,20},{20,16},{24,28},{28,24},{1,5},{5... | collective-permute-start | bytes 2359304 | tf_op jit(solution)/shard_map/ppermute | solution.py:19
  34.8 11.2 %collective-permute-start.12 = (bf16[768,512]{1,0:T(8,128)(2,1)S(1)}, bf16[768,512]{1,0:T(8,128)(2,1)S(1)}, u32[]{:S(2)}, u32[]{:S(2)}) collective-permute-start(bf16[768,512]{1,0:T(8,128)(2,1)S(1)} %get-tuple-element.102), channel_id=1, source_target_pairs={{0,4},{4,0},{8,12},{12,8},{16,20},{20,16},{24,28},{28,24},{1,5},{5... | collective-permute-start | bytes 2359304 | tf_op jit(solution)/shard_map/ppermute | solution.py:19
  35.3 9.2 %collective-permute-start.7 = (bf16[128,1024]{1,0:T(8,128)(2,1)S(1)}, bf16[128,1024]{1,0:T(8,128)(2,1)S(1)}, u32[]{:S(2)}, u32[]{:S(2)}) collective-permute-start(bf16[128,1024]{1,0:T(8,128)(2,1)S(1)} %get-tuple-element.83), channel_id=1, source_target_pairs={{0,24},{4,28},{8,16},{12,20},{16,8},{20,12},{24,0},{28,4},{1,25},{... | collective-permute-start | bytes 786440 | tf_op jit(solution)/shard_map/ppermute | solution.py:19
  37.6 8.4 %collective-permute-start.5 = (bf16[64,3072]{1,0:T(8,128)(2,1)S(1)}, bf16[64,3072]{1,0:T(8,128)(2,1)S(1)}, u32[]{:S(2)}, u32[]{:S(2)}) collective-permute-start(bf16[64,3072]{1,0:T(8,128)(2,1)S(1)} %collective-permute-done.3.refs_0_), channel_id=1, source_target_pairs={{0,4},{4,0},{8,12},{12,8},{16,20},{20,16},{24,28},{28,24},{1,5},{5... | collective-permute-start | bytes 1179656 | tf_op jit(solution)/shard_map/ppermute | solution.py:19
  37.6 8.4 %collective-permute-start.6 = (bf16[64,3072]{1,0:T(8,128)(2,1)S(1)}, bf16[64,3072]{1,0:T(8,128)(2,1)S(1)}, u32[]{:S(2)}, u32[]{:S(2)}) collective-permute-start(bf16[64,3072]{1,0:T(8,128)(2,1)S(1)} %collective-permute-done.4.refs_1_), channel_id=1, source_target_pairs={{0,4},{4,0},{8,12},{12,8},{16,20},{20,16},{24,28},{28,24},{1,5},{5... | collective-permute-start | bytes 1179656 | tf_op jit(solution)/shard_map/ppermute | solution.py:19
  44.5 1.4 %collective-permute-start.10 = (bf16[128,512]{1,0:T(8,128)(2,1)S(1)}, bf16[128,512]{1,0:T(8,128)(2,1)S(1)}, u32[]{:S(2)}, u32[]{:S(2)}) collective-permute-start(bf16[128,512]{1,0:T(8,128)(2,1)S(1)} %get-tuple-element.98), channel_id=1, source_target_pairs={{0,4},{4,0},{8,12},{12,8},{16,20},{20,16},{24,28},{28,24},{1,5},{5... | collective-permute-start | bytes 393224 | tf_op jit(solution)/shard_map/ppermute | solution.py:19
  46.6 19.7 %collective-permute-start.13 = (bf16[768,512]{1,0:T(8,128)(2,1)S(1)}, bf16[768,512]{1,0:T(8,128)(2,1)S(1)}, u32[]{:S(2)}, u32[]{:S(2)}) collective-permute-start(bf16[768,512]{1,0:T(8,128)(2,1)S(1)} %get-tuple-element.103), channel_id=1, source_target_pairs={{0,1},{1,0},{2,3},{3,2},{4,5},{5,4},{6,7},{7,6},{8,9},{9,8},{10,11... | collective-permute-start | bytes 2359304 | tf_op jit(solution)/shard_map/ppermute | solution.py:23
  48.3 26.0 %collective-permute-start.17 = (bf16[128,4096]{1,0:T(8,128)(2,1)S(1)}, bf16[128,4096]{1,0:T(8,128)(2,1)S(1)}, u32[]{:S(2)}, u32[]{:S(2)}) collective-permute-start(bf16[128,4096]{1,0:T(8,128)(2,1)S(1)} %get-tuple-element.118), channel_id=1, source_target_pairs={{0,8},{4,12},{8,0},{12,4},{16,24},{20,28},{24,16},{28,20},{1,9},{5... | collective-permute-start | bytes 3145736 | tf_op jit(solution)/shard_map/ppermute | solution.py:19
  48.8 19.0 %collective-permute-start.14 = (bf16[768,512]{1,0:T(8,128)(2,1)S(1)}, bf16[768,512]{1,0:T(8,128)(2,1)S(1)}, u32[]{:S(2)}, u32[]{:S(2)}) collective-permute-start(bf16[768,512]{1,0:T(8,128)(2,1)S(1)} %get-tuple-element.129), channel_id=1, source_target_pairs={{1,2},{2,1},{5,6},{6,5},{9,10},{10,9},{13,14},{14,13},{17,18},{18,... | collective-permute-start | bytes 2359304 | tf_op jit(solution)/shard_map/ppermute | solution.py:23
  51.5 16.3 %collective-permute-start.15 = (bf16[768,512]{1,0:T(8,128)(2,1)S(1)}, bf16[768,512]{1,0:T(8,128)(2,1)S(1)}, u32[]{:S(2)}, u32[]{:S(2)}) collective-permute-start(bf16[768,512]{1,0:T(8,128)(2,1)S(1)} %get-tuple-element.115), channel_id=1, source_target_pairs={{0,4},{4,0},{8,12},{12,8},{16,20},{20,16},{24,28},{28,24},{1,5},{5... | collective-permute-start | bytes 2359304 | tf_op jit(solution)/shard_map/ppermute | solution.py:19
  51.6 48.0 %collective-permute-start.18 = (bf16[128,4096]{1,0:T(8,128)(2,1)S(1)}, bf16[128,4096]{1,0:T(8,128)(2,1)S(1)}, u32[]{:S(2)}, u32[]{:S(2)}) collective-permute-start(bf16[128,4096]{1,0:T(8,128)(2,1)S(1)} %get-tuple-element.119), channel_id=1, source_target_pairs={{0,16},{4,20},{8,24},{12,28},{16,0},{20,4},{24,8},{28,12},{1,17},{... | collective-permute-start | bytes 3145736 | tf_op jit(solution)/shard_map/ppermute | solution.py:19
  56.0 43.7 %copy-start.2 = (bf16[1,128,4096]{2,1,0:T(8,128)(2,1)S(1)}, bf16[1,128,4096]{2,1,0:T(8,128)(2,1)}, u32[]{:S(2)}) copy-start(bf16[1,128,4096]{2,1,0:T(8,128)(2,1)} %param.6) | copy-start | bytes 3145732
  66.3 33.4 %collective-permute-start.19 = (bf16[128,4096]{1,0:T(8,128)(2,1)S(1)}, bf16[128,4096]{1,0:T(8,128)(2,1)S(1)}, u32[]{:S(2)}, u32[]{:S(2)}) collective-permute-start(bf16[128,4096]{1,0:T(8,128)(2,1)S(1)} %returns.3), channel_id=1, source_target_pairs={{0,24},{4,28},{8,16},{12,20},{16,8},{20,12},{24,0},{28,4},{1,25},{... | collective-permute-start | bytes 3145736 | tf_op jit(solution)/shard_map/ppermute | solution.py:19
  68.1 33.3 %collective-permute-start.16 = (bf16[768,512]{1,0:T(8,128)(2,1)S(1)}, bf16[768,512]{1,0:T(8,128)(2,1)S(1)}, u32[]{:S(2)}, u32[]{:S(2)}) collective-permute-start(bf16[768,512]{1,0:T(8,128)(2,1)S(1)} %add_passed.1), channel_id=1, source_target_pairs={{0,1},{1,3},{2,0},{3,2},{4,5},{5,7},{6,4},{7,6},{8,9},{9,11},{10,8... | collective-permute-start | bytes 2359304 | tf_op jit(solution)/shard_map/ppermute | solution.py:23
  71.5 29.9 %collective-permute-start.20 = (bf16[768,512]{1,0:T(8,128)(2,1)S(1)}, bf16[768,512]{1,0:T(8,128)(2,1)S(1)}, u32[]{:S(2)}, u32[]{:S(2)}) collective-permute-start(bf16[768,512]{1,0:T(8,128)(2,1)S(1)} %get-tuple-element.127), channel_id=1, source_target_pairs={{0,4},{4,0},{8,12},{12,8},{16,20},{20,16},{24,28},{28,24},{1,5},{5... | collective-permute-start | bytes 2359304 | tf_op jit(solution)/shard_map/ppermute | solution.py:19
  74.3 30.1 %collective-permute-start.21 = (bf16[768,512]{1,0:T(8,128)(2,1)S(1)}, bf16[768,512]{1,0:T(8,128)(2,1)S(1)}, u32[]{:S(2)}, u32[]{:S(2)}) collective-permute-start(bf16[768,512]{1,0:T(8,128)(2,1)S(1)} %get-tuple-element.129), channel_id=1, source_target_pairs={{0,2},{3,1},{4,6},{7,5},{8,10},{11,9},{12,14},{15,13},{16,18},{19,... | collective-permute-start | bytes 2359304 | tf_op jit(solution)/shard_map/ppermute | solution.py:23
